TPU v7x, 32 devices: a whole 2x2x4 slice. The times are simulated.
32 devices in a mesh: seq: 32 (over z, y, x, core), tp: 1.
Axes of the slice: x: 2, y: 2, z: 4, core: 2. Of those that a mesh axis runs over, the one named last changes fastest.
Arguments:
- queries: bfloat16 [4096, 4096], P('seq', 'tp'), may hold values from -6 to 6
- keys: bfloat16 [4096, 4096], P('seq', 'tp'), may hold values from -6 to 6
- values: bfloat16 [4096, 4096], P('seq', 'tp'), may hold values from -6 to 6
- w_out: bfloat16 [4096, 4096], P('seq', 'tp'), may hold values from -0.09375 to 0.09375
- taps: bfloat16 [4096, 128], P('tp'), may hold values from -0.6 to 0.6, as said below
- seg_ids: int32 [32], replicated, may hold values from 0 to 3, never falling along the last dimension, each value on 1 to 16 neighbouring positions
- cotangent: bfloat16 [4096, 4096], P('seq', 'tp'), may hold values from -6 to 6
Outputs:
- outputs: bfloat16 [4096, 4096], P('seq', 'tp')
- grad_queries: bfloat16 [4096, 4096], P('seq', 'tp')
- grad_keys: bfloat16 [4096, 4096], P('seq', 'tp')
- grad_values: bfloat16 [4096, 4096], P('seq', 'tp')
- taps_grad: float32 [4096, 128], P(('tp', 'seq'))
Inputs may be any that keep to these rules, and one draw needn't show every extreme that they name: `seg_ids`: ids never fall along the pack, each segment covers 1 to 16 blocks. taps decay along the lag at a rate of each channel.
All inputs are finite; a program needn't handle non-finite values.
Results may differ from a plain program's by a relative error of at most 0.013.
Values may be sent and summed in bfloat16 or wider, within the bound.
No kernel may reach another device: no remote copies, remote signals or barrier semaphores. Data moves between devices by JAX's collectives and lax.ppermute only.
A program may use at most 128 MiB of HBM per device.

v0:
```python
import functools

import jax
import jax.numpy as jnp
import numpy as np
from jax import lax
from jax.experimental import pallas as pl
from jax.experimental.pallas import tpu as pltpu
from jax.sharding import PartitionSpec as P

F32 = jnp.float32
BF16 = jnp.bfloat16
GRANT = 16 << 20


def spectrum_table(length):
    angles = np.pi * (2 * np.arange(length)[:, None] + 1) * np.arange(-length, length)[None, :] / (2 * length)
    table = np.concatenate([np.cos(angles), -np.sin(angles)], 0).astype(np.float32)
    high = table.astype(BF16)
    low = (table - high.astype(np.float32)).astype(BF16)
    return table, high, low


def forward_dft(high, low, data, dims):
    first = lax.dot_general(high, data, (dims, ((), ())), preferred_element_type=F32)
    second = lax.dot_general(low, data, (dims, ((), ())), preferred_element_type=F32)
    return first + second


def times(a, b):
    half = a.shape[0] // 2
    ar, ai, br, bi = a[:half], a[half:], b[:half], b[half:]
    return jnp.concatenate([ar * br - ai * bi, ar * bi + ai * br], 0)


def times_conj(a, b):
    half = a.shape[0] // 2
    ar, ai, br, bi = a[:half], a[half:], b[:half], b[half:]
    return jnp.concatenate([ar * br + ai * bi, ai * br - ar * bi], 0)


def inverse_dft(table, spectrum, scale):
    done = lax.dot_general(
        table, spectrum, (((0,), (0,)), ((), ())), precision=lax.Precision.HIGH, preferred_element_type=F32
    )
    return done * scale


def mul(a, b):
    return (a.astype(F32) * b.astype(F32)).astype(BF16)


def pick(data, width, side):
    blocks = [data[:, i : i + width] for i in range(0, data.shape[1], width)]
    return jnp.concatenate([jnp.where(side == 0, a, b) for a, b in zip(blocks[::2], blocks[1::2])], 1)


def scatter_sum(part, nseq, place, order):
    share = part.shape[1] // nseq
    bits = nseq.bit_length() - 1
    if nseq != 1 << bits:
        return lax.psum_scatter(part, "seq", scatter_dimension=1, tiled=True)
    left = list(range(bits))
    for step in [b for b in order if b < bits] + [b for b in range(bits) if b not in order]:
        width = share << sum(b < step for b in left)
        left.remove(step)
        mine = (place >> step) & 1
        away = pick(part, width, 1 - mine)
        if step:
            away = away.astype(BF16)
        away = lax.ppermute(away, "seq", [(i, i ^ (1 << step)) for i in range(nseq)])
        part = pick(part, width, mine) + away.astype(F32)
    return part


def deal_kernel(sides, scalars, data, kept, away):
    width = kept.shape[-1]
    for i in range(data.shape[1] // (2 * width)):
        for ref, side in ((kept, scalars[0]), (away, 1 - scalars[0])):
            block = data[:, pl.ds(pl.multiple_of((2 * i + side) * width, width), width)]
            if sides:
                ref[i % sides, i // sides] = block
            else:
                ref[i] = block


def deal(side, data, width, sides=0):
    rows, chans = data.shape
    count = chans // (2 * width)
    lead = (sides, count // sides) if sides else (count,)
    out = jax.ShapeDtypeStruct(lead + (rows, width), data.dtype)
    vmem = pl.BlockSpec(memory_space=pltpu.VMEM)
    return pl.pallas_call(
        functools.partial(deal_kernel, sides),
        out_shape=(out, out),
        in_specs=[pl.BlockSpec(memory_space=pltpu.SMEM), vmem],
        out_specs=(vmem, vmem),
        compiler_params=pltpu.CompilerParams(vmem_limit_bytes=GRANT),
        cost_estimate=pl.CostEstimate(flops=0, bytes_accessed=8 * rows * chans, transcendentals=0),
    )(side.reshape(1), data)


def sum_over_ring(part, nseq, place):
    core, pair, row = place & 1, (place >> 1) & 1, place >> 2
    lags, chans = part.shape
    size, chans = nseq // 4, chans // nseq

    def halve(part, bit, mine, kind):
        away = lax.dynamic_index_in_dim(part, 1 - mine, 1, False).astype(kind)
        away = lax.ppermute(away, "seq", [(i, i ^ bit) for i in range(nseq)])
        return lax.dynamic_index_in_dim(part, mine, 1, False) + away.astype(F32)

    kept, away = deal(core.astype(jnp.int32), part, chans, 2)
    part = kept + lax.ppermute(away, "seq", [(i, i ^ 1) for i in range(nseq)])
    part = part.reshape(2, size, lags, chans)
    left = size
    while left > 1:
        bit = size // left
        mine = (row // bit) & 1
        part = part.reshape(2 * left // 2, 2, lags, chans)
        part = halve(part, 4 * bit, mine, BF16).reshape(2, left // 2, lags, chans)
        left //= 2
    return halve(part.reshape(1, 2, lags, chans), 2, pair, BF16).reshape(lags, chans)


def links(seg_ids, place):
    own = lax.dynamic_index_in_dim(seg_ids, place, 0, False)
    prior = lax.dynamic_index_in_dim(seg_ids, jnp.maximum(place - 1, 0), 0, False)
    return (place > 0) & (own == prior)


def gathered_products(gated, cotangent, w_out):
    weights = lax.all_gather(w_out, "seq", axis=0, tiled=True)
    grad_gated = lax.dot_general(cotangent, weights, (((1,), (1,)), ((), ())), preferred_element_type=F32)
    grad_gated = lax.psum_scatter(grad_gated, "tp", scatter_dimension=1, tiled=True).astype(BF16)
    outputs = jnp.dot(
        lax.all_gather(gated, "tp", axis=1, tiled=True), weights, preferred_element_type=F32
    ).astype(BF16)
    return grad_gated, outputs


def ring_place(step, size):
    half = (size + 1) // 2
    return jnp.where(step < half, 2 * step, 2 * (size - 1 - step) + 1)


def ring_step(row, size):
    return jnp.where(row & 1 == 0, row >> 1, size - 1 - (row >> 1))


def products_kernel(size, scalars, cot_own, cot_away, gated_own, gated_away, *refs):
    pieces, (grad_own, grad_away, out_own, out_away, grad) = refs[: 4 * size], refs[4 * size :]
    rows = cot_own.shape[0]

    @pl.when(pl.program_id(0) == 0)
    def _():
        grad[...] = jnp.zeros_like(grad)

    def add(order):
        cot = jnp.concatenate([cot_own[...], cot_away[...]], 0)
        total = None
        for s in range(size):
            m = (size - s) % size
            block = (pieces[4 * s], pieces[4 * m + 2], pieces[4 * s + 1], pieces[4 * m + 3])
            block = jnp.concatenate([block[k][...] for k in order], 0)
            grad[s] += lax.dot_general(cot, block, (((1,), (1,)), ((), ())), preferred_element_type=F32)
            left = jnp.concatenate([gated_own[scalars[1 + s]], gated_away[scalars[1 + s]]], 0)
            part = jnp.dot(left, block, preferred_element_type=F32)
            total = part if total is None else total + part
        out_own[...] = total[:rows]
        out_away[...] = total[rows:].astype(BF16)

    @pl.when(scalars[0] == 0)
    def _():
        add((0, 1, 2, 3))

    @pl.when(scalars[0] != 0)
    def _():
        add((2, 3, 0, 1))

    @pl.when(pl.program_id(0) == pl.num_programs(0) - 1)
    def _():
        for s in range(size):
            grad_own[scalars[1 + s]] = grad[s, :rows].astype(BF16)
            grad_away[scalars[1 + s]] = grad[s, rows:].astype(BF16)


def products(scalars, cot_own, cot_away, gated_own, gated_away, pieces):
    rows, feats = cot_own.shape
    size, _, width = gated_own.shape
    depth = pieces[0].shape[0]
    tile = min(512, feats)
    block = pl.BlockSpec((rows, tile), lambda j, s: (0, j))
    whole = pl.BlockSpec(gated_own.shape, lambda j, s: (0, 0, 0))
    return pl.pallas_call(
        functools.partial(products_kernel, size),
        out_shape=(
            jax.ShapeDtypeStruct(gated_own.shape, BF16),
            jax.ShapeDtypeStruct(gated_own.shape, BF16),
            jax.ShapeDtypeStruct((rows, feats), F32),
            jax.ShapeDtypeStruct((rows, feats), BF16),
        ),
        grid_spec=pltpu.PrefetchScalarGridSpec(
            num_scalar_prefetch=1,
            grid=(feats // tile,),
            in_specs=[block] * 2 + [whole] * 2 + [pl.BlockSpec((depth, tile), lambda j, s: (0, j))] * len(pieces),
            out_specs=(whole, whole, block, block),
            scratch_shapes=[pltpu.VMEM((size, 2 * rows, width), F32)],
        ),
        compiler_params=pltpu.CompilerParams(vmem_limit_bytes=28 << 20),
        cost_estimate=pl.CostEstimate(
            flops=8 * rows * depth * len(pieces) * feats,
            bytes_accessed=2 * depth * len(pieces) * feats + 10 * rows * feats,
            transcendentals=0,
        ),
    )(
        scalars,
        *[
            pltpu.with_memory_space_constraint(a, pltpu.HBM)
            for a in (cot_own, cot_away, gated_own, gated_away, *pieces)
        ],
    )


def merge_kernel(scalars, own, away, out):
    size, _, width = own.shape
    for r in range(size):
        for ref, side in ((own, scalars[0]), (away, 1 - scalars[0])):
            out[:, pl.ds(pl.multiple_of((2 * r + side) * width, width), width)] = ref[r]


def merge(side, own, away):
    size, rows, width = own.shape
    vmem = pl.BlockSpec(memory_space=pltpu.VMEM)
    return pl.pallas_call(
        merge_kernel,
        out_shape=jax.ShapeDtypeStruct((rows, 2 * size * width), own.dtype),
        in_specs=[pl.BlockSpec(memory_space=pltpu.SMEM), vmem, vmem],
        out_specs=vmem,
        compiler_params=pltpu.CompilerParams(vmem_limit_bytes=GRANT),
        cost_estimate=pl.CostEstimate(flops=0, bytes_accessed=8 * own.size, transcendentals=0),
    )(side.reshape(1), own, away)


def on_ring(queries, keys, values, w_out, taps, seg_ids, cotangent):
    rows, chans = queries.shape
    length = rows
    nseq = lax.axis_size("seq")
    place = lax.axis_index("seq")
    size = nseq // 4
    core, pair, row = [i.astype(jnp.int32) for i in (place & 1, (place >> 1) & 1, place >> 2)]
    at = ring_step(row, size)
    swap_core = [(i, i ^ 1) for i in range(nseq)]
    swap_pair = [(i, i ^ 2) for i in range(nseq)]
    walk = list(range(0, size, 2)) + list(range(1, size, 2))[::-1]
    onward = [(4 * walk[i] + k, 4 * walk[(i + 1) % size] + k) for i in range(size) for k in range(4)]
    behind = [(b, a) for a, b in onward]
    later = [(i, i + 1) for i in range(nseq - 1)]
    earlier = [(i + 1, i) for i in range(nseq - 1)]
    send = functools.partial(lax.ppermute, axis_name="seq")
    tie = lax.optimization_barrier
    linked = links(seg_ids, place)
    table, high, low = spectrum_table(length)
    table_now, high_now, low_now = table[:, length:], high[:, length:], low[:, length:]
    scale = 1.0 / length

    half = rows // 2
    first, second = w_out[:half], w_out[half:]
    swapped = send(w_out, perm=swap_core)
    cot_away = send(cotangent, perm=swap_pair)
    product, cot_away = tie((mul(keys, values), cot_away))
    before = send(product, perm=later)
    filt = forward_dft(high_now, low_now, tie(taps.T), ((1,), (0,)))

    pieces = [first, swapped[:half], second, swapped[half:]]
    for step in range(1, size):
        first, second = send(first, perm=onward), send(second, perm=behind)
        swap = (first, second)
        if step == 1:
            *swap, filt = tie((*swap, filt))
        if step == 3:
            before = jnp.where(linked, before, jnp.zeros_like(before))
            data = forward_dft(high, low, jnp.concatenate([before, product], 0), ((1,), (0,)))
            filtered = inverse_dft(table_now, times(filt, data), scale).astype(BF16)
            gated = mul(queries, filtered)
            gated_own, gated_away = deal(pair, gated, chans // (2 * size))
            *swap, gated_own, gated_away = tie((*swap, gated_own, gated_away))
            gated_away = send(gated_away, perm=swap_pair)
        pieces += [first, send(swap[0], perm=swap_core), second, send(swap[1], perm=swap_core)]
    places = [core] + [ring_place(lax.rem(at - s + size, size), size) for s in range(size)]
    grad_own, grad_away, out_own, out_away = products(
        jnp.stack(places), cotangent, cot_away, gated_own, gated_away, pieces
    )
    grad_gated = merge(pair, grad_own, send(grad_away, perm=swap_pair))
    out_away = send(out_away, perm=swap_pair)
    grad_queries = mul(grad_gated, filtered)
    grad_filtered = mul(grad_gated, queries)
    grads = forward_dft(high_now, low_now, grad_filtered, ((1,), (0,)))
    back = inverse_dft(table, times_conj(grads, filt), scale)
    across = jnp.where(linked, back[:length], 0.0).astype(BF16)
    ahead = send(across, perm=earlier)
    taps_part = inverse_dft(table_now, times_conj(grads, data), scale)
    taps_grad = sum_over_ring(taps_part, nseq, place).T
    outputs = (out_own + out_away.astype(F32)).astype(BF16)
    grad_product = (back[length:] + ahead.astype(F32)).astype(BF16)
    grad_keys = mul(grad_product, values)
    grad_values = mul(grad_product, keys)
    return (outputs, grad_queries, grad_keys, grad_values, taps_grad)


def on_device(queries, keys, values, w_out, taps, seg_ids, cotangent):
    rows, chans = queries.shape
    length = taps.shape[1]
    assert rows == length
    nseq = lax.axis_size("seq")
    place = lax.axis_index("seq")
    table, high, low = spectrum_table(length)
    table_now, high_now, low_now = table[:, length:], high[:, length:], low[:, length:]
    scale = 1.0 / length
    later = [(i, i + 1) for i in range(nseq - 1)]
    earlier = [(i + 1, i) for i in range(nseq - 1)]
    linked = links(seg_ids, place)

    product = mul(keys, values)
    before = lax.ppermute(product, "seq", later)
    before = jnp.where(linked, before, jnp.zeros_like(before))
    data = forward_dft(high, low, jnp.concatenate([before, product], 0), ((1,), (0,)))
    filt = forward_dft(high_now, low_now, taps, ((1,), (1,)))
    filtered = inverse_dft(table_now, times(filt, data), scale).astype(BF16)
    gated = mul(queries, filtered)

    grad_gated, outputs = gathered_products(gated, cotangent, w_out)
    grad_queries = mul(grad_gated, filtered)
    grad_filtered = mul(grad_gated, queries)
    grads = forward_dft(high_now, low_now, grad_filtered, ((1,), (0,)))
    back = inverse_dft(table, times_conj(grads, filt), scale)
    across = jnp.where(linked, back[:length], 0.0).astype(BF16)
    ahead = lax.ppermute(across, "seq", earlier)
    taps_part = inverse_dft(table_now, times_conj(grads, data), scale)
    taps_grad = scatter_sum(taps_part, nseq, place, ()).T
    grad_product = (back[length:] + ahead.astype(F32)).astype(BF16)
    grad_keys = mul(grad_product, values)
    grad_values = mul(grad_product, keys)
    return (outputs, grad_queries, grad_keys, grad_values, taps_grad)


def solution(mesh):
    block = P("seq", "tp")
    count = mesh.shape["seq"]
    ring = mesh.shape["tp"] == 1 and count & (count - 1) == 0 and count >= 16

    def run(queries, keys, values, w_out, taps, seg_ids, cotangent):
        rows, chans = queries.shape
        place = on_ring if ring and rows * count == chans else on_device
        return place(queries, keys, values, w_out, taps, seg_ids, cotangent)

    return jax.shard_map(
        run,
        mesh=mesh,
        in_specs=(block, block, block, block, P("tp", None), P(), block),
        out_specs=(block, block, block, block, P(("tp", "seq"), None)),
        check_vma=False,
    )
```

profile of v0, /device:TPU:0, one launch (start us, length us, event | category | flops | bytes accessed | tf_op | source)
XLA Modules:
  0.0 195.9 jit_solution(5404221762979032809)
XLA Ops:
  0.7 3.0 %collective-permute-start = (bf16[128,4096]{1,0:T(8,128)(2,1)}, bf16[128,4096]{1,0:T(8,128)(2,1)}, u32[]{:S(2)}, u32[]{:S(2)}) collective-permute-start(bf16[128,4096]{1,0:T(8,128)(2,1)} %cot_own.1), channel_id=1, source_target_pairs={{0,2},{1,3},{2,0},{3,1},{4,6},{5,7},{6,4},{7,5},{8,10},{9,11},{10,... | collective-permute-start | bytes 3145736 | tf_op jit(solution)/shard_map/ppermute | solution.py:270
  8.6 2.6 %copy.48 = bf16[128,4096]{0,1:T(8,128)(2,1)} copy(bf16[128,4096]{1,0:T(8,128)(2,1)} %param.15) | data formatting | bytes 2097152 | tf_op args[2]
  12.8 7.7 %collective-permute-done.1.refs_4_ = bf16[64,4096]{1,0:T(8,128)(2,1)} collective-permute-done((bf16[64,4096]{1,0:T(8,128)(2,1)}, bf16[64,4096]{1,0:T(8,128)(2,1)}, u32[]{:S(2)}, u32[]{:S(2)}) %collective-permute-start.1) | collective-permute-done | bytes 524320 | tf_op jit(solution)/shard_map/ppermute | solution.py:277
  22.6 2.7 %fusion.77 = f32[256,4096]{1,0:T(8,128)} fusion(bf16[256,128]{1,0:T(8,128)(2,1)S(1)} %copy-done.20, bf16[128,4096]{0,1:T(8,128)(2,1)S(1)} %bitcast.64), kind=kOutput, calls=%fused_computation.100 | convolution fusion | flops 268435456 | bytes 5308416 | tf_op jit(solution)/shard_map/dot_general | solution.py:25
  28.6 2.9 %convolution_add_fusion.4 = f32[256,4096]{1,0:T(8,128)S(1)} fusion(f32[256,4096]{1,0:T(8,128)} %fusion.77, bf16[256,128]{1,0:T(8,128)(2,1)S(1)} %copy-done.19, bf16[128,4096]{0,1:T(8,128)(2,1)S(1)} %bitcast.63), kind=kOutput, calls=%fused_computation.9 | convolution fusion | flops 269484032 | bytes 9502720 | tf_op jit(solution)/shard_map/dot_general | solution.py:26
  31.5 2.4 %collective-permute-start.10 = (bf16[64,4096]{1,0:T(8,128)(2,1)}, bf16[64,4096]{1,0:T(8,128)(2,1)S(1)}, u32[]{:S(2)}, u32[]{:S(2)}) collective-permute-start(bf16[64,4096]{1,0:T(8,128)(2,1)} %collective-permute-done.1.refs_4_), channel_id=1, source_target_pairs={{0,1},{1,0},{2,3},{3,2},{4,5},{5,4},{6,7},{7,6},{8,9},{9,8},{10,11... | collective-permute-start | bytes 1572872 | tf_op jit(solution)/shard_map/ppermute | solution.py:289
  35.9 10.3 %collective-permute-done.5.refs_10_ = bf16[64,4096]{1,0:T(8,128)(2,1)S(1)} collective-permute-done((bf16[64,4096]{1,0:T(8,128)(2,1)}, bf16[64,4096]{1,0:T(8,128)(2,1)S(1)}, u32[]{:S(2)}, u32[]{:S(2)}) %collective-permute-start.5) | collective-permute-done | bytes 524320 | tf_op jit(solution)/shard_map/ppermute | solution.py:277
  46.2 2.4 %collective-permute-start.6 = (bf16[64,4096]{1,0:T(8,128)(2,1)S(1)}, bf16[64,4096]{1,0:T(8,128)(2,1)S(1)}, u32[]{:S(2)}, u32[]{:S(2)}) collective-permute-start(bf16[64,4096]{1,0:T(8,128)(2,1)S(1)} %collective-permute-done.5.refs_10_), channel_id=1, source_target_pairs={{8,0},{9,1},{10,2},{11,3},{16,8},{17,9},{18,10},{19,11},{24,16},{2... | collective-permute-start | bytes 1572872 | tf_op jit(solution)/shard_map/ppermute | solution.py:277
  50.1 8.0 %collective-permute-done.6.refs_14_ = bf16[64,4096]{1,0:T(8,128)(2,1)S(1)} collective-permute-done((bf16[64,4096]{1,0:T(8,128)(2,1)S(1)}, bf16[64,4096]{1,0:T(8,128)(2,1)S(1)}, u32[]{:S(2)}, u32[]{:S(2)}) %collective-permute-start.6) | collective-permute-done | bytes 524320 | tf_op jit(solution)/shard_map/ppermute | solution.py:277
  58.2 2.5 %collective-permute-start.18 = (bf16[64,4096]{1,0:T(8,128)(2,1)S(1)}, bf16[64,4096]{1,0:T(8,128)(2,1)S(1)}, u32[]{:S(2)}, u32[]{:S(2)}) collective-permute-start(bf16[64,4096]{1,0:T(8,128)(2,1)S(1)} %collective-permute-done.6.refs_14_), channel_id=1, source_target_pairs={{8,0},{9,1},{10,2},{11,3},{16,8},{17,9},{18,10},{19,11},{24,16},{2... | collective-permute-start | bytes 1572872 | tf_op jit(solution)/shard_map/ppermute | solution.py:277
  62.9 6.7 %collective-permute-done.16.refs_16_ = bf16[64,4096]{1,0:T(8,128)(2,1)} collective-permute-done((bf16[64,4096]{1,0:T(8,128)(2,1)S(1)}, bf16[64,4096]{1,0:T(8,128)(2,1)}, u32[]{:S(2)}, u32[]{:S(2)}) %collective-permute-start.16) | collective-permute-done | bytes 524320 | tf_op jit(solution)/shard_map/ppermute | solution.py:277
  72.9 2.7 %fusion.12 = (bf16[128,4096]{1,0:T(8,128)(2,1)S(1)}, f32[128,4096]{1,0:T(8,128)}) fusion(bf16[128,4096]{1,0:T(8,128)(2,1)S(1)} %copy-done.12, f32[4096,128]{0,1:T(8,128)S(1)} %fusion.36, f32[128,128]{1,0:T(8,128)S(1)} %copy-done.21, f32[256,4096]{1,0:T(8,128)S(1)} %fusion.4, f32[256,4096]{1,0:T(8,128)S(1)} %convolution_add_fusion.4), kind=kOutput, calls=%fused_computation.25 | convolution fusion | flops 407896064 | bytes 14745600 | tf_op jit(solution)/shard_map/dot_general | solution.py:43
  79.1 2.4 %collective-permute-start.24 = (bf16[64,4096]{1,0:T(8,128)(2,1)}, bf16[64,4096]{1,0:T(8,128)(2,1)}, u32[]{:S(2)}, u32[]{:S(2)}) collective-permute-start(bf16[64,4096]{1,0:T(8,128)(2,1)} %collective-permute-done.20.refs_20_), channel_id=1, source_target_pairs={{0,8},{1,9},{2,10},{3,11},{8,16},{9,17},{10,18},{11,19},{16,24},{1... | collective-permute-start | bytes 1572872 | tf_op jit(solution)/shard_map/ppermute | solution.py:277
  82.4 2.7 %collective-permute-start.26 = (bf16[64,4096]{1,0:T(8,128)(2,1)S(1)}, bf16[64,4096]{1,0:T(8,128)(2,1)}, u32[]{:S(2)}, u32[]{:S(2)}) collective-permute-start(bf16[64,4096]{1,0:T(8,128)(2,1)S(1)} %collective-permute-done.22.refs_22_), channel_id=1, source_target_pairs={{8,0},{9,1},{10,2},{11,3},{16,8},{17,9},{18,10},{19,11},{24,16},{2... | collective-permute-start | bytes 1572872 | tf_op jit(solution)/shard_map/ppermute | solution.py:277
  85.6 5.5 %collective-permute-done.8.gated_away = bf16[8,128,256]{2,1,0:T(8,128)(2,1)S(1)} collective-permute-done((bf16[8,128,256]{2,1,0:T(8,128)(2,1)S(1)}, bf16[8,128,256]{2,1,0:T(8,128)(2,1)S(1)}, u32[]{:S(2)}, u32[]{:S(2)}) %collective-permute-start.8) | collective-permute-done | bytes 524320 | tf_op jit(solution)/shard_map/ppermute | solution.py:288
  91.1 5.6 %collective-permute-done.24.refs_24_ = bf16[64,4096]{1,0:T(8,128)(2,1)} collective-permute-done((bf16[64,4096]{1,0:T(8,128)(2,1)}, bf16[64,4096]{1,0:T(8,128)(2,1)}, u32[]{:S(2)}, u32[]{:S(2)}) %collective-permute-start.24) | collective-permute-done | bytes 524320 | tf_op jit(solution)/shard_map/ppermute | solution.py:277
  96.9 2.9 %collective-permute-start.30 = (bf16[64,4096]{1,0:T(8,128)(2,1)}, bf16[64,4096]{1,0:T(8,128)(2,1)}, u32[]{:S(2)}, u32[]{:S(2)}) collective-permute-start(bf16[64,4096]{1,0:T(8,128)(2,1)} %collective-permute-done.26.refs_26_), channel_id=1, source_target_pairs={{8,0},{9,1},{10,2},{11,3},{16,8},{17,9},{18,10},{19,11},{24,16},{2... | collective-permute-start | bytes 1572872 | tf_op jit(solution)/shard_map/ppermute | solution.py:277
  100.5 10.3 %collective-permute-done.28.refs_28_ = bf16[64,4096]{1,0:T(8,128)(2,1)} collective-permute-done((bf16[64,4096]{1,0:T(8,128)(2,1)}, bf16[64,4096]{1,0:T(8,128)(2,1)}, u32[]{:S(2)}, u32[]{:S(2)}) %collective-permute-start.28) | collective-permute-done | bytes 524320 | tf_op jit(solution)/shard_map/ppermute | solution.py:277
  115.2 14.6 %shard_map.165 = (bf16[8,128,256]{2,1,0:T(8,128)(2,1)S(1)}, bf16[8,128,256]{2,1,0:T(8,128)(2,1)S(1)}, f32[128,4096]{1,0:T(8,128)S(1)}, bf16[128,4096]{1,0:T(8,128)(2,1)S(1)}) custom-call(s32[9]{0:T(128)S(1)} %stack.39.scalars, bf16[128,4096]{1,0:T(8,128)(2,1)} %cot_own.1, bf16[128,4096]{1,0:T(8,128)(2,1)} %collective-permute-done.cot_away, ...), custom_call_target="tpu_custom_call" | custom-call | flops 8589934592 | bytes 22020096 | tf_op jit(solution)/shard_map/pallas_call | solution.py:195
  129.9 13.8 %collective-permute-done.33.away = bf16[8,128,256]{2,1,0:T(8,128)(2,1)S(1)} collective-permute-done((bf16[8,128,256]{2,1,0:T(8,128)(2,1)S(1)}, bf16[8,128,256]{2,1,0:T(8,128)(2,1)S(1)}, u32[]{:S(2)}, u32[]{:S(2)}) %collective-permute-start.33) | collective-permute-done | bytes 524320 | tf_op jit(solution)/shard_map/ppermute | solution.py:294
  152.8 5.9 %fusion.29 = f32[4096,256]{1,0:T(8,128)S(1)} fusion(f32[128,256]{1,0:T(8,128)S(1)} %copy-done.24, f32[256,4096]{1,0:T(8,128)} %copy-done.10, f32[256,4096]{1,0:T(8,128)} %copy-done.6), kind=kOutput, calls=%fused_computation.44 | convolution fusion | flops 806879232 | bytes 12713984 | tf_op jit(solution)/shard_map/dot_general | solution.py:43
  165.9 5.1 %collective-permute-done.36 = bf16[8,128,128]{2,1,0:T(8,128)(2,1)S(1)} collective-permute-done((bf16[8,128,128]{2,1,0:T(8,128)(2,1)S(1)}, bf16[8,128,128]{2,1,0:T(8,128)(2,1)S(1)}, u32[]{:S(2)}, u32[]{:S(2)}) %collective-permute-start.36) | collective-permute-done | bytes 262176 | tf_op jit(solution)/shard_map/ppermute | solution.py:110
  174.1 11.7 %collective-permute-done.37 = bf16[4,128,128]{2,1,0:T(8,128)(2,1)S(1)} collective-permute-done((bf16[4,128,128]{2,1,0:T(8,128)(2,1)S(1)}, bf16[4,128,128]{2,1,0:T(8,128)(2,1)S(1)}, u32[]{:S(2)}, u32[]{:S(2)}) %collective-permute-start.37) | collective-permute-done | bytes 131104 | tf_op jit(solution)/shard_map/ppermute | solution.py:110
  185.9 2.8 %collective-permute-start.38 = (bf16[2,128,128]{2,1,0:T(8,128)(2,1)S(1)}, bf16[2,128,128]{2,1,0:T(8,128)(2,1)S(1)}, u32[]{:S(2)}, u32[]{:S(2)}) collective-permute-start(bf16[2,128,128]{2,1,0:T(8,128)(2,1)S(1)} %fusion.71), channel_id=1, source_target_pairs={{0,16},{1,17},{2,18},{3,19},{4,20},{5,21},{6,22},{7,23},{8,24},{9,... | collective-permute-start | bytes 196616 | tf_op jit(solution)/shard_map/ppermute | solution.py:110
  (189 shorter events, 55.8 us)
Async XLA Ops:
  0.7 26.6 %collective-permute-start = (bf16[128,4096]{1,0:T(8,128)(2,1)}, bf16[128,4096]{1,0:T(8,128)(2,1)}, u32[]{:S(2)}, u32[]{:S(2)}) collective-permute-start(bf16[128,4096]{1,0:T(8,128)(2,1)} %cot_own.1), channel_id=1, source_target_pairs={{0,2},{1,3},{2,0},{3,1},{4,6},{5,7},{6,4},{7,5},{8,10},{9,11},{10,... | collective-permute-start | bytes 3145736 | tf_op jit(solution)/shard_map/ppermute | solution.py:270
  3.7 72.9 %collective-permute-start.9 = (bf16[128,4096]{1,0:T(8,128)(2,1)}, bf16[128,4096]{1,0:T(8,128)(2,1)}, u32[]{:S(2)}, u32[]{:S(2)}) collective-permute-start(bf16[128,4096]{1,0:T(8,128)(2,1)} %param.16), channel_id=1, source_target_pairs={{0,1},{1,0},{2,3},{3,2},{4,5},{5,4},{6,7},{7,6},{8,9},{9,8},{10,11... | collective-permute-start | bytes 3145736 | tf_op jit(solution)/shard_map/ppermute | solution.py:269
  5.9 14.7 %collective-permute-start.1 = (bf16[64,4096]{1,0:T(8,128)(2,1)}, bf16[64,4096]{1,0:T(8,128)(2,1)}, u32[]{:S(2)}, u32[]{:S(2)}) collective-permute-start(bf16[64,4096]{1,0:T(8,128)(2,1)} %get-tuple-element.59.refs_0_), channel_id=1, source_target_pairs={{0,8},{1,9},{2,10},{3,11},{8,16},{9,17},{10,18},{11,19},{16,24},{1... | collective-permute-start | bytes 1572872 | tf_op jit(solution)/shard_map/ppermute | solution.py:277
  7.5 14.7 %collective-permute-start.4 = (bf16[64,4096]{1,0:T(8,128)(2,1)}, bf16[64,4096]{1,0:T(8,128)(2,1)}, u32[]{:S(2)}, u32[]{:S(2)}) collective-permute-start(bf16[64,4096]{1,0:T(8,128)(2,1)} %get-tuple-element.58.refs_2_), channel_id=1, source_target_pairs={{8,0},{9,1},{10,2},{11,3},{16,8},{17,9},{18,10},{19,11},{24,16},{2... | collective-permute-start | bytes 1572872 | tf_op jit(solution)/shard_map/ppermute | solution.py:277
  20.6 13.8 %collective-permute-start.2 = (bf16[64,4096]{1,0:T(8,128)(2,1)}, bf16[64,4096]{1,0:T(8,128)(2,1)S(1)}, u32[]{:S(2)}, u32[]{:S(2)}) collective-permute-start(bf16[64,4096]{1,0:T(8,128)(2,1)} %collective-permute-done.1.refs_4_), channel_id=1, source_target_pairs={{0,8},{1,9},{2,10},{3,11},{8,16},{9,17},{10,18},{11,19},{16,24},{1... | collective-permute-start | bytes 1572872 | tf_op jit(solution)/shard_map/ppermute | solution.py:277
  22.2 24.1 %collective-permute-start.5 = (bf16[64,4096]{1,0:T(8,128)(2,1)}, bf16[64,4096]{1,0:T(8,128)(2,1)S(1)}, u32[]{:S(2)}, u32[]{:S(2)}) collective-permute-start(bf16[64,4096]{1,0:T(8,128)(2,1)} %collective-permute-done.4.refs_6_), channel_id=1, source_target_pairs={{8,0},{9,1},{10,2},{11,3},{16,8},{17,9},{18,10},{19,11},{24,16},{2... | collective-permute-start | bytes 1572872 | tf_op jit(solution)/shard_map/ppermute | solution.py:277
  27.2 30.9 %collective-permute-start.7 = (bf16[128,4096]{0,1:T(8,128)(2,1)S(1)}, bf16[128,4096]{0,1:T(8,128)(2,1)S(1)}, u32[]{:S(2)}, u32[]{:S(2)}) collective-permute-start(bf16[128,4096]{0,1:T(8,128)(2,1)S(1)} %fusion.11), channel_id=1, source_target_pairs={{0,1},{1,2},{2,3},{3,4},{4,5},{5,6},{6,7},{7,8},{8,9},{9,10},{10,1... | collective-permute-start | bytes 3145736 | tf_op jit(solution)/shard_map/ppermute | solution.py:272
  31.5 30.7 %collective-permute-start.10 = (bf16[64,4096]{1,0:T(8,128)(2,1)}, bf16[64,4096]{1,0:T(8,128)(2,1)S(1)}, u32[]{:S(2)}, u32[]{:S(2)}) collective-permute-start(bf16[64,4096]{1,0:T(8,128)(2,1)} %collective-permute-done.1.refs_4_), channel_id=1, source_target_pairs={{0,1},{1,0},{2,3},{3,2},{4,5},{5,4},{6,7},{7,6},{8,9},{9,8},{10,11... | collective-permute-start | bytes 1572872 | tf_op jit(solution)/shard_map/ppermute | solution.py:289
  34.4 15.7 %collective-permute-start.3 = (bf16[64,4096]{1,0:T(8,128)(2,1)S(1)}, bf16[64,4096]{1,0:T(8,128)(2,1)S(1)}, u32[]{:S(2)}, u32[]{:S(2)}) collective-permute-start(bf16[64,4096]{1,0:T(8,128)(2,1)S(1)} %collective-permute-done.2.refs_8_), channel_id=1, source_target_pairs={{0,8},{1,9},{2,10},{3,11},{8,16},{9,17},{10,18},{11,19},{16,24},{1... | collective-permute-start | bytes 1572872 | tf_op jit(solution)/shard_map/ppermute | solution.py:277
  62.2 14.4 %collective-permute-start.12 = (bf16[64,4096]{1,0:T(8,128)(2,1)S(1)}, bf16[64,4096]{1,0:T(8,128)(2,1)S(1)}, u32[]{:S(2)}, u32[]{:S(2)}) collective-permute-start(bf16[64,4096]{1,0:T(8,128)(2,1)S(1)} %collective-permute-done.2.refs_8_), channel_id=1, source_target_pairs={{0,1},{1,0},{2,3},{3,2},{4,5},{5,4},{6,7},{7,6},{8,9},{9,8},{10,11... | collective-permute-start | bytes 1572872 | tf_op jit(solution)/shard_map/ppermute | solution.py:289
  62.3 14.8 %collective-permute-start.13 = (bf16[64,4096]{1,0:T(8,128)(2,1)S(1)}, bf16[64,4096]{1,0:T(8,128)(2,1)S(1)}, u32[]{:S(2)}, u32[]{:S(2)}) collective-permute-start(bf16[64,4096]{1,0:T(8,128)(2,1)S(1)} %collective-permute-done.5.refs_10_), channel_id=1, source_target_pairs={{0,1},{1,0},{2,3},{3,2},{4,5},{5,4},{6,7},{7,6},{8,9},{9,8},{10,11... | collective-permute-start | bytes 1572872 | tf_op jit(solution)/shard_map/ppermute | solution.py:289
  77.2 13.9 %collective-permute-start.8 = (bf16[8,128,256]{2,1,0:T(8,128)(2,1)S(1)}, bf16[8,128,256]{2,1,0:T(8,128)(2,1)S(1)}, u32[]{:S(2)}, u32[]{:S(2)}) collective-permute-start(bf16[8,128,256]{2,1,0:T(8,128)(2,1)S(1)} %get-tuple-element.28), channel_id=1, source_target_pairs={{0,2},{1,3},{2,0},{3,1},{4,6},{5,7},{6,4},{7,5},{8,10},{9,11},{10,... | collective-permute-start | bytes 1572872 | tf_op jit(solution)/shard_map/ppermute | solution.py:288
  79.1 17.6 %collective-permute-start.24 = (bf16[64,4096]{1,0:T(8,128)(2,1)}, bf16[64,4096]{1,0:T(8,128)(2,1)}, u32[]{:S(2)}, u32[]{:S(2)}) collective-permute-start(bf16[64,4096]{1,0:T(8,128)(2,1)} %collective-permute-done.20.refs_20_), channel_id=1, source_target_pairs={{0,8},{1,9},{2,10},{3,11},{8,16},{9,17},{10,18},{11,19},{16,24},{1... | collective-permute-start | bytes 1572872 | tf_op jit(solution)/shard_map/ppermute | solution.py:277
  82.4 14.5 %collective-permute-start.26 = (bf16[64,4096]{1,0:T(8,128)(2,1)S(1)}, bf16[64,4096]{1,0:T(8,128)(2,1)}, u32[]{:S(2)}, u32[]{:S(2)}) collective-permute-start(bf16[64,4096]{1,0:T(8,128)(2,1)S(1)} %collective-permute-done.22.refs_22_), channel_id=1, source_target_pairs={{8,0},{9,1},{10,2},{11,3},{16,8},{17,9},{18,10},{19,11},{24,16},{2... | collective-permute-start | bytes 1572872 | tf_op jit(solution)/shard_map/ppermute | solution.py:277
  85.1 14.8 %collective-permute-start.17 = (bf16[64,4096]{1,0:T(8,128)(2,1)}, bf16[64,4096]{1,0:T(8,128)(2,1)}, u32[]{:S(2)}, u32[]{:S(2)}) collective-permute-start(bf16[64,4096]{1,0:T(8,128)(2,1)} %collective-permute-done.16.refs_16_), channel_id=1, source_target_pairs={{0,1},{1,0},{2,3},{3,2},{4,5},{5,4},{6,7},{7,6},{8,9},{9,8},{10,11... | collective-permute-start | bytes 1572872 | tf_op jit(solution)/shard_map/ppermute | solution.py:289
  85.1 14.8 %collective-permute-start.19 = (bf16[64,4096]{1,0:T(8,128)(2,1)S(1)}, bf16[64,4096]{1,0:T(8,128)(2,1)}, u32[]{:S(2)}, u32[]{:S(2)}) collective-permute-start(bf16[64,4096]{1,0:T(8,128)(2,1)S(1)} %collective-permute-done.18.refs_18_), channel_id=1, source_target_pairs={{0,1},{1,0},{2,3},{3,2},{4,5},{5,4},{6,7},{7,6},{8,9},{9,8},{10,11... | collective-permute-start | bytes 1572872 | tf_op jit(solution)/shard_map/ppermute | solution.py:289
  96.7 14.1 %collective-permute-start.28 = (bf16[64,4096]{1,0:T(8,128)(2,1)}, bf16[64,4096]{1,0:T(8,128)(2,1)}, u32[]{:S(2)}, u32[]{:S(2)}) collective-permute-start(bf16[64,4096]{1,0:T(8,128)(2,1)} %collective-permute-done.24.refs_24_), channel_id=1, source_target_pairs={{0,8},{1,9},{2,10},{3,11},{8,16},{9,17},{10,18},{11,19},{16,24},{1... | collective-permute-start | bytes 1572872 | tf_op jit(solution)/shard_map/ppermute | solution.py:277
  96.9 14.0 %collective-permute-start.30 = (bf16[64,4096]{1,0:T(8,128)(2,1)}, bf16[64,4096]{1,0:T(8,128)(2,1)}, u32[]{:S(2)}, u32[]{:S(2)}) collective-permute-start(bf16[64,4096]{1,0:T(8,128)(2,1)} %collective-permute-done.26.refs_26_), channel_id=1, source_target_pairs={{8,0},{9,1},{10,2},{11,3},{16,8},{17,9},{18,10},{19,11},{24,16},{2... | collective-permute-start | bytes 1572872 | tf_op jit(solution)/shard_map/ppermute | solution.py:277
  99.9 13.8 %collective-permute-start.23 = (bf16[64,4096]{1,0:T(8,128)(2,1)}, bf16[64,4096]{1,0:T(8,128)(2,1)S(1)}, u32[]{:S(2)}, u32[]{:S(2)}) collective-permute-start(bf16[64,4096]{1,0:T(8,128)(2,1)} %copy-done.37), channel_id=1, source_target_pairs={{0,1},{1,0},{2,3},{3,2},{4,5},{5,4},{6,7},{7,6},{8,9},{9,8},{10,11... | collective-permute-start | bytes 1572872 | tf_op jit(solution)/shard_map/ppermute | solution.py:289
  99.9 13.7 %collective-permute-start.25 = (bf16[64,4096]{1,0:T(8,128)(2,1)}, bf16[64,4096]{1,0:T(8,128)(2,1)S(1)}, u32[]{:S(2)}, u32[]{:S(2)}) collective-permute-start(bf16[64,4096]{1,0:T(8,128)(2,1)} %collective-permute-done.24.refs_24_), channel_id=1, source_target_pairs={{0,1},{1,0},{2,3},{3,2},{4,5},{5,4},{6,7},{7,6},{8,9},{9,8},{10,11... | collective-permute-start | bytes 1572872 | tf_op jit(solution)/shard_map/ppermute | solution.py:289
  129.9 13.9 %collective-permute-start.33 = (bf16[8,128,256]{2,1,0:T(8,128)(2,1)S(1)}, bf16[8,128,256]{2,1,0:T(8,128)(2,1)S(1)}, u32[]{:S(2)}, u32[]{:S(2)}) collective-permute-start(bf16[8,128,256]{2,1,0:T(8,128)(2,1)S(1)} %get-tuple-element.36), channel_id=1, source_target_pairs={{0,2},{1,3},{2,0},{3,1},{4,6},{5,7},{6,4},{7,5},{8,10},{9,11},{10,... | collective-permute-start | bytes 1572872 | tf_op jit(solution)/shard_map/ppermute | solution.py:294
  152.5 36.3 %collective-permute-start.32 = (bf16[128,4096]{1,0:T(8,128)(2,1)}, bf16[128,4096]{1,0:T(8,128)(2,1)S(1)}, u32[]{:S(2)}, u32[]{:S(2)}) collective-permute-start(bf16[128,4096]{1,0:T(8,128)(2,1)} %copy-done.4), channel_id=1, source_target_pairs={{0,2},{1,3},{2,0},{3,1},{4,6},{5,7},{6,4},{7,5},{8,10},{9,11},{10,... | collective-permute-start | bytes 3145736 | tf_op jit(solution)/shard_map/ppermute | solution.py:295
  164.6 26.6 %collective-permute-start.34 = (bf16[128,4096]{0,1:T(8,128)(2,1)S(1)}, bf16[128,4096]{0,1:T(8,128)(2,1)S(1)}, u32[]{:S(2)}, u32[]{:S(2)}) collective-permute-start(bf16[128,4096]{0,1:T(8,128)(2,1)S(1)} %fusion.17), channel_id=1, source_target_pairs={{1,0},{2,1},{3,2},{4,3},{5,4},{6,5},{7,6},{8,7},{9,8},{10,9},{11,1... | collective-permute-start | bytes 3145736 | tf_op jit(solution)/shard_map/ppermute | solution.py:301
  171.1 14.7 %collective-permute-start.37 = (bf16[4,128,128]{2,1,0:T(8,128)(2,1)S(1)}, bf16[4,128,128]{2,1,0:T(8,128)(2,1)S(1)}, u32[]{:S(2)}, u32[]{:S(2)}) collective-permute-start(bf16[4,128,128]{2,1,0:T(8,128)(2,1)S(1)} %fusion.70), channel_id=1, source_target_pairs={{0,8},{1,9},{2,10},{3,11},{4,12},{5,13},{6,14},{7,15},{8,0},{9,1},... | collective-permute-start | bytes 393224 | tf_op jit(solution)/shard_map/ppermute | solution.py:110
  (62 other events, 658.5 us)
where the time goes:
time: 196 us
  waiting for transfers between devices  90.1 us (46%)
  starting transfers between devices  38.4 us (20%)
  matrix products  24.8 us (13%)
  local copies, waits for them, and re-layouts  17.5 us (9%)
  Pallas kernels  16.1 us (8%)
  other arithmetic  6.18 us (3%)
  between operations  2.75 us (1%)
    ppermute x14, waiting for transfers between devices, on_ring(): first, second = (send(first, perm=onward), send(second, perm=behind))  52.1 us
    ppermute x14, starting transfers between devices, on_ring(): first, second = (send(first, perm=onward), send(second, perm=behind))  20.5 us
    ppermute x4, waiting for transfers between devices, halve(): away = lax.ppermute(away, 'seq', [(i, i ^ bit) for i in range(nseq)])  18.7 us
    dot_general x6, matrix products, inverse_dft(): lax.dot_general(table, spectrum, (((0,), (0,)), ((), ())), precision=lax....  14.8 us
    pallas_call x1, Pallas kernels, products(): pl.pallas_call(functools.partial(products_kernel, size), out_shape=(jax.S...  14.6 us
    ppermute x1, waiting for transfers between devices, on_ring(): grad_gated = merge(pair, grad_own, send(grad_away, perm=swap_pair))  13.8 us
    unnamed x97, local copies, waits for them, and re-layouts  12.2 us
    ppermute x4, starting transfers between devices, halve(): away = lax.ppermute(away, 'seq', [(i, i ^ bit) for i in range(nseq)])  6.51 us
  transfers between devices with their start and end apart: 40, of which 16 were waited for; matrix products, arithmetic and copies ran while one was open for 19% of the time, Pallas kernels for 0%

commit v1 on v0

--- a/solution.py
+++ b/solution.py
@@ -100,7 +100,7 @@
     )(side.reshape(1), data)
 
 
-def sum_over_ring(part, nseq, place):
+def sum_over_ring(part, nseq, place, guest):
     core, pair, row = place & 1, (place >> 1) & 1, place >> 2
     lags, chans = part.shape
     size, chans = nseq // 4, chans // nseq
@@ -119,8 +119,10 @@
         mine = (row // bit) & 1
         part = part.reshape(2 * left // 2, 2, lags, chans)
         part = halve(part, 4 * bit, mine, BF16).reshape(2, left // 2, lags, chans)
+        if left == size:
+            part, guest = lax.optimization_barrier((part, guest))
         left //= 2
-    return halve(part.reshape(1, 2, lags, chans), 2, pair, BF16).reshape(lags, chans)
+    return halve(part.reshape(1, 2, lags, chans), 2, pair, BF16).reshape(lags, chans), guest
 
 
 def links(seg_ids, place):
@@ -148,8 +150,10 @@
     return jnp.where(row & 1 == 0, row >> 1, size - 1 - (row >> 1))
 
 
-def products_kernel(size, scalars, cot_own, cot_away, gated_own, gated_away, *refs):
-    pieces, (grad_own, grad_away, out_own, out_away, grad) = refs[: 4 * size], refs[4 * size :]
+def products_kernel(count, last, scalars, cot_own, cot_away, gated_own, gated_away, *refs):
+    pieces, refs = refs[: 4 * count], refs[4 * count :]
+    before, refs = (refs[:1], refs[1:]) if last else ((), refs)
+    grad_own, grad_away, *outs, grad = refs
     rows = cot_own.shape[0]
 
     @pl.when(pl.program_id(0) == 0)
@@ -158,17 +162,18 @@
 
     def add(order):
         cot = jnp.concatenate([cot_own[...], cot_away[...]], 0)
-        total = None
-        for s in range(size):
-            m = (size - s) % size
-            block = (pieces[4 * s], pieces[4 * m + 2], pieces[4 * s + 1], pieces[4 * m + 3])
-            block = jnp.concatenate([block[k][...] for k in order], 0)
+        total = before[0][...] if last else None
+        for s in range(count):
+            block = jnp.concatenate([pieces[4 * s + k][...] for k in order], 0)
             grad[s] += lax.dot_general(cot, block, (((1,), (1,)), ((), ())), preferred_element_type=F32)
             left = jnp.concatenate([gated_own[scalars[1 + s]], gated_away[scalars[1 + s]]], 0)
             part = jnp.dot(left, block, preferred_element_type=F32)
             total = part if total is None else total + part
-        out_own[...] = total[:rows]
-        out_away[...] = total[rows:].astype(BF16)
+        if last:
+            outs[0][...] = total[:rows]
+            outs[1][...] = total[rows:].astype(BF16)
+        else:
+            outs[0][...] = total
 
     @pl.when(scalars[0] == 0)
     def _():
@@ -180,66 +185,75 @@
 
     @pl.when(pl.program_id(0) == pl.num_programs(0) - 1)
     def _():
-        for s in range(size):
-            grad_own[scalars[1 + s]] = grad[s, :rows].astype(BF16)
-            grad_away[scalars[1 + s]] = grad[s, rows:].astype(BF16)
-
-
-def products(scalars, cot_own, cot_away, gated_own, gated_away, pieces):
+        for s in range(count):
+            grad_own[s] = grad[s, :rows].astype(BF16)
+            grad_away[s] = grad[s, rows:].astype(BF16)
+
+
+def products(scalars, cot_own, cot_away, gated_own, gated_away, groups, before=None):
     rows, feats = cot_own.shape
-    size, _, width = gated_own.shape
+    width = gated_own.shape[2]
+    count = len(groups)
+    pieces = [p for group in groups for p in group]
     depth = pieces[0].shape[0]
     tile = min(512, feats)
+    last = before is not None
     block = pl.BlockSpec((rows, tile), lambda j, s: (0, j))
+    double = pl.BlockSpec((2 * rows, tile), lambda j, s: (0, j))
     whole = pl.BlockSpec(gated_own.shape, lambda j, s: (0, 0, 0))
+    part = pl.BlockSpec((count, rows, width), lambda j, s: (0, 0, 0))
+    grad = (jax.ShapeDtypeStruct((count, rows, width), BF16), pltpu.HBM((count, rows, width), BF16))
+    halves = (pltpu.HBM((rows, feats), F32), pltpu.HBM((rows, feats), BF16))
     return pl.pallas_call(
-        functools.partial(products_kernel, size),
-        out_shape=(
-            jax.ShapeDtypeStruct(gated_own.shape, BF16),
-            jax.ShapeDtypeStruct(gated_own.shape, BF16),
-            jax.ShapeDtypeStruct((rows, feats), F32),
-            jax.ShapeDtypeStruct((rows, feats), BF16),
-        ),
+        functools.partial(products_kernel, count, last),
+        out_shape=grad + (halves if last else (pltpu.HBM((2 * rows, feats), F32),)),
         grid_spec=pltpu.PrefetchScalarGridSpec(
             num_scalar_prefetch=1,
             grid=(feats // tile,),
-            in_specs=[block] * 2 + [whole] * 2 + [pl.BlockSpec((depth, tile), lambda j, s: (0, j))] * len(pieces),
-            out_specs=(whole, whole, block, block),
-            scratch_shapes=[pltpu.VMEM((size, 2 * rows, width), F32)],
+            in_specs=[block] * 2
+            + [whole] * 2
+            + [pl.BlockSpec((depth, tile), lambda j, s: (0, j))] * len(pieces)
+            + [double] * last,
+            out_specs=(part, part) + ((block, block) if last else (double,)),
+            scratch_shapes=[pltpu.VMEM((count, 2 * rows, width), F32)],
         ),
         compiler_params=pltpu.CompilerParams(vmem_limit_bytes=28 << 20),
         cost_estimate=pl.CostEstimate(
             flops=8 * rows * depth * len(pieces) * feats,
-            bytes_accessed=2 * depth * len(pieces) * feats + 10 * rows * feats,
+            bytes_accessed=2 * depth * len(pieces) * feats + 12 * rows * feats,
             transcendentals=0,
         ),
     )(
         scalars,
         *[
             pltpu.with_memory_space_constraint(a, pltpu.HBM)
-            for a in (cot_own, cot_away, gated_own, gated_away, *pieces)
+            for a in (cot_own, cot_away, gated_own, gated_away, *pieces, *([before] if last else []))
         ],
     )
 
 
-def merge_kernel(scalars, own, away, out):
-    size, _, width = own.shape
-    for r in range(size):
-        for ref, side in ((own, scalars[0]), (away, 1 - scalars[0])):
-            out[:, pl.ds(pl.multiple_of((2 * r + side) * width, width), width)] = ref[r]
-
-
-def merge(side, own, away):
-    size, rows, width = own.shape
+def merge_kernel(scalars, *refs):
+    out = refs[-1]
+    at = 1
+    for own, away in zip(refs[:-1:2], refs[1:-1:2]):
+        count, _, width = own.shape
+        for i in range(count):
+            for ref, side in ((own, scalars[0]), (away, 1 - scalars[0])):
+                out[:, pl.ds(pl.multiple_of((2 * scalars[at] + side) * width, width), width)] = ref[i]
+            at += 1
+
+
+def merge(scalars, pairs, chans):
+    rows = pairs[0].shape[1]
     vmem = pl.BlockSpec(memory_space=pltpu.VMEM)
     return pl.pallas_call(
         merge_kernel,
-        out_shape=jax.ShapeDtypeStruct((rows, 2 * size * width), own.dtype),
-        in_specs=[pl.BlockSpec(memory_space=pltpu.SMEM), vmem, vmem],
+        out_shape=jax.ShapeDtypeStruct((rows, chans), BF16),
+        in_specs=[pl.BlockSpec(memory_space=pltpu.SMEM)] + [vmem] * len(pairs),
         out_specs=vmem,
         compiler_params=pltpu.CompilerParams(vmem_limit_bytes=GRANT),
-        cost_estimate=pl.CostEstimate(flops=0, bytes_accessed=8 * own.size, transcendentals=0),
-    )(side.reshape(1), own, away)
+        cost_estimate=pl.CostEstimate(flops=0, bytes_accessed=4 * rows * chans, transcendentals=0),
+    )(scalars, *pairs)
 
 
 def on_ring(queries, keys, values, w_out, taps, seg_ids, cotangent):
@@ -272,7 +286,21 @@
     before = send(product, perm=later)
     filt = forward_dft(high_now, low_now, tie(taps.T), ((1,), (0,)))
 
-    pieces = [first, swapped[:half], second, swapped[half:]]
+    firsts, seconds = [(first, swapped[:half])], [(second, swapped[half:])]
+    block = [ring_place(lax.rem(at - s + size, size), size) for s in range(size)]
+    ready = [max(s, size - s) if s else 0 for s in range(size)]
+    early = [s for s in range(size) if ready[s] <= size - 3]
+    late = [s for s in range(size) if ready[s] > size - 3]
+
+    def products_of(sets, before):
+        groups = []
+        for s in sets:
+            m = (size - s) % size
+            groups.append((firsts[s][0], seconds[m][0], firsts[s][1], seconds[m][1]))
+        scalars = jnp.stack([core] + [block[s] for s in sets])
+        grad_own, grad_away, *sums = products(scalars, cotangent, cot_away, gated_own, gated_away, groups, before)
+        return grad_own, send(grad_away, perm=swap_pair), sums
+
     for step in range(1, size):
         first, second = send(first, perm=onward), send(second, perm=behind)
         swap = (first, second)
@@ -286,12 +314,16 @@
             gated_own, gated_away = deal(pair, gated, chans // (2 * size))
             *swap, gated_own, gated_away = tie((*swap, gated_own, gated_away))
             gated_away = send(gated_away, perm=swap_pair)
-        pieces += [first, send(swap[0], perm=swap_core), second, send(swap[1], perm=swap_core)]
-    places = [core] + [ring_place(lax.rem(at - s + size, size), size) for s in range(size)]
-    grad_own, grad_away, out_own, out_away = products(
-        jnp.stack(places), cotangent, cot_away, gated_own, gated_away, pieces
+        if step == size - 1:
+            grad_own, grad_away, sums = products_of(early, None)
+            *swap, grad_own, sums[0] = tie((*swap, grad_own, sums[0]))
+        firsts.append((first, send(swap[0], perm=swap_core)))
+        seconds.append((second, send(swap[1], perm=swap_core)))
+    grad_away, sums[0] = tie((grad_away, sums[0]))
+    late_own, late_away, (out_own, out_away) = products_of(late, sums[0])
+    grad_gated = merge(
+        jnp.stack([pair] + [block[s] for s in early + late]), (grad_own, grad_away, late_own, late_away), chans
     )
-    grad_gated = merge(pair, grad_own, send(grad_away, perm=swap_pair))
     out_away = send(out_away, perm=swap_pair)
     grad_queries = mul(grad_gated, filtered)
     grad_filtered = mul(grad_gated, queries)
@@ -300,7 +332,8 @@
     across = jnp.where(linked, back[:length], 0.0).astype(BF16)
     ahead = send(across, perm=earlier)
     taps_part = inverse_dft(table_now, times_conj(grads, data), scale)
-    taps_grad = sum_over_ring(taps_part, nseq, place).T
+    taps_grad, out_away = sum_over_ring(taps_part, nseq, place, out_away)
+    taps_grad = taps_grad.T
     outputs = (out_own + out_away.astype(F32)).astype(BF16)
     grad_product = (back[length:] + ahead.astype(F32)).astype(BF16)
     grad_keys = mul(grad_product, values)

time: 196 us -> 207 us (1.056)
  Pallas kernels: 16.1 us -> 25.4 us
  waiting for transfers between devices: 90.1 us -> 93.4 us
  starting transfers between devices: 38.4 us -> 35.4 us
    ppermute x1, waiting for transfers between devices: 0.01 us -> 16.4 us  [on_ring(): out_away = send(out_away, perm=swap_pair)]
    ppermute x4, waiting for transfers between devices: 18.7 us -> 8.28 us  [halve(): away = lax.ppermute(away, 'seq', [(i, i ^ bit) for i in range(nseq)])]
    pallas_call x2 -> x3, Pallas kernels: 14.7 us -> 25 us  [the longest x2 24.4 us: products(): pl.pallas_call(functools.partial(products_kernel, count, last), out_shape...]
    ppermute x1, waiting for transfers between devices: 5.47 us -> 0.01 us  [on_ring(): gated_away = send(gated_away, perm=swap_pair)]
    ppermute x14, starting transfers between devices: 20.5 us -> 18 us  [on_ring(): first, second = (send(first, perm=onward), send(second, perm=behind))]
    ppermute x15 -> x16, waiting for transfers between devices: 13.9 us -> 16.1 us  [the longest x2 14.7 us: products_of(): return (grad_own, send(grad_away, perm=swap_pair), sums)]
    ppermute x15 -> x16, starting transfers between devices: 5.35 us -> 3.18 us  [the longest x7 2.07 us: on_ring(): seconds.append((second, send(swap[1], perm=swap_core)))]
    unnamed x97 -> x85, local copies, waits for them, and re-layouts: 12.2 us -> 11.5 us
  transfers between devices with their start and end apart: 40 -> 41, of which waited for: 16 -> 13; matrix products, arithmetic and copies ran while one was open for 19% -> 19% of each run, Pallas kernels for 0% -> 6%
where the time goes in v1:
time: 207 us
  waiting for transfers between devices  93.4 us (45%)
  starting transfers between devices  35.4 us (17%)
  Pallas kernels  25.4 us (12%)
  matrix products  25 us (12%)
  local copies, waits for them, and re-layouts  17 us (8%)
  other arithmetic  7.77 us (4%)
  between operations  2.64 us (1%)
    ppermute x14, waiting for transfers between devices, on_ring(): first, second = (send(first, perm=onward), send(second, perm=behind))  52.6 us
    pallas_call x2, Pallas kernels, products(): pl.pallas_call(functools.partial(products_kernel, count, last), out_shape...  24.4 us
    ppermute x14, starting transfers between devices, on_ring(): first, second = (send(first, perm=onward), send(second, perm=behind))  18 us
    ppermute x1, waiting for transfers between devices, on_ring(): out_away = send(out_away, perm=swap_pair)  16.4 us
    dot_general x6, matrix products, inverse_dft(): lax.dot_general(table, spectrum, (((0,), (0,)), ((), ())), precision=lax....  14.9 us
    ppermute x2, waiting for transfers between devices, products_of(): return (grad_own, send(grad_away, perm=swap_pair), sums)  14.7 us
    unnamed x85, local copies, waits for them, and re-layouts  11.5 us
    ppermute x4, waiting for transfers between devices, halve(): away = lax.ppermute(away, 'seq', [(i, i ^ bit) for i in range(nseq)])  8.28 us
  transfers between devices with their start and end apart: 41, of which 13 were waited for; matrix products, arithmetic and copies ran while one was open for 19% of the time, Pallas kernels for 6%

profile of v1, /device:TPU:0, one launch (start us, length us, event | category | flops | bytes accessed | tf_op | source)
XLA Modules:
  0.0 206.5 jit_solution(418809910309379979)
XLA Ops:
  0.7 3.0 %collective-permute-start = (bf16[128,4096]{1,0:T(8,128)(2,1)}, bf16[128,4096]{1,0:T(8,128)(2,1)}, u32[]{:S(2)}, u32[]{:S(2)}) collective-permute-start(bf16[128,4096]{1,0:T(8,128)(2,1)} %cot_own.3), channel_id=1, source_target_pairs={{0,2},{1,3},{2,0},{3,1},{4,6},{5,7},{6,4},{7,5},{8,10},{9,11},{10,... | collective-permute-start | bytes 3145736 | tf_op jit(solution)/shard_map/ppermute | solution.py:284
  8.6 2.6 %copy.48 = bf16[128,4096]{0,1:T(8,128)(2,1)} copy(bf16[128,4096]{1,0:T(8,128)(2,1)} %param.15) | data formatting | bytes 2097152 | tf_op args[2]
  12.8 7.7 %collective-permute-done.1.refs_0_ = bf16[64,4096]{1,0:T(8,128)(2,1)} collective-permute-done((bf16[64,4096]{1,0:T(8,128)(2,1)}, bf16[64,4096]{1,0:T(8,128)(2,1)}, u32[]{:S(2)}, u32[]{:S(2)}) %collective-permute-start.1) | collective-permute-done | bytes 524320 | tf_op jit(solution)/shard_map/ppermute | solution.py:305
  22.6 2.7 %fusion.77 = f32[256,4096]{1,0:T(8,128)} fusion(bf16[256,128]{1,0:T(8,128)(2,1)S(1)} %copy-done.18, bf16[128,4096]{0,1:T(8,128)(2,1)S(1)} %bitcast.61), kind=kOutput, calls=%fused_computation.100 | convolution fusion | flops 268435456 | bytes 5308416 | tf_op jit(solution)/shard_map/dot_general | solution.py:25
  28.6 2.9 %convolution_add_fusion.4 = f32[256,4096]{1,0:T(8,128)S(1)} fusion(f32[256,4096]{1,0:T(8,128)} %fusion.77, bf16[256,128]{1,0:T(8,128)(2,1)S(1)} %copy-done.17, bf16[128,4096]{0,1:T(8,128)(2,1)S(1)} %bitcast.60), kind=kOutput, calls=%fused_computation.9 | convolution fusion | flops 269484032 | bytes 9502720 | tf_op jit(solution)/shard_map/dot_general | solution.py:26
  31.6 2.8 %collective-permute-done.2.refs_4_ = bf16[64,4096]{1,0:T(8,128)(2,1)S(1)} collective-permute-done((bf16[64,4096]{1,0:T(8,128)(2,1)}, bf16[64,4096]{1,0:T(8,128)(2,1)S(1)}, u32[]{:S(2)}, u32[]{:S(2)}) %collective-permute-start.2) | collective-permute-done | bytes 524320 | tf_op jit(solution)/shard_map/ppermute | solution.py:305
  35.9 10.3 %collective-permute-done.5.refs_9_ = bf16[64,4096]{1,0:T(8,128)(2,1)S(1)} collective-permute-done((bf16[64,4096]{1,0:T(8,128)(2,1)}, bf16[64,4096]{1,0:T(8,128)(2,1)S(1)}, u32[]{:S(2)}, u32[]{:S(2)}) %collective-permute-start.5) | collective-permute-done | bytes 524320 | tf_op jit(solution)/shard_map/ppermute | solution.py:305
  46.2 2.4 %collective-permute-start.6 = (bf16[64,4096]{1,0:T(8,128)(2,1)S(1)}, bf16[64,4096]{1,0:T(8,128)(2,1)}, u32[]{:S(2)}, u32[]{:S(2)}) collective-permute-start(bf16[64,4096]{1,0:T(8,128)(2,1)S(1)} %collective-permute-done.5.refs_9_), channel_id=1, source_target_pairs={{8,0},{9,1},{10,2},{11,3},{16,8},{17,9},{18,10},{19,11},{24,16},{2... | collective-permute-start | bytes 1572872 | tf_op jit(solution)/shard_map/ppermute | solution.py:305
  50.0 7.8 %collective-permute-done.6.refs_13_ = bf16[64,4096]{1,0:T(8,128)(2,1)} collective-permute-done((bf16[64,4096]{1,0:T(8,128)(2,1)S(1)}, bf16[64,4096]{1,0:T(8,128)(2,1)}, u32[]{:S(2)}, u32[]{:S(2)}) %collective-permute-start.6) | collective-permute-done | bytes 524320 | tf_op jit(solution)/shard_map/ppermute | solution.py:305
  57.9 2.6 %collective-permute-start.9 = (bf16[64,4096]{1,0:T(8,128)(2,1)}, bf16[64,4096]{1,0:T(8,128)(2,1)S(1)}, u32[]{:S(2)}, u32[]{:S(2)}) collective-permute-start(bf16[64,4096]{1,0:T(8,128)(2,1)} %collective-permute-done.6.refs_13_), channel_id=1, source_target_pairs={{8,0},{9,1},{10,2},{11,3},{16,8},{17,9},{18,10},{19,11},{24,16},{2... | collective-permute-start | bytes 1572872 | tf_op jit(solution)/shard_map/ppermute | solution.py:305
  64.1 2.8 %fusion.12 = (bf16[128,4096]{1,0:T(8,128)(2,1)S(1)}, f32[128,4096]{1,0:T(8,128)}) fusion(bf16[128,4096]{1,0:T(8,128)(2,1)S(1)} %copy-done.9, f32[4096,128]{0,1:T(8,128)S(1)} %fusion.36, f32[128,128]{1,0:T(8,128)S(1)} %copy-done.19, f32[256,4096]{1,0:T(8,128)S(1)} %fusion.4, f32[256,4096]{1,0:T(8,128)S(1)} %convolution_add_fusion.4), kind=kOutput, calls=%fused_computation.25 | convolution fusion | flops 407896064 | bytes 14745600 | tf_op jit(solution)/shard_map/dot_general | solution.py:43
  70.6 11.7 %collective-permute-done.10.refs_5_ = bf16[64,4096]{1,0:T(8,128)(2,1)} collective-permute-done((bf16[64,4096]{1,0:T(8,128)(2,1)S(1)}, bf16[64,4096]{1,0:T(8,128)(2,1)}, u32[]{:S(2)}, u32[]{:S(2)}) %collective-permute-start.10) | collective-permute-done | bytes 524320 | tf_op jit(solution)/shard_map/ppermute | solution.py:305
  86.2 11.6 %collective-permute-done.11.refs_5_ = bf16[64,4096]{1,0:T(8,128)(2,1)} collective-permute-done((bf16[64,4096]{1,0:T(8,128)(2,1)}, bf16[64,4096]{1,0:T(8,128)(2,1)}, u32[]{:S(2)}, u32[]{:S(2)}) %collective-permute-start.11) | collective-permute-done | bytes 524320 | tf_op jit(solution)/shard_map/ppermute | solution.py:305
  102.9 11.9 %shard_map.165 = (bf16[4,128,256]{2,1,0:T(8,128)(2,1)S(1)}, bf16[4,128,256]{2,1,0:T(8,128)(2,1)}, f32[256,4096]{1,0:T(8,128)}) custom-call(s32[5]{0:T(128)S(1)} %stack.56.scalars, bf16[128,4096]{1,0:T(8,128)(2,1)} %cot_own.3, bf16[128,4096]{1,0:T(8,128)(2,1)} %collective-permute-done.cot_away, bf16[8,128,256]{2,1,0:T(8,128)(2,1)} %copy-done.2, ...), custom_call_target="tpu_custom_call" | custom-call | flops 4294967296 | bytes 14680064 | tf_op jit(solution)/shard_map/pallas_call | solution.py:207
  116.7 6.6 %collective-permute-done.32.refs_1_ = bf16[4,128,256]{2,1,0:T(8,128)(2,1)S(1)} collective-permute-done((bf16[4,128,256]{2,1,0:T(8,128)(2,1)}, bf16[4,128,256]{2,1,0:T(8,128)(2,1)S(1)}, u32[]{:S(2)}, u32[]{:S(2)}) %collective-permute-start.32) | collective-permute-done | bytes 262176 | tf_op jit(solution)/shard_map/ppermute | solution.py:302
  125.6 12.5 %shard_map.166 = (bf16[4,128,256]{2,1,0:T(8,128)(2,1)S(1)}, bf16[4,128,256]{2,1,0:T(8,128)(2,1)}, f32[128,4096]{1,0:T(8,128)}, bf16[128,4096]{1,0:T(8,128)(2,1)}) custom-call(s32[5]{0:T(128)S(1)} %stack.51.scalars, bf16[128,4096]{1,0:T(8,128)(2,1)} %cot_own.3, bf16[128,4096]{1,0:T(8,128)(2,1)} %collective-permute-done.cot_away, ...), custom_call_target="tpu_custom_call" | custom-call | flops 4294967296 | bytes 14680064 | tf_op jit(solution)/shard_map/pallas_call | solution.py:207
  138.5 8.2 %collective-permute-done.33.refs_3_ = bf16[4,128,256]{2,1,0:T(8,128)(2,1)S(1)} collective-permute-done((bf16[4,128,256]{2,1,0:T(8,128)(2,1)}, bf16[4,128,256]{2,1,0:T(8,128)(2,1)S(1)}, u32[]{:S(2)}, u32[]{:S(2)}) %collective-permute-start.33) | collective-permute-done | bytes 262176 | tf_op jit(solution)/shard_map/ppermute | solution.py:302
  154.6 6.0 %fusion.22 = f32[4096,256]{1,0:T(8,128)S(1)} fusion(f32[128,256]{1,0:T(8,128)S(1)} %copy-done.22, f32[256,4096]{1,0:T(8,128)} %copy-done.7, f32[256,4096]{1,0:T(8,128)} %copy-done.3), kind=kOutput, calls=%fused_computation.37 | convolution fusion | flops 806879232 | bytes 12713984 | tf_op jit(solution)/shard_map/dot_general | solution.py:43
  160.6 2.3 %fusion.1 = f32[256,4096]{0,1:T(8,128)S(1)} fusion(f32[4096,256]{1,0:T(8,128)S(1)} %fusion.22, f32[128,256]{1,0:T(8,128)S(1)} %copy-done.21, f32[256,4096]{1,0:T(8,128)S(1)} %copy-done.8, f32[256,4096]{1,0:T(8,128)S(1)} %copy-done.4), kind=kOutput, calls=%fused_computation.2 | convolution fusion | flops 808976384 | bytes 16908288 | tf_op jit(solution)/shard_map/dot_general | solution.py:43
  166.3 6.2 %collective-permute-done.35 = bf16[8,128,128]{2,1,0:T(8,128)(2,1)S(1)} collective-permute-done((bf16[8,128,128]{2,1,0:T(8,128)(2,1)S(1)}, bf16[8,128,128]{2,1,0:T(8,128)(2,1)S(1)}, u32[]{:S(2)}, u32[]{:S(2)}) %collective-permute-start.35) | collective-permute-done | bytes 262176 | tf_op jit(solution)/shard_map/ppermute | solution.py:110
  172.6 16.4 %collective-permute-done.36 = bf16[128,4096]{1,0:T(8,128)(2,1)S(1)} collective-permute-done((bf16[128,4096]{1,0:T(8,128)(2,1)}, bf16[128,4096]{1,0:T(8,128)(2,1)S(1)}, u32[]{:S(2)}, u32[]{:S(2)}) %collective-permute-start.36) | collective-permute-done | bytes 1048608 | tf_op jit(solution)/shard_map/ppermute | solution.py:327
  194.2 3.0 %collective-permute-start.39 = (bf16[2,128,128]{2,1,0:T(8,128)(2,1)S(1)}, bf16[2,128,128]{2,1,0:T(8,128)(2,1)S(1)}, u32[]{:S(2)}, u32[]{:S(2)}) collective-permute-start(bf16[2,128,128]{2,1,0:T(8,128)(2,1)S(1)} %fusion.71), channel_id=1, source_target_pairs={{0,16},{1,17},{2,18},{3,19},{4,20},{5,21},{6,22},{7,23},{8,24},{9,... | collective-permute-start | bytes 196616 | tf_op jit(solution)/shard_map/ppermute | solution.py:110
  200.5 2.4 %collective-permute-start.40 = (bf16[1,128,128]{2,1,0:T(8,128)(2,1)S(1)}, bf16[1,128,128]{2,1,0:T(8,128)(2,1)S(1)}, u32[]{:S(2)}, u32[]{:S(2)}) collective-permute-start(bf16[1,128,128]{2,1,0:T(8,128)(2,1)S(1)} %dynamic-slice_convert_fusion.3), channel_id=1, source_target_pairs={{0,2},{1,3},{2,0},{3,1},{4,6},{5,7},{6,4},{7,5},{8,10},{9,11},{10,... | collective-permute-start | bytes 98312 | tf_op jit(solution)/shard_map/ppermute | solution.py:110
  202.9 2.9 %add_convert_fusion = bf16[128,4096]{1,0:T(8,128)(2,1)} fusion(f32[128,4096]{1,0:T(8,128)} %get-tuple-element.51, bf16[128,4096]{1,0:T(8,128)(2,1)S(1)} %copy-done.16), kind=kLoop, calls=%fused_computation.41 | loop fusion | flops 1572864 | bytes 4194304 | tf_op jit(solution)/shard_map/convert_element_type | solution.py:337
  (182 shorter events, 54.7 us)
Async XLA Ops:
  0.7 26.6 %collective-permute-start = (bf16[128,4096]{1,0:T(8,128)(2,1)}, bf16[128,4096]{1,0:T(8,128)(2,1)}, u32[]{:S(2)}, u32[]{:S(2)}) collective-permute-start(bf16[128,4096]{1,0:T(8,128)(2,1)} %cot_own.3), channel_id=1, source_target_pairs={{0,2},{1,3},{2,0},{3,1},{4,6},{5,7},{6,4},{7,5},{8,10},{9,11},{10,... | collective-permute-start | bytes 3145736 | tf_op jit(solution)/shard_map/ppermute | solution.py:284
  3.7 66.4 %collective-permute-start.18 = (bf16[128,4096]{1,0:T(8,128)(2,1)}, bf16[128,4096]{1,0:T(8,128)(2,1)}, u32[]{:S(2)}, u32[]{:S(2)}) collective-permute-start(bf16[128,4096]{1,0:T(8,128)(2,1)} %param.16), channel_id=1, source_target_pairs={{0,1},{1,0},{2,3},{3,2},{4,5},{5,4},{6,7},{7,6},{8,9},{9,8},{10,11... | collective-permute-start | bytes 3145736 | tf_op jit(solution)/shard_map/ppermute | solution.py:283
  5.9 14.7 %collective-permute-start.1 = (bf16[64,4096]{1,0:T(8,128)(2,1)}, bf16[64,4096]{1,0:T(8,128)(2,1)}, u32[]{:S(2)}, u32[]{:S(2)}) collective-permute-start(bf16[64,4096]{1,0:T(8,128)(2,1)} %get-tuple-element.81.refs_0_), channel_id=1, source_target_pairs={{0,8},{1,9},{2,10},{3,11},{8,16},{9,17},{10,18},{11,19},{16,24},{1... | collective-permute-start | bytes 1572872 | tf_op jit(solution)/shard_map/ppermute | solution.py:305
  7.5 14.7 %collective-permute-start.4 = (bf16[64,4096]{1,0:T(8,128)(2,1)}, bf16[64,4096]{1,0:T(8,128)(2,1)}, u32[]{:S(2)}, u32[]{:S(2)}) collective-permute-start(bf16[64,4096]{1,0:T(8,128)(2,1)} %get-tuple-element.80.refs_1_), channel_id=1, source_target_pairs={{8,0},{9,1},{10,2},{11,3},{16,8},{17,9},{18,10},{19,11},{24,16},{2... | collective-permute-start | bytes 1572872 | tf_op jit(solution)/shard_map/ppermute | solution.py:305
  22.2 24.1 %collective-permute-start.5 = (bf16[64,4096]{1,0:T(8,128)(2,1)}, bf16[64,4096]{1,0:T(8,128)(2,1)S(1)}, u32[]{:S(2)}, u32[]{:S(2)}) collective-permute-start(bf16[64,4096]{1,0:T(8,128)(2,1)} %collective-permute-done.4.refs_13_), channel_id=1, source_target_pairs={{8,0},{9,1},{10,2},{11,3},{16,8},{17,9},{18,10},{19,11},{24,16},{2... | collective-permute-start | bytes 1572872 | tf_op jit(solution)/shard_map/ppermute | solution.py:305
  27.3 33.2 %collective-permute-start.7 = (bf16[128,4096]{0,1:T(8,128)(2,1)S(1)}, bf16[128,4096]{0,1:T(8,128)(2,1)S(1)}, u32[]{:S(2)}, u32[]{:S(2)}) collective-permute-start(bf16[128,4096]{0,1:T(8,128)(2,1)S(1)} %fusion.11), channel_id=1, source_target_pairs={{0,1},{1,2},{2,3},{3,4},{4,5},{5,6},{6,7},{7,8},{8,9},{9,10},{10,1... | collective-permute-start | bytes 3145736 | tf_op jit(solution)/shard_map/ppermute | solution.py:286
  34.4 26.1 %collective-permute-start.3 = (bf16[64,4096]{1,0:T(8,128)(2,1)S(1)}, bf16[64,4096]{1,0:T(8,128)(2,1)S(1)}, u32[]{:S(2)}, u32[]{:S(2)}) collective-permute-start(bf16[64,4096]{1,0:T(8,128)(2,1)S(1)} %collective-permute-done.2.refs_4_), channel_id=1, source_target_pairs={{0,8},{1,9},{2,10},{3,11},{8,16},{9,17},{10,18},{11,19},{16,24},{1... | collective-permute-start | bytes 1572872 | tf_op jit(solution)/shard_map/ppermute | solution.py:305
  67.8 14.4 %collective-permute-start.10 = (bf16[64,4096]{1,0:T(8,128)(2,1)S(1)}, bf16[64,4096]{1,0:T(8,128)(2,1)}, u32[]{:S(2)}, u32[]{:S(2)}) collective-permute-start(bf16[64,4096]{1,0:T(8,128)(2,1)S(1)} %collective-permute-done.9.refs_9_), channel_id=1, source_target_pairs={{8,0},{9,1},{10,2},{11,3},{16,8},{17,9},{18,10},{19,11},{24,16},{2... | collective-permute-start | bytes 1572872 | tf_op jit(solution)/shard_map/ppermute | solution.py:305
  69.9 14.5 %collective-permute-start.24 = (bf16[64,4096]{1,0:T(8,128)(2,1)}, bf16[64,4096]{1,0:T(8,128)(2,1)}, u32[]{:S(2)}, u32[]{:S(2)}) collective-permute-start(bf16[64,4096]{1,0:T(8,128)(2,1)} %collective-permute-done.6.refs_13_), channel_id=1, source_target_pairs={{0,1},{1,0},{2,3},{3,2},{4,5},{5,4},{6,7},{7,6},{8,9},{9,8},{10,11... | collective-permute-start | bytes 1572872 | tf_op jit(solution)/shard_map/ppermute | solution.py:321
  70.1 14.3 %collective-permute-start.8 = (bf16[8,128,256]{2,1,0:T(8,128)(2,1)S(1)}, bf16[8,128,256]{2,1,0:T(8,128)(2,1)S(1)}, u32[]{:S(2)}, u32[]{:S(2)}) collective-permute-start(bf16[8,128,256]{2,1,0:T(8,128)(2,1)S(1)} %get-tuple-element.39), channel_id=1, source_target_pairs={{0,2},{1,3},{2,0},{3,1},{4,6},{5,7},{6,4},{7,5},{8,10},{9,11},{10,... | collective-permute-start | bytes 1572872 | tf_op jit(solution)/shard_map/ppermute | solution.py:316
  70.3 14.6 %collective-permute-start.15 = (bf16[64,4096]{1,0:T(8,128)(2,1)}, bf16[64,4096]{1,0:T(8,128)(2,1)}, u32[]{:S(2)}, u32[]{:S(2)}) collective-permute-start(bf16[64,4096]{1,0:T(8,128)(2,1)} %collective-permute-done.14.refs_8_), channel_id=1, source_target_pairs={{0,8},{1,9},{2,10},{3,11},{8,16},{9,17},{10,18},{11,19},{16,24},{1... | collective-permute-start | bytes 1572872 | tf_op jit(solution)/shard_map/ppermute | solution.py:305
  70.3 14.7 %collective-permute-start.21 = (bf16[64,4096]{1,0:T(8,128)(2,1)}, bf16[64,4096]{1,0:T(8,128)(2,1)}, u32[]{:S(2)}, u32[]{:S(2)}) collective-permute-start(bf16[64,4096]{1,0:T(8,128)(2,1)} %collective-permute-done.14.refs_8_), channel_id=1, source_target_pairs={{0,1},{1,0},{2,3},{3,2},{4,5},{5,4},{6,7},{7,6},{8,9},{9,8},{10,11... | collective-permute-start | bytes 1572872 | tf_op jit(solution)/shard_map/ppermute | solution.py:320
  82.3 15.4 %collective-permute-start.11 = (bf16[64,4096]{1,0:T(8,128)(2,1)}, bf16[64,4096]{1,0:T(8,128)(2,1)}, u32[]{:S(2)}, u32[]{:S(2)}) collective-permute-start(bf16[64,4096]{1,0:T(8,128)(2,1)} %collective-permute-done.10.refs_5_), channel_id=1, source_target_pairs={{8,0},{9,1},{10,2},{11,3},{16,8},{17,9},{18,10},{19,11},{24,16},{2... | collective-permute-start | bytes 1572872 | tf_op jit(solution)/shard_map/ppermute | solution.py:305
  84.4 16.0 %collective-permute-start.22 = (bf16[64,4096]{1,0:T(8,128)(2,1)}, bf16[64,4096]{1,0:T(8,128)(2,1)S(1)}, u32[]{:S(2)}, u32[]{:S(2)}) collective-permute-start(bf16[64,4096]{1,0:T(8,128)(2,1)} %copy-done.31), channel_id=1, source_target_pairs={{0,1},{1,0},{2,3},{3,2},{4,5},{5,4},{6,7},{7,6},{8,9},{9,8},{10,11... | collective-permute-start | bytes 1572872 | tf_op jit(solution)/shard_map/ppermute | solution.py:321
  84.4 16.0 %collective-permute-start.20 = (bf16[64,4096]{1,0:T(8,128)(2,1)}, bf16[64,4096]{1,0:T(8,128)(2,1)S(1)}, u32[]{:S(2)}, u32[]{:S(2)}) collective-permute-start(bf16[64,4096]{1,0:T(8,128)(2,1)} %collective-permute-done.10.refs_5_), channel_id=1, source_target_pairs={{0,1},{1,0},{2,3},{3,2},{4,5},{5,4},{6,7},{7,6},{8,9},{9,8},{10,11... | collective-permute-start | bytes 1572872 | tf_op jit(solution)/shard_map/ppermute | solution.py:321
  84.9 16.0 %collective-permute-start.23 = (bf16[64,4096]{1,0:T(8,128)(2,1)}, bf16[64,4096]{1,0:T(8,128)(2,1)S(1)}, u32[]{:S(2)}, u32[]{:S(2)}) collective-permute-start(bf16[64,4096]{1,0:T(8,128)(2,1)} %collective-permute-done.15.refs_12_), channel_id=1, source_target_pairs={{0,1},{1,0},{2,3},{3,2},{4,5},{5,4},{6,7},{7,6},{8,9},{9,8},{10,11... | collective-permute-start | bytes 1572872 | tf_op jit(solution)/shard_map/ppermute | solution.py:320
  85.0 16.1 %collective-permute-start.16 = (bf16[64,4096]{1,0:T(8,128)(2,1)}, bf16[64,4096]{1,0:T(8,128)(2,1)}, u32[]{:S(2)}, u32[]{:S(2)}) collective-permute-start(bf16[64,4096]{1,0:T(8,128)(2,1)} %collective-permute-done.15.refs_12_), channel_id=1, source_target_pairs={{0,8},{1,9},{2,10},{3,11},{8,16},{9,17},{10,18},{11,19},{16,24},{1... | collective-permute-start | bytes 1572872 | tf_op jit(solution)/shard_map/ppermute | solution.py:305
  97.7 17.1 %collective-permute-start.12 = (bf16[64,4096]{1,0:T(8,128)(2,1)}, bf16[64,4096]{1,0:T(8,128)(2,1)}, u32[]{:S(2)}, u32[]{:S(2)}) collective-permute-start(bf16[64,4096]{1,0:T(8,128)(2,1)} %collective-permute-done.11.refs_5_), channel_id=1, source_target_pairs={{8,0},{9,1},{10,2},{11,3},{16,8},{17,9},{18,10},{19,11},{24,16},{2... | collective-permute-start | bytes 1572872 | tf_op jit(solution)/shard_map/ppermute | solution.py:305
  100.4 15.3 %collective-permute-start.13 = (bf16[64,4096]{1,0:T(8,128)(2,1)}, bf16[64,4096]{1,0:T(8,128)(2,1)S(1)}, u32[]{:S(2)}, u32[]{:S(2)}) collective-permute-start(bf16[64,4096]{1,0:T(8,128)(2,1)} %collective-permute-done.1.refs_0_), channel_id=1, source_target_pairs={{0,1},{1,0},{2,3},{3,2},{4,5},{5,4},{6,7},{7,6},{8,9},{9,8},{10,11... | collective-permute-start | bytes 1572872 | tf_op jit(solution)/shard_map/ppermute | solution.py:320
  100.4 15.7 %collective-permute-start.31 = (bf16[64,4096]{1,0:T(8,128)(2,1)}, bf16[64,4096]{1,0:T(8,128)(2,1)S(1)}, u32[]{:S(2)}, u32[]{:S(2)}) collective-permute-start(bf16[64,4096]{1,0:T(8,128)(2,1)} %collective-permute-done.4.refs_13_), channel_id=1, source_target_pairs={{0,1},{1,0},{2,3},{3,2},{4,5},{5,4},{6,7},{7,6},{8,9},{9,8},{10,11... | collective-permute-start | bytes 1572872 | tf_op jit(solution)/shard_map/ppermute | solution.py:321
  100.9 15.3 %collective-permute-start.26 = (bf16[64,4096]{1,0:T(8,128)(2,1)S(1)}, bf16[64,4096]{1,0:T(8,128)(2,1)S(1)}, u32[]{:S(2)}, u32[]{:S(2)}) collective-permute-start(bf16[64,4096]{1,0:T(8,128)(2,1)S(1)} %collective-permute-done.2.refs_4_), channel_id=1, source_target_pairs={{0,1},{1,0},{2,3},{3,2},{4,5},{5,4},{6,7},{7,6},{8,9},{9,8},{10,11... | collective-permute-start | bytes 1572872 | tf_op jit(solution)/shard_map/ppermute | solution.py:320
  101.1 14.6 %collective-permute-start.17 = (bf16[64,4096]{1,0:T(8,128)(2,1)}, bf16[64,4096]{1,0:T(8,128)(2,1)}, u32[]{:S(2)}, u32[]{:S(2)}) collective-permute-start(bf16[64,4096]{1,0:T(8,128)(2,1)} %collective-permute-done.16.refs_8_), channel_id=1, source_target_pairs={{0,8},{1,9},{2,10},{3,11},{8,16},{9,17},{10,18},{11,19},{16,24},{1... | collective-permute-start | bytes 1572872 | tf_op jit(solution)/shard_map/ppermute | solution.py:305
  154.1 34.9 %collective-permute-start.36 = (bf16[128,4096]{1,0:T(8,128)(2,1)}, bf16[128,4096]{1,0:T(8,128)(2,1)S(1)}, u32[]{:S(2)}, u32[]{:S(2)}) collective-permute-start(bf16[128,4096]{1,0:T(8,128)(2,1)} %get-tuple-element.58), channel_id=1, source_target_pairs={{0,2},{1,3},{2,0},{3,1},{4,6},{5,7},{6,4},{7,5},{8,10},{9,11},{10,... | collective-permute-start | bytes 3145736 | tf_op jit(solution)/shard_map/ppermute | solution.py:327
  165.0 32.2 %collective-permute-start.37 = (bf16[128,4096]{0,1:T(8,128)(2,1)S(1)}, bf16[128,4096]{0,1:T(8,128)(2,1)S(1)}, u32[]{:S(2)}, u32[]{:S(2)}) collective-permute-start(bf16[128,4096]{0,1:T(8,128)(2,1)S(1)} %fusion.17), channel_id=1, source_target_pairs={{1,0},{2,1},{3,2},{4,3},{5,4},{6,5},{7,6},{8,7},{9,8},{10,9},{11,1... | collective-permute-start | bytes 3145736 | tf_op jit(solution)/shard_map/ppermute | solution.py:333
  (57 other events, 481.6 us)

commit v2 on v0

--- a/solution.py
+++ b/solution.py
@@ -11,6 +11,7 @@
 F32 = jnp.float32
 BF16 = jnp.bfloat16
 GRANT = 16 << 20
+CHUNKS = 4
 
 
 def spectrum_table(length):
@@ -100,7 +101,7 @@
     )(side.reshape(1), data)
 
 
-def sum_over_ring(part, nseq, place):
+def sum_over_ring(part, nseq, place, guests):
     core, pair, row = place & 1, (place >> 1) & 1, place >> 2
     lags, chans = part.shape
     size, chans = nseq // 4, chans // nseq
@@ -113,14 +114,17 @@
     kept, away = deal(core.astype(jnp.int32), part, chans, 2)
     part = kept + lax.ppermute(away, "seq", [(i, i ^ 1) for i in range(nseq)])
     part = part.reshape(2, size, lags, chans)
-    left = size
+    left, done = size, 0
     while left > 1:
         bit = size // left
         mine = (row // bit) & 1
+        if done < len(guests) - 1:
+            part, guests[done] = lax.optimization_barrier((part, guests[done]))
+            done += 1
         part = part.reshape(2 * left // 2, 2, lags, chans)
         part = halve(part, 4 * bit, mine, BF16).reshape(2, left // 2, lags, chans)
         left //= 2
-    return halve(part.reshape(1, 2, lags, chans), 2, pair, BF16).reshape(lags, chans)
+    return halve(part.reshape(1, 2, lags, chans), 2, pair, BF16).reshape(lags, chans), guests
 
 
 def links(seg_ids, place):
@@ -148,9 +152,19 @@
     return jnp.where(row & 1 == 0, row >> 1, size - 1 - (row >> 1))
 
 
-def products_kernel(size, scalars, cot_own, cot_away, gated_own, gated_away, *refs):
-    pieces, (grad_own, grad_away, out_own, out_away, grad) = refs[: 4 * size], refs[4 * size :]
+def stacked(pieces, size, order):
+    rows = []
+    for s in range(size):
+        m = (size - s) % size
+        block = (pieces[4 * s], pieces[4 * m + 2], pieces[4 * s + 1], pieces[4 * m + 3])
+        rows += [block[k][...] for k in order]
+    return jnp.concatenate(rows, 0)
+
+
+def grad_kernel(size, scalars, cot_own, cot_away, *refs):
+    pieces, (grad_own, grad_away, grad) = refs[: 4 * size], refs[4 * size :]
     rows = cot_own.shape[0]
+    width = grad_own.shape[2]
 
     @pl.when(pl.program_id(0) == 0)
     def _():
@@ -158,17 +172,45 @@
 
     def add(order):
         cot = jnp.concatenate([cot_own[...], cot_away[...]], 0)
-        total = None
+        dims = (((1,), (1,)), ((), ()))
+        grad[...] += lax.dot_general(cot, stacked(pieces, size, order), dims, preferred_element_type=F32)
+
+    @pl.when(scalars[0] == 0)
+    def _():
+        add((0, 1, 2, 3))
+
+    @pl.when(scalars[0] != 0)
+    def _():
+        add((2, 3, 0, 1))
+
+    @pl.when(pl.program_id(0) == pl.num_programs(0) - 1)
+    def _():
         for s in range(size):
-            m = (size - s) % size
-            block = (pieces[4 * s], pieces[4 * m + 2], pieces[4 * s + 1], pieces[4 * m + 3])
-            block = jnp.concatenate([block[k][...] for k in order], 0)
-            grad[s] += lax.dot_general(cot, block, (((1,), (1,)), ((), ())), preferred_element_type=F32)
-            left = jnp.concatenate([gated_own[scalars[1 + s]], gated_away[scalars[1 + s]]], 0)
-            part = jnp.dot(left, block, preferred_element_type=F32)
-            total = part if total is None else total + part
+            block = grad[:, s * width : (s + 1) * width].astype(BF16)
+            grad_own[scalars[1 + s]] = block[:rows]
+            grad_away[scalars[1 + s]] = block[rows:]
+
+
+def output_kernel(size, scalars, gated_own, gated_away, *refs):
+    pieces, (out_own, *out_away, left) = refs[: 4 * size], refs[4 * size :]
+    rows = out_own.shape[0]
+    width = gated_own.shape[2]
+    run = pl.num_programs(0) // len(out_away)
+
+    @pl.when(pl.program_id(0) == 0)
+    def _():
+        for s in range(size):
+            left[:rows, s * width : (s + 1) * width] = gated_own[scalars[1 + s]]
+            left[rows:, s * width : (s + 1) * width] = gated_away[scalars[1 + s]]
+
+    def add(order):
+        total = jnp.dot(left[...], stacked(pieces, size, order), preferred_element_type=F32)
         out_own[...] = total[:rows]
-        out_away[...] = total[rows:].astype(BF16)
+        for k, ref in enumerate(out_away):
+
+            @pl.when(pl.program_id(0) // run == k)
+            def _(ref=ref):
+                ref[...] = total[rows:].astype(BF16)
 
     @pl.when(scalars[0] == 0)
     def _():
@@ -178,48 +220,65 @@
     def _():
         add((2, 3, 0, 1))
 
-    @pl.when(pl.program_id(0) == pl.num_programs(0) - 1)
-    def _():
-        for s in range(size):
-            grad_own[scalars[1 + s]] = grad[s, :rows].astype(BF16)
-            grad_away[scalars[1 + s]] = grad[s, rows:].astype(BF16)
-
-
-def products(scalars, cot_own, cot_away, gated_own, gated_away, pieces):
+
+def far(arrays):
+    return [pltpu.with_memory_space_constraint(a, pltpu.HBM) for a in arrays]
+
+
+def grad_of_gated(scalars, cot_own, cot_away, pieces):
     rows, feats = cot_own.shape
-    size, _, width = gated_own.shape
-    depth = pieces[0].shape[0]
+    size, depth = len(pieces) // 4, pieces[0].shape[0]
     tile = min(512, feats)
-    block = pl.BlockSpec((rows, tile), lambda j, s: (0, j))
-    whole = pl.BlockSpec(gated_own.shape, lambda j, s: (0, 0, 0))
+    out = (size, rows, 4 * depth)
+    whole = pl.BlockSpec(out, lambda j, s: (0, 0, 0))
     return pl.pallas_call(
-        functools.partial(products_kernel, size),
-        out_shape=(
-            jax.ShapeDtypeStruct(gated_own.shape, BF16),
-            jax.ShapeDtypeStruct(gated_own.shape, BF16),
-            jax.ShapeDtypeStruct((rows, feats), F32),
-            jax.ShapeDtypeStruct((rows, feats), BF16),
-        ),
+        functools.partial(grad_kernel, size),
+        out_shape=(jax.ShapeDtypeStruct(out, BF16), pltpu.HBM(out, BF16)),
         grid_spec=pltpu.PrefetchScalarGridSpec(
             num_scalar_prefetch=1,
             grid=(feats // tile,),
-            in_specs=[block] * 2 + [whole] * 2 + [pl.BlockSpec((depth, tile), lambda j, s: (0, j))] * len(pieces),
-            out_specs=(whole, whole, block, block),
-            scratch_shapes=[pltpu.VMEM((size, 2 * rows, width), F32)],
+            in_specs=[pl.BlockSpec((rows, tile), lambda j, s: (0, j))] * 2
+            + [pl.BlockSpec((depth, tile), lambda j, s: (0, j))] * len(pieces),
+            out_specs=(whole, whole),
+            scratch_shapes=[pltpu.VMEM((2 * rows, 4 * depth * size), F32)],
         ),
         compiler_params=pltpu.CompilerParams(vmem_limit_bytes=28 << 20),
         cost_estimate=pl.CostEstimate(
-            flops=8 * rows * depth * len(pieces) * feats,
-            bytes_accessed=2 * depth * len(pieces) * feats + 10 * rows * feats,
+            flops=4 * rows * depth * len(pieces) * feats,
+            bytes_accessed=2 * depth * len(pieces) * feats + 4 * rows * feats,
             transcendentals=0,
         ),
-    )(
-        scalars,
-        *[
-            pltpu.with_memory_space_constraint(a, pltpu.HBM)
-            for a in (cot_own, cot_away, gated_own, gated_away, *pieces)
-        ],
-    )
+    )(scalars, *far([cot_own, cot_away, *pieces]))
+
+
+def output_of(scalars, gated_own, gated_away, pieces):
+    size, rows, width = gated_own.shape
+    depth, feats = pieces[0].shape
+    tile = min(512, feats // CHUNKS)
+    run = feats // CHUNKS // tile
+    block = pl.BlockSpec((rows, tile), lambda j, s: (0, j))
+
+    def chunk(k):
+        return pl.BlockSpec((rows, tile), lambda j, s: (0, jnp.clip(j - k * run, 0, run - 1)))
+
+    return pl.pallas_call(
+        functools.partial(output_kernel, size),
+        out_shape=(pltpu.HBM((rows, feats), F32),) + (pltpu.HBM((rows, feats // CHUNKS), BF16),) * CHUNKS,
+        grid_spec=pltpu.PrefetchScalarGridSpec(
+            num_scalar_prefetch=1,
+            grid=(feats // tile,),
+            in_specs=[pl.BlockSpec(gated_own.shape, lambda j, s: (0, 0, 0))] * 2
+            + [pl.BlockSpec((depth, tile), lambda j, s: (0, j))] * len(pieces),
+            out_specs=(block,) + tuple(chunk(k) for k in range(CHUNKS)),
+            scratch_shapes=[pltpu.VMEM((2 * rows, size * width), BF16)],
+        ),
+        compiler_params=pltpu.CompilerParams(vmem_limit_bytes=28 << 20),
+        cost_estimate=pl.CostEstimate(
+            flops=4 * rows * depth * len(pieces) * feats,
+            bytes_accessed=2 * depth * len(pieces) * feats + 6 * rows * feats,
+            transcendentals=0,
+        ),
+    )(scalars, *far([gated_own, gated_away, *pieces]))
 
 
 def merge_kernel(scalars, own, away, out):
@@ -265,7 +324,7 @@
     scale = 1.0 / length
 
     half = rows // 2
-    first, second = w_out[:half], w_out[half:]
+    first, second, cotangent, w_out = tie((w_out[:half], w_out[half:], cotangent, w_out))
     swapped = send(w_out, perm=swap_core)
     cot_away = send(cotangent, perm=swap_pair)
     product, cot_away = tie((mul(keys, values), cot_away))
@@ -286,22 +345,28 @@
             gated_own, gated_away = deal(pair, gated, chans // (2 * size))
             *swap, gated_own, gated_away = tie((*swap, gated_own, gated_away))
             gated_away = send(gated_away, perm=swap_pair)
+        if step == max(size - 2, 3):
+            *swap, gated_away = tie((*swap, gated_away))
         pieces += [first, send(swap[0], perm=swap_core), second, send(swap[1], perm=swap_core)]
     places = [core] + [ring_place(lax.rem(at - s + size, size), size) for s in range(size)]
-    grad_own, grad_away, out_own, out_away = products(
-        jnp.stack(places), cotangent, cot_away, gated_own, gated_away, pieces
-    )
-    grad_gated = merge(pair, grad_own, send(grad_away, perm=swap_pair))
-    out_away = send(out_away, perm=swap_pair)
+    scalars = jnp.stack(places)
+    grad_own, grad_away = grad_of_gated(scalars, cotangent, cot_away, pieces)
+    grad_away = send(grad_away, perm=swap_pair)
+    out_own, *out_away = output_of(scalars, gated_own, gated_away, pieces)
+    grad_away, out_own, out_away = tie((grad_away, out_own, out_away))
+    grad_gated = merge(pair, grad_own, grad_away)
+    out_away = [send(chunk, perm=swap_pair) for chunk in out_away]
     grad_queries = mul(grad_gated, filtered)
     grad_filtered = mul(grad_gated, queries)
     grads = forward_dft(high_now, low_now, grad_filtered, ((1,), (0,)))
+    filt, out_away[0] = tie((filt, out_away[0]))
     back = inverse_dft(table, times_conj(grads, filt), scale)
     across = jnp.where(linked, back[:length], 0.0).astype(BF16)
     ahead = send(across, perm=earlier)
     taps_part = inverse_dft(table_now, times_conj(grads, data), scale)
-    taps_grad = sum_over_ring(taps_part, nseq, place).T
-    outputs = (out_own + out_away.astype(F32)).astype(BF16)
+    taps_grad, out_away[1:] = sum_over_ring(taps_part, nseq, place, out_away[1:])
+    taps_grad = taps_grad.T
+    outputs = (out_own + jnp.concatenate(out_away, 1).astype(F32)).astype(BF16)
     grad_product = (back[length:] + ahead.astype(F32)).astype(BF16)
     grad_keys = mul(grad_product, values)
     grad_values = mul(grad_product, keys)

time: 196 us -> 200 us (1.020)
  Pallas kernels: 16.1 us -> 25.6 us
  starting transfers between devices: 38.4 us -> 35.3 us
  waiting for transfers between devices: 90.1 us -> 87.8 us
    pallas_call x1 -> x2, Pallas kernels: 14.6 us -> 25.1 us  [the longest x1 12.8 us: output_of(): pl.pallas_call(functools.partial(output_kernel, size), out_shape=(pltpu.H...]
    ppermute x2 -> x5, waiting for transfers between devices: 13.8 us -> 5.85 us  [the longest x4 4.63 us: on_ring(): out_away = [send(chunk, perm=swap_pair) for chunk in out_away]]
    ppermute x14, starting transfers between devices: 20.5 us -> 14.2 us  [on_ring(): first, second = (send(first, perm=onward), send(second, perm=behind))]
    ppermute x14, waiting for transfers between devices: 52.1 us -> 57.3 us  [on_ring(): first, second = (send(first, perm=onward), send(second, perm=behind))]
    ppermute x2 -> x5, starting transfers between devices: 0.42 us -> 3.8 us  [the longest x4 3.73 us: on_ring(): out_away = [send(chunk, perm=swap_pair) for chunk in out_away]]
    ppermute x1, waiting for transfers between devices: 0.01 us -> 3.12 us  [on_ring(): cot_away = send(cotangent, perm=swap_pair)]
  transfers between devices with their start and end apart: 40 -> 43, of which waited for: 16 -> 16; matrix products, arithmetic and copies ran while one was open for 19% -> 19% of each run, Pallas kernels for 0% -> 7%
where the time goes in v2:
time: 200 us; the launch traced here: 199 us
  waiting for transfers between devices  87.8 us (44%)
  starting transfers between devices  35.3 us (18%)
  Pallas kernels  25.6 us (13%)
  matrix products  24.7 us (12%)
  local copies, waits for them, and re-layouts  16 us (8%)
  other arithmetic  7.08 us (4%)
  between operations  2.75 us (1%)
    ppermute x14, waiting for transfers between devices, on_ring(): first, second = (send(first, perm=onward), send(second, perm=behind))  57.3 us
    ppermute x4, waiting for transfers between devices, halve(): away = lax.ppermute(away, 'seq', [(i, i ^ bit) for i in range(nseq)])  17.3 us
    dot_general x6, matrix products, inverse_dft(): lax.dot_general(table, spectrum, (((0,), (0,)), ((), ())), precision=lax....  14.7 us
    ppermute x14, starting transfers between devices, on_ring(): first, second = (send(first, perm=onward), send(second, perm=behind))  14.2 us
    pallas_call x1, Pallas kernels, output_of(): pl.pallas_call(functools.partial(output_kernel, size), out_shape=(pltpu.H...  12.8 us
    pallas_call x1, Pallas kernels, grad_of_gated(): pl.pallas_call(functools.partial(grad_kernel, size), out_shape=(jax.Shape...  12.3 us
    unnamed x97, local copies, waits for them, and re-layouts  10.5 us
    ppermute x4, starting transfers between devices, halve(): away = lax.ppermute(away, 'seq', [(i, i ^ bit) for i in range(nseq)])  6.17 us
  transfers between devices with their start and end apart: 43, of which 16 were waited for; matrix products, arithmetic and copies ran while one was open for 19% of the time, Pallas kernels for 7%

profile of v2, /device:TPU:0, one launch (start us, length us, event | category | flops | bytes accessed | tf_op | source)
XLA Modules:
  0.0 199.1 jit_solution(1972735593215040251)
XLA Ops:
  3.1 2.9 %collective-permute-start = (bf16[128,4096]{1,0:T(8,128)(2,1)}, bf16[128,4096]{1,0:T(8,128)(2,1)}, u32[]{:S(2)}, u32[]{:S(2)}) collective-permute-start(bf16[128,4096]{1,0:T(8,128)(2,1)} %cot_own), channel_id=1, source_target_pairs={{0,2},{1,3},{2,0},{3,1},{4,6},{5,7},{6,4},{7,5},{8,10},{9,11},{10,... | collective-permute-start | bytes 3145736 | tf_op jit(solution)/shard_map/ppermute | solution.py:329
  8.7 2.6 %copy.48 = bf16[128,4096]{0,1:T(8,128)(2,1)} copy(bf16[128,4096]{1,0:T(8,128)(2,1)} %param.15) | data formatting | bytes 2097152 | tf_op args[2]
  12.9 6.8 %collective-permute-done.2.refs_4_ = bf16[64,4096]{1,0:T(8,128)(2,1)} collective-permute-done((bf16[64,4096]{1,0:T(8,128)(2,1)}, bf16[64,4096]{1,0:T(8,128)(2,1)}, u32[]{:S(2)}, u32[]{:S(2)}) %collective-permute-start.2) | collective-permute-done | bytes 524320 | tf_op jit(solution)/shard_map/ppermute | solution.py:336
  21.8 2.7 %fusion.77 = f32[256,4096]{1,0:T(8,128)} fusion(bf16[256,128]{1,0:T(8,128)(2,1)S(1)} %copy-done.35, bf16[128,4096]{0,1:T(8,128)(2,1)S(1)} %bitcast.61), kind=kOutput, calls=%fused_computation.100 | convolution fusion | flops 268435456 | bytes 5308416 | tf_op jit(solution)/shard_map/dot_general | solution.py:26
  26.4 3.1 %collective-permute-done.cot_away = bf16[128,4096]{1,0:T(8,128)(2,1)} collective-permute-done((bf16[128,4096]{1,0:T(8,128)(2,1)}, bf16[128,4096]{1,0:T(8,128)(2,1)}, u32[]{:S(2)}, u32[]{:S(2)}) %collective-permute-start) | collective-permute-done | bytes 1048608 | tf_op jit(solution)/shard_map/ppermute | solution.py:329
  30.9 2.9 %convolution_add_fusion.4 = f32[256,4096]{1,0:T(8,128)S(1)} fusion(f32[256,4096]{1,0:T(8,128)} %fusion.77, bf16[256,128]{1,0:T(8,128)(2,1)S(1)} %copy-done.34, bf16[128,4096]{0,1:T(8,128)(2,1)S(1)} %bitcast.60), kind=kOutput, calls=%fused_computation.9 | convolution fusion | flops 269484032 | bytes 9502720 | tf_op jit(solution)/shard_map/dot_general | solution.py:27
  33.8 2.5 %collective-permute-start.4 = (bf16[64,4096]{1,0:T(8,128)(2,1)}, bf16[64,4096]{1,0:T(8,128)(2,1)S(1)}, u32[]{:S(2)}, u32[]{:S(2)}) collective-permute-start(bf16[64,4096]{1,0:T(8,128)(2,1)} %collective-permute-done.2.refs_4_), channel_id=1, source_target_pairs={{0,1},{1,0},{2,3},{3,2},{4,5},{5,4},{6,7},{7,6},{8,9},{9,8},{10,11... | collective-permute-start | bytes 1572872 | tf_op jit(solution)/shard_map/ppermute | solution.py:350
  39.7 10.4 %collective-permute-done.10.refs_12_ = bf16[64,4096]{1,0:T(8,128)(2,1)S(1)} collective-permute-done((bf16[64,4096]{1,0:T(8,128)(2,1)S(1)}, bf16[64,4096]{1,0:T(8,128)(2,1)S(1)}, u32[]{:S(2)}, u32[]{:S(2)}) %collective-permute-start.10) | collective-permute-done | bytes 524320 | tf_op jit(solution)/shard_map/ppermute | solution.py:336
  50.2 6.9 %collective-permute-done.11.refs_14_ = bf16[64,4096]{1,0:T(8,128)(2,1)S(1)} collective-permute-done((bf16[64,4096]{1,0:T(8,128)(2,1)S(1)}, bf16[64,4096]{1,0:T(8,128)(2,1)S(1)}, u32[]{:S(2)}, u32[]{:S(2)}) %collective-permute-start.11) | collective-permute-done | bytes 524320 | tf_op jit(solution)/shard_map/ppermute | solution.py:336
  57.0 2.5 %collective-permute-start.17 = (bf16[64,4096]{1,0:T(8,128)(2,1)S(1)}, bf16[64,4096]{1,0:T(8,128)(2,1)S(1)}, u32[]{:S(2)}, u32[]{:S(2)}) collective-permute-start(bf16[64,4096]{1,0:T(8,128)(2,1)S(1)} %collective-permute-done.11.refs_14_), channel_id=1, source_target_pairs={{8,0},{9,1},{10,2},{11,3},{16,8},{17,9},{18,10},{19,11},{24,16},{2... | collective-permute-start | bytes 1572872 | tf_op jit(solution)/shard_map/ppermute | solution.py:336
  61.8 9.9 %collective-permute-done.15.refs_16_ = bf16[64,4096]{1,0:T(8,128)(2,1)} collective-permute-done((bf16[64,4096]{1,0:T(8,128)(2,1)S(1)}, bf16[64,4096]{1,0:T(8,128)(2,1)}, u32[]{:S(2)}, u32[]{:S(2)}) %collective-permute-start.15) | collective-permute-done | bytes 524320 | tf_op jit(solution)/shard_map/ppermute | solution.py:336
  75.1 2.7 %fusion.12 = (bf16[128,4096]{1,0:T(8,128)(2,1)S(1)}, f32[128,4096]{1,0:T(8,128)}) fusion(bf16[128,4096]{1,0:T(8,128)(2,1)S(1)} %copy-done.9, f32[4096,128]{0,1:T(8,128)S(1)} %fusion.36, f32[128,128]{1,0:T(8,128)S(1)} %copy-done.37, f32[256,4096]{1,0:T(8,128)S(1)} %convolution_add_fusion.4, f32[256,4096]{1,0:T(8,128)S(1)} %fusion.4), kind=kOutput, calls=%fused_computation.25 | convolution fusion | flops 407896064 | bytes 14745600 | tf_op jit(solution)/shard_map/dot_general | solution.py:44
  79.4 5.9 %collective-permute-done.19.refs_20_ = bf16[64,4096]{1,0:T(8,128)(2,1)} collective-permute-done((bf16[64,4096]{1,0:T(8,128)(2,1)}, bf16[64,4096]{1,0:T(8,128)(2,1)}, u32[]{:S(2)}, u32[]{:S(2)}) %collective-permute-start.19) | collective-permute-done | bytes 524320 | tf_op jit(solution)/shard_map/ppermute | solution.py:336
  87.4 4.1 %collective-permute-done.25.gated_away = bf16[8,128,256]{2,1,0:T(8,128)(2,1)S(1)} collective-permute-done((bf16[8,128,256]{2,1,0:T(8,128)(2,1)S(1)}, bf16[8,128,256]{2,1,0:T(8,128)(2,1)S(1)}, u32[]{:S(2)}, u32[]{:S(2)}) %collective-permute-start.25) | collective-permute-done | bytes 524320 | tf_op jit(solution)/shard_map/ppermute | solution.py:347
  92.2 5.8 %collective-permute-done.23.refs_24_ = bf16[64,4096]{1,0:T(8,128)(2,1)S(1)} collective-permute-done((bf16[64,4096]{1,0:T(8,128)(2,1)}, bf16[64,4096]{1,0:T(8,128)(2,1)S(1)}, u32[]{:S(2)}, u32[]{:S(2)}) %collective-permute-start.23) | collective-permute-done | bytes 524320 | tf_op jit(solution)/shard_map/ppermute | solution.py:336
  101.8 10.0 %collective-permute-done.28.refs_28_ = bf16[64,4096]{1,0:T(8,128)(2,1)} collective-permute-done((bf16[64,4096]{1,0:T(8,128)(2,1)S(1)}, bf16[64,4096]{1,0:T(8,128)(2,1)}, u32[]{:S(2)}, u32[]{:S(2)}) %collective-permute-start.28) | collective-permute-done | bytes 524320 | tf_op jit(solution)/shard_map/ppermute | solution.py:336
  116.2 12.3 %shard_map.165 = (bf16[8,128,256]{2,1,0:T(8,128)(2,1)S(1)}, bf16[8,128,256]{2,1,0:T(8,128)(2,1)}) custom-call(s32[9]{0:T(128)S(1)} %stack.39.scalars, bf16[128,4096]{1,0:T(8,128)(2,1)} %cot_own, bf16[128,4096]{1,0:T(8,128)(2,1)} %collective-permute-done.cot_away, bf16[64,4096]{1,0:T(8,128)(2,1)} %get-tuple-element.46.refs_0_, ...), custom_call_target="tpu_custom_call" | custom-call | flops 4294967296 | bytes 18874368 | tf_op jit(solution)/shard_map/pallas_call | solution.py:234
  128.6 12.8 %shard_map.166 = (f32[128,4096]{1,0:T(8,128)}, bf16[128,1024]{1,0:T(8,128)(2,1)}, bf16[128,1024]{1,0:T(8,128)(2,1)}, bf16[128,1024]{1,0:T(8,128)(2,1)}, bf16[128,1024]{1,0:T(8,128)(2,1)}) custom-call(s32[9]{0:T(128)S(1)} %stack.39.scalars, bf16[8,128,256]{2,1,0:T(8,128)(2,1)} %copy-done.2, bf16[8,128,256]{2,1,0:T(8,128)(2,1)} %copy-done.36, ...), custom_call_target="tpu_custom_call" | custom-call | flops 4294967296 | bytes 19922944 | tf_op jit(solution)/shard_map/pallas_call | solution.py:264
  151.6 4.6 %collective-permute-done.33 = bf16[128,1024]{1,0:T(8,128)(2,1)} collective-permute-done((bf16[128,1024]{1,0:T(8,128)(2,1)}, bf16[128,1024]{1,0:T(8,128)(2,1)}, u32[]{:S(2)}, u32[]{:S(2)}) %collective-permute-start.33) | collective-permute-done | bytes 262176 | tf_op jit(solution)/shard_map/ppermute | solution.py:358
  156.2 5.7 %fusion.22 = f32[4096,256]{1,0:T(8,128)S(1)} fusion(f32[128,256]{1,0:T(8,128)S(1)} %copy-done.40, f32[256,4096]{1,0:T(8,128)} %copy-done.3, f32[256,4096]{1,0:T(8,128)} %copy-done.7), kind=kOutput, calls=%fused_computation.37 | convolution fusion | flops 806879232 | bytes 12713984 | tf_op jit(solution)/shard_map/dot_general | solution.py:44
  165.8 2.5 %collective-permute-start.36 = (bf16[8,128,128]{2,1,0:T(8,128)(2,1)S(1)}, bf16[8,128,128]{2,1,0:T(8,128)(2,1)S(1)}, u32[]{:S(2)}, u32[]{:S(2)}) collective-permute-start(bf16[8,128,128]{2,1,0:T(8,128)(2,1)S(1)} %fusion.69), channel_id=1, source_target_pairs={{0,4},{1,5},{2,6},{3,7},{4,0},{5,1},{6,2},{7,3},{8,12},{9,13},{10,... | collective-permute-start | bytes 786440 | tf_op jit(solution)/shard_map/ppermute | solution.py:111
  169.7 2.9 %collective-permute-done.36 = bf16[8,128,128]{2,1,0:T(8,128)(2,1)S(1)} collective-permute-done((bf16[8,128,128]{2,1,0:T(8,128)(2,1)S(1)}, bf16[8,128,128]{2,1,0:T(8,128)(2,1)S(1)}, u32[]{:S(2)}, u32[]{:S(2)}) %collective-permute-start.36) | collective-permute-done | bytes 262176 | tf_op jit(solution)/shard_map/ppermute | solution.py:111
  176.3 11.9 %collective-permute-done.40 = bf16[4,128,128]{2,1,0:T(8,128)(2,1)S(1)} collective-permute-done((bf16[4,128,128]{2,1,0:T(8,128)(2,1)S(1)}, bf16[4,128,128]{2,1,0:T(8,128)(2,1)S(1)}, u32[]{:S(2)}, u32[]{:S(2)}) %collective-permute-start.40) | collective-permute-done | bytes 131104 | tf_op jit(solution)/shard_map/ppermute | solution.py:111
  190.9 2.6 %collective-permute-done.41 = bf16[2,128,128]{2,1,0:T(8,128)(2,1)S(1)} collective-permute-done((bf16[2,128,128]{2,1,0:T(8,128)(2,1)S(1)}, bf16[2,128,128]{2,1,0:T(8,128)(2,1)S(1)}, u32[]{:S(2)}, u32[]{:S(2)}) %collective-permute-start.41) | collective-permute-done | bytes 65568 | tf_op jit(solution)/shard_map/ppermute | solution.py:111
  (196 shorter events, 59.3 us)
Async XLA Ops:
  3.1 26.4 %collective-permute-start = (bf16[128,4096]{1,0:T(8,128)(2,1)}, bf16[128,4096]{1,0:T(8,128)(2,1)}, u32[]{:S(2)}, u32[]{:S(2)}) collective-permute-start(bf16[128,4096]{1,0:T(8,128)(2,1)} %cot_own), channel_id=1, source_target_pairs={{0,2},{1,3},{2,0},{3,1},{4,6},{5,7},{6,4},{7,5},{8,10},{9,11},{10,... | collective-permute-start | bytes 3145736 | tf_op jit(solution)/shard_map/ppermute | solution.py:329
  6.0 13.7 %collective-permute-start.2 = (bf16[64,4096]{1,0:T(8,128)(2,1)}, bf16[64,4096]{1,0:T(8,128)(2,1)}, u32[]{:S(2)}, u32[]{:S(2)}) collective-permute-start(bf16[64,4096]{1,0:T(8,128)(2,1)} %get-tuple-element.46.refs_0_), channel_id=1, source_target_pairs={{0,8},{1,9},{2,10},{3,11},{8,16},{9,17},{10,18},{11,19},{16,24},{1... | collective-permute-start | bytes 1572872 | tf_op jit(solution)/shard_map/ppermute | solution.py:336
  7.6 13.7 %collective-permute-start.3 = (bf16[64,4096]{1,0:T(8,128)(2,1)}, bf16[64,4096]{1,0:T(8,128)(2,1)}, u32[]{:S(2)}, u32[]{:S(2)}) collective-permute-start(bf16[64,4096]{1,0:T(8,128)(2,1)} %get-tuple-element.48.refs_2_), channel_id=1, source_target_pairs={{8,0},{9,1},{10,2},{11,3},{16,8},{17,9},{18,10},{19,11},{24,16},{2... | collective-permute-start | bytes 1572872 | tf_op jit(solution)/shard_map/ppermute | solution.py:336
  8.1 70.7 %collective-permute-start.1 = (bf16[128,4096]{1,0:T(8,128)(2,1)}, bf16[128,4096]{1,0:T(8,128)(2,1)}, u32[]{:S(2)}, u32[]{:S(2)}) collective-permute-start(bf16[128,4096]{1,0:T(8,128)(2,1)} %param.16), channel_id=1, source_target_pairs={{0,1},{1,0},{2,3},{3,2},{4,5},{5,4},{6,7},{7,6},{8,9},{9,8},{10,11... | collective-permute-start | bytes 3145736 | tf_op jit(solution)/shard_map/ppermute | solution.py:328
  19.7 16.5 %collective-permute-start.6 = (bf16[64,4096]{1,0:T(8,128)(2,1)}, bf16[64,4096]{1,0:T(8,128)(2,1)S(1)}, u32[]{:S(2)}, u32[]{:S(2)}) collective-permute-start(bf16[64,4096]{1,0:T(8,128)(2,1)} %collective-permute-done.2.refs_4_), channel_id=1, source_target_pairs={{0,8},{1,9},{2,10},{3,11},{8,16},{9,17},{10,18},{11,19},{16,24},{1... | collective-permute-start | bytes 1572872 | tf_op jit(solution)/shard_map/ppermute | solution.py:336
  21.3 16.5 %collective-permute-start.8 = (bf16[64,4096]{1,0:T(8,128)(2,1)}, bf16[64,4096]{1,0:T(8,128)(2,1)S(1)}, u32[]{:S(2)}, u32[]{:S(2)}) collective-permute-start(bf16[64,4096]{1,0:T(8,128)(2,1)} %collective-permute-done.3.refs_6_), channel_id=1, source_target_pairs={{8,0},{9,1},{10,2},{11,3},{16,8},{17,9},{18,10},{19,11},{24,16},{2... | collective-permute-start | bytes 1572872 | tf_op jit(solution)/shard_map/ppermute | solution.py:336
  29.5 27.5 %collective-permute-start.12 = (bf16[128,4096]{0,1:T(8,128)(2,1)S(1)}, bf16[128,4096]{0,1:T(8,128)(2,1)S(1)}, u32[]{:S(2)}, u32[]{:S(2)}) collective-permute-start(bf16[128,4096]{0,1:T(8,128)(2,1)S(1)} %fusion.11), channel_id=1, source_target_pairs={{0,1},{1,2},{2,3},{3,4},{4,5},{5,6},{6,7},{7,8},{8,9},{9,10},{10,1... | collective-permute-start | bytes 3145736 | tf_op jit(solution)/shard_map/ppermute | solution.py:331
  33.8 27.3 %collective-permute-start.4 = (bf16[64,4096]{1,0:T(8,128)(2,1)}, bf16[64,4096]{1,0:T(8,128)(2,1)S(1)}, u32[]{:S(2)}, u32[]{:S(2)}) collective-permute-start(bf16[64,4096]{1,0:T(8,128)(2,1)} %collective-permute-done.2.refs_4_), channel_id=1, source_target_pairs={{0,1},{1,0},{2,3},{3,2},{4,5},{5,4},{6,7},{7,6},{8,9},{9,8},{10,11... | collective-permute-start | bytes 1572872 | tf_op jit(solution)/shard_map/ppermute | solution.py:350
  36.3 13.9 %collective-permute-start.10 = (bf16[64,4096]{1,0:T(8,128)(2,1)S(1)}, bf16[64,4096]{1,0:T(8,128)(2,1)S(1)}, u32[]{:S(2)}, u32[]{:S(2)}) collective-permute-start(bf16[64,4096]{1,0:T(8,128)(2,1)S(1)} %collective-permute-done.6.refs_8_), channel_id=1, source_target_pairs={{0,8},{1,9},{2,10},{3,11},{8,16},{9,17},{10,18},{11,19},{16,24},{1... | collective-permute-start | bytes 1572872 | tf_op jit(solution)/shard_map/ppermute | solution.py:336
  37.8 19.2 %collective-permute-start.11 = (bf16[64,4096]{1,0:T(8,128)(2,1)S(1)}, bf16[64,4096]{1,0:T(8,128)(2,1)S(1)}, u32[]{:S(2)}, u32[]{:S(2)}) collective-permute-start(bf16[64,4096]{1,0:T(8,128)(2,1)S(1)} %collective-permute-done.8.refs_10_), channel_id=1, source_target_pairs={{8,0},{9,1},{10,2},{11,3},{16,8},{17,9},{18,10},{19,11},{24,16},{2... | collective-permute-start | bytes 1572872 | tf_op jit(solution)/shard_map/ppermute | solution.py:336
  57.0 14.7 %collective-permute-start.15 = (bf16[64,4096]{1,0:T(8,128)(2,1)S(1)}, bf16[64,4096]{1,0:T(8,128)(2,1)}, u32[]{:S(2)}, u32[]{:S(2)}) collective-permute-start(bf16[64,4096]{1,0:T(8,128)(2,1)S(1)} %collective-permute-done.10.refs_12_), channel_id=1, source_target_pairs={{0,8},{1,9},{2,10},{3,11},{8,16},{9,17},{10,18},{11,19},{16,24},{1... | collective-permute-start | bytes 1572872 | tf_op jit(solution)/shard_map/ppermute | solution.py:336
  57.0 14.7 %collective-permute-start.17 = (bf16[64,4096]{1,0:T(8,128)(2,1)S(1)}, bf16[64,4096]{1,0:T(8,128)(2,1)S(1)}, u32[]{:S(2)}, u32[]{:S(2)}) collective-permute-start(bf16[64,4096]{1,0:T(8,128)(2,1)S(1)} %collective-permute-done.11.refs_14_), channel_id=1, source_target_pairs={{8,0},{9,1},{10,2},{11,3},{16,8},{17,9},{18,10},{19,11},{24,16},{2... | collective-permute-start | bytes 1572872 | tf_op jit(solution)/shard_map/ppermute | solution.py:336
  61.1 17.6 %collective-permute-start.7 = (bf16[64,4096]{1,0:T(8,128)(2,1)S(1)}, bf16[64,4096]{1,0:T(8,128)(2,1)S(1)}, u32[]{:S(2)}, u32[]{:S(2)}) collective-permute-start(bf16[64,4096]{1,0:T(8,128)(2,1)S(1)} %collective-permute-done.6.refs_8_), channel_id=1, source_target_pairs={{0,1},{1,0},{2,3},{3,2},{4,5},{5,4},{6,7},{7,6},{8,9},{9,8},{10,11... | collective-permute-start | bytes 1572872 | tf_op jit(solution)/shard_map/ppermute | solution.py:350
  61.3 17.6 %collective-permute-start.9 = (bf16[64,4096]{1,0:T(8,128)(2,1)S(1)}, bf16[64,4096]{1,0:T(8,128)(2,1)S(1)}, u32[]{:S(2)}, u32[]{:S(2)}) collective-permute-start(bf16[64,4096]{1,0:T(8,128)(2,1)S(1)} %collective-permute-done.8.refs_10_), channel_id=1, source_target_pairs={{0,1},{1,0},{2,3},{3,2},{4,5},{5,4},{6,7},{7,6},{8,9},{9,8},{10,11... | collective-permute-start | bytes 1572872 | tf_op jit(solution)/shard_map/ppermute | solution.py:350
  71.7 13.6 %collective-permute-start.19 = (bf16[64,4096]{1,0:T(8,128)(2,1)}, bf16[64,4096]{1,0:T(8,128)(2,1)}, u32[]{:S(2)}, u32[]{:S(2)}) collective-permute-start(bf16[64,4096]{1,0:T(8,128)(2,1)} %collective-permute-done.15.refs_16_), channel_id=1, source_target_pairs={{0,8},{1,9},{2,10},{3,11},{8,16},{9,17},{10,18},{11,19},{16,24},{1... | collective-permute-start | bytes 1572872 | tf_op jit(solution)/shard_map/ppermute | solution.py:336
  71.7 15.0 %collective-permute-start.21 = (bf16[64,4096]{1,0:T(8,128)(2,1)S(1)}, bf16[64,4096]{1,0:T(8,128)(2,1)S(1)}, u32[]{:S(2)}, u32[]{:S(2)}) collective-permute-start(bf16[64,4096]{1,0:T(8,128)(2,1)S(1)} %collective-permute-done.17.refs_18_), channel_id=1, source_target_pairs={{8,0},{9,1},{10,2},{11,3},{16,8},{17,9},{18,10},{19,11},{24,16},{2... | collective-permute-start | bytes 1572872 | tf_op jit(solution)/shard_map/ppermute | solution.py:336
  98.0 13.8 %collective-permute-start.28 = (bf16[64,4096]{1,0:T(8,128)(2,1)S(1)}, bf16[64,4096]{1,0:T(8,128)(2,1)}, u32[]{:S(2)}, u32[]{:S(2)}) collective-permute-start(bf16[64,4096]{1,0:T(8,128)(2,1)S(1)} %collective-permute-done.23.refs_24_), channel_id=1, source_target_pairs={{0,8},{1,9},{2,10},{3,11},{8,16},{9,17},{10,18},{11,19},{16,24},{1... | collective-permute-start | bytes 1572872 | tf_op jit(solution)/shard_map/ppermute | solution.py:336
  128.5 14.1 %collective-permute-start.32 = (bf16[8,128,256]{2,1,0:T(8,128)(2,1)}, bf16[8,128,256]{2,1,0:T(8,128)(2,1)S(1)}, u32[]{:S(2)}, u32[]{:S(2)}) collective-permute-start(bf16[8,128,256]{2,1,0:T(8,128)(2,1)} %get-tuple-element.60), channel_id=1, source_target_pairs={{0,2},{1,3},{2,0},{3,1},{4,6},{5,7},{6,4},{7,5},{8,10},{9,11},{10,... | collective-permute-start | bytes 1572872 | tf_op jit(solution)/shard_map/ppermute | solution.py:354
  149.3 15.0 %collective-permute-start.34 = (f32[2,8,128,128]{3,2,1,0:T(8,128)S(1)}, f32[2,8,128,128]{3,2,1,0:T(8,128)}, u32[]{:S(2)}, u32[]{:S(2)}) collective-permute-start(f32[2,8,128,128]{3,2,1,0:T(8,128)S(1)} %get-tuple-element.74), channel_id=1, source_target_pairs={{0,1},{1,0},{2,3},{3,2},{4,5},{5,4},{6,7},{7,6},{8,9},{9,8},{10,11... | collective-permute-start | bytes 3145736 | tf_op jit(solution)/shard_map/ppermute | solution.py:115
  149.5 16.2 %collective-permute-start.35 = (bf16[128,1024]{1,0:T(8,128)(2,1)}, bf16[128,1024]{1,0:T(8,128)(2,1)S(1)}, u32[]{:S(2)}, u32[]{:S(2)}) collective-permute-start(bf16[128,1024]{1,0:T(8,128)(2,1)} %get-tuple-element.75), channel_id=1, source_target_pairs={{0,2},{1,3},{2,0},{3,1},{4,6},{5,7},{6,4},{7,5},{8,10},{9,11},{10,... | collective-permute-start | bytes 786440 | tf_op jit(solution)/shard_map/ppermute | solution.py:358
  150.9 21.8 %collective-permute-start.37 = (bf16[128,1024]{1,0:T(8,128)(2,1)S(1)}, bf16[128,1024]{1,0:T(8,128)(2,1)S(1)}, u32[]{:S(2)}, u32[]{:S(2)}) collective-permute-start(bf16[128,1024]{1,0:T(8,128)(2,1)S(1)} %copy-done.45), channel_id=1, source_target_pairs={{0,2},{1,3},{2,0},{3,1},{4,6},{5,7},{6,4},{7,5},{8,10},{9,11},{10,... | collective-permute-start | bytes 786440 | tf_op jit(solution)/shard_map/ppermute | solution.py:358
  168.4 21.8 %collective-permute-start.39 = (bf16[128,4096]{0,1:T(8,128)(2,1)S(1)}, bf16[128,4096]{0,1:T(8,128)(2,1)S(1)}, u32[]{:S(2)}, u32[]{:S(2)}) collective-permute-start(bf16[128,4096]{0,1:T(8,128)(2,1)S(1)} %fusion.17), channel_id=1, source_target_pairs={{1,0},{2,1},{3,2},{4,3},{5,4},{6,5},{7,6},{8,7},{9,8},{10,9},{11,1... | collective-permute-start | bytes 3145736 | tf_op jit(solution)/shard_map/ppermute | solution.py:365
  172.7 15.5 %collective-permute-start.40 = (bf16[4,128,128]{2,1,0:T(8,128)(2,1)S(1)}, bf16[4,128,128]{2,1,0:T(8,128)(2,1)S(1)}, u32[]{:S(2)}, u32[]{:S(2)}) collective-permute-start(bf16[4,128,128]{2,1,0:T(8,128)(2,1)S(1)} %fusion.70), channel_id=1, source_target_pairs={{0,8},{1,9},{2,10},{3,11},{4,12},{5,13},{6,14},{7,15},{8,0},{9,1},... | collective-permute-start | bytes 393224 | tf_op jit(solution)/shard_map/ppermute | solution.py:111
  175.5 18.1 %collective-permute-start.38 = (bf16[128,1024]{1,0:T(8,128)(2,1)S(1)}, bf16[128,1024]{1,0:T(8,128)(2,1)S(1)}, u32[]{:S(2)}, u32[]{:S(2)}) collective-permute-start(bf16[128,1024]{1,0:T(8,128)(2,1)S(1)} %copy-done.44), channel_id=1, source_target_pairs={{0,2},{1,3},{2,0},{3,1},{4,6},{5,7},{6,4},{7,5},{8,10},{9,11},{10,... | collective-permute-start | bytes 786440 | tf_op jit(solution)/shard_map/ppermute | solution.py:358
  (65 other events, 749.1 us)

commit v3 on v2

--- a/solution.py
+++ b/solution.py
@@ -228,7 +228,7 @@
 def grad_of_gated(scalars, cot_own, cot_away, pieces):
     rows, feats = cot_own.shape
     size, depth = len(pieces) // 4, pieces[0].shape[0]
-    tile = min(512, feats)
+    tile = min(1024, feats)
     out = (size, rows, 4 * depth)
     whole = pl.BlockSpec(out, lambda j, s: (0, 0, 0))
     return pl.pallas_call(
@@ -254,7 +254,7 @@
 def output_of(scalars, gated_own, gated_away, pieces):
     size, rows, width = gated_own.shape
     depth, feats = pieces[0].shape
-    tile = min(512, feats // CHUNKS)
+    tile = min(1024, feats // CHUNKS)
     run = feats // CHUNKS // tile
     block = pl.BlockSpec((rows, tile), lambda j, s: (0, j))
 
@@ -362,9 +362,10 @@
     filt, out_away[0] = tie((filt, out_away[0]))
     back = inverse_dft(table, times_conj(grads, filt), scale)
     across = jnp.where(linked, back[:length], 0.0).astype(BF16)
+    taps_part = inverse_dft(table_now, times_conj(grads, data), scale)
+    guests = [out_away[1], (out_away[2], across), out_away[3]]
+    taps_grad, (out_away[1], (out_away[2], across), out_away[3]) = sum_over_ring(taps_part, nseq, place, guests)
     ahead = send(across, perm=earlier)
-    taps_part = inverse_dft(table_now, times_conj(grads, data), scale)
-    taps_grad, out_away[1:] = sum_over_ring(taps_part, nseq, place, out_away[1:])
     taps_grad = taps_grad.T
     outputs = (out_own + jnp.concatenate(out_away, 1).astype(F32)).astype(BF16)
     grad_product = (back[length:] + ahead.astype(F32)).astype(BF16)

time: 200 us -> 208 us (1.040)
  other arithmetic: 7.08 us -> 12.7 us
  Pallas kernels: 25.6 us -> 22.2 us
  local copies, waits for them, and re-layouts: 16 us -> 18.6 us
    convert_element_type x3, other arithmetic: 3.29 us -> 6.14 us  [mul(): return (a.astype(F32) * b.astype(F32)).astype(BF16)]
    unnamed x97 -> x101, local copies, waits for them, and re-layouts: 10.5 us -> 13.2 us
    ppermute x4, waiting for transfers between devices: 4.63 us -> 2.29 us  [on_ring(): out_away = [send(chunk, perm=swap_pair) for chunk in out_away]]
  transfers between devices with their start and end apart: 43 -> 43, of which waited for: 16 -> 16; matrix products, arithmetic and copies ran while one was open for 19% -> 19% of each run, Pallas kernels for 7% -> 6%
where the time goes in v3:
time: 208 us; the launch traced here: 207 us
  waiting for transfers between devices  89.3 us (43%)
  starting transfers between devices  36.2 us (17%)
  matrix products  24.9 us (12%)
  Pallas kernels  22.2 us (11%)
  local copies, waits for them, and re-layouts  18.6 us (9%)
  other arithmetic  12.7 us (6%)
  between operations  2.74 us (1%)
    ppermute x14, waiting for transfers between devices, on_ring(): first, second = (send(first, perm=onward), send(second, perm=behind))  57.9 us
    ppermute x4, waiting for transfers between devices, halve(): away = lax.ppermute(away, 'seq', [(i, i ^ bit) for i in range(nseq)])  19.1 us
    dot_general x6, matrix products, inverse_dft(): lax.dot_general(table, spectrum, (((0,), (0,)), ((), ())), precision=lax....  15 us
    ppermute x14, starting transfers between devices, on_ring(): first, second = (send(first, perm=onward), send(second, perm=behind))  13.7 us
    unnamed x101, local copies, waits for them, and re-layouts  13.2 us
    pallas_call x1, Pallas kernels, output_of(): pl.pallas_call(functools.partial(output_kernel, size), out_shape=(pltpu.H...  11.2 us
    pallas_call x1, Pallas kernels, grad_of_gated(): pl.pallas_call(functools.partial(grad_kernel, size), out_shape=(jax.Shape...  10.5 us
    ppermute x4, starting transfers between devices, halve(): away = lax.ppermute(away, 'seq', [(i, i ^ bit) for i in range(nseq)])  7.28 us
  transfers between devices with their start and end apart: 43, of which 16 were waited for; matrix products, arithmetic and copies ran while one was open for 19% of the time, Pallas kernels for 6%

profile of v3, /device:TPU:0, one launch (start us, length us, event | category | flops | bytes accessed | tf_op | source)
XLA Modules:
  0.0 206.8 jit_solution(6850422184360967172)
XLA Ops:
  3.1 2.9 %collective-permute-start = (bf16[128,4096]{1,0:T(8,128)(2,1)}, bf16[128,4096]{1,0:T(8,128)(2,1)}, u32[]{:S(2)}, u32[]{:S(2)}) collective-permute-start(bf16[128,4096]{1,0:T(8,128)(2,1)} %cot_own), channel_id=1, source_target_pairs={{0,2},{1,3},{2,0},{3,1},{4,6},{5,7},{6,4},{7,5},{8,10},{9,11},{10,... | collective-permute-start | bytes 3145736 | tf_op jit(solution)/shard_map/ppermute | solution.py:329
  8.7 2.6 %copy.48 = bf16[128,4096]{0,1:T(8,128)(2,1)} copy(bf16[128,4096]{1,0:T(8,128)(2,1)} %param.15) | data formatting | bytes 2097152 | tf_op args[2]
  12.9 6.8 %collective-permute-done.2.refs_4_ = bf16[64,4096]{1,0:T(8,128)(2,1)} collective-permute-done((bf16[64,4096]{1,0:T(8,128)(2,1)}, bf16[64,4096]{1,0:T(8,128)(2,1)}, u32[]{:S(2)}, u32[]{:S(2)}) %collective-permute-start.2) | collective-permute-done | bytes 524320 | tf_op jit(solution)/shard_map/ppermute | solution.py:336
  21.7 2.7 %fusion.77 = f32[256,4096]{1,0:T(8,128)} fusion(bf16[256,128]{1,0:T(8,128)(2,1)S(1)} %copy-done.36, bf16[128,4096]{0,1:T(8,128)(2,1)S(1)} %bitcast.61), kind=kOutput, calls=%fused_computation.100 | convolution fusion | flops 268435456 | bytes 5308416 | tf_op jit(solution)/shard_map/dot_general | solution.py:26
  26.4 3.1 %collective-permute-done.cot_away = bf16[128,4096]{1,0:T(8,128)(2,1)} collective-permute-done((bf16[128,4096]{1,0:T(8,128)(2,1)}, bf16[128,4096]{1,0:T(8,128)(2,1)}, u32[]{:S(2)}, u32[]{:S(2)}) %collective-permute-start) | collective-permute-done | bytes 1048608 | tf_op jit(solution)/shard_map/ppermute | solution.py:329
  30.8 2.9 %convolution_add_fusion.4 = f32[256,4096]{1,0:T(8,128)S(1)} fusion(f32[256,4096]{1,0:T(8,128)} %fusion.77, bf16[256,128]{1,0:T(8,128)(2,1)S(1)} %copy-done.35, bf16[128,4096]{0,1:T(8,128)(2,1)S(1)} %bitcast.60), kind=kOutput, calls=%fused_computation.9 | convolution fusion | flops 269484032 | bytes 9502720 | tf_op jit(solution)/shard_map/dot_general | solution.py:27
  33.8 2.5 %collective-permute-start.4 = (bf16[64,4096]{1,0:T(8,128)(2,1)}, bf16[64,4096]{1,0:T(8,128)(2,1)S(1)}, u32[]{:S(2)}, u32[]{:S(2)}) collective-permute-start(bf16[64,4096]{1,0:T(8,128)(2,1)} %collective-permute-done.2.refs_4_), channel_id=1, source_target_pairs={{0,1},{1,0},{2,3},{3,2},{4,5},{5,4},{6,7},{7,6},{8,9},{9,8},{10,11... | collective-permute-start | bytes 1572872 | tf_op jit(solution)/shard_map/ppermute | solution.py:350
  39.7 10.4 %collective-permute-done.10.refs_12_ = bf16[64,4096]{1,0:T(8,128)(2,1)S(1)} collective-permute-done((bf16[64,4096]{1,0:T(8,128)(2,1)S(1)}, bf16[64,4096]{1,0:T(8,128)(2,1)S(1)}, u32[]{:S(2)}, u32[]{:S(2)}) %collective-permute-start.10) | collective-permute-done | bytes 524320 | tf_op jit(solution)/shard_map/ppermute | solution.py:336
  50.2 6.9 %collective-permute-done.11.refs_14_ = bf16[64,4096]{1,0:T(8,128)(2,1)S(1)} collective-permute-done((bf16[64,4096]{1,0:T(8,128)(2,1)S(1)}, bf16[64,4096]{1,0:T(8,128)(2,1)S(1)}, u32[]{:S(2)}, u32[]{:S(2)}) %collective-permute-start.11) | collective-permute-done | bytes 524320 | tf_op jit(solution)/shard_map/ppermute | solution.py:336
  57.0 2.5 %collective-permute-start.17 = (bf16[64,4096]{1,0:T(8,128)(2,1)S(1)}, bf16[64,4096]{1,0:T(8,128)(2,1)}, u32[]{:S(2)}, u32[]{:S(2)}) collective-permute-start(bf16[64,4096]{1,0:T(8,128)(2,1)S(1)} %collective-permute-done.11.refs_14_), channel_id=1, source_target_pairs={{8,0},{9,1},{10,2},{11,3},{16,8},{17,9},{18,10},{19,11},{24,16},{2... | collective-permute-start | bytes 1572872 | tf_op jit(solution)/shard_map/ppermute | solution.py:336
  61.8 9.9 %collective-permute-done.15.refs_16_ = bf16[64,4096]{1,0:T(8,128)(2,1)} collective-permute-done((bf16[64,4096]{1,0:T(8,128)(2,1)S(1)}, bf16[64,4096]{1,0:T(8,128)(2,1)}, u32[]{:S(2)}, u32[]{:S(2)}) %collective-permute-start.15) | collective-permute-done | bytes 524320 | tf_op jit(solution)/shard_map/ppermute | solution.py:336
  75.0 2.7 %fusion.12 = (bf16[128,4096]{1,0:T(8,128)(2,1)S(1)}, f32[128,4096]{1,0:T(8,128)}) fusion(bf16[128,4096]{1,0:T(8,128)(2,1)S(1)} %copy-done.10, f32[4096,128]{0,1:T(8,128)S(1)} %fusion.36, f32[128,128]{1,0:T(8,128)S(1)} %copy-done.38, f32[256,4096]{1,0:T(8,128)S(1)} %convolution_add_fusion.4, f32[256,4096]{1,0:T(8,128)S(1)} %fusion.4), kind=kOutput, calls=%fused_computation.25 | convolution fusion | flops 407896064 | bytes 14745600 | tf_op jit(solution)/shard_map/dot_general | solution.py:44
  79.4 6.0 %collective-permute-done.19.refs_20_ = bf16[64,4096]{1,0:T(8,128)(2,1)} collective-permute-done((bf16[64,4096]{1,0:T(8,128)(2,1)}, bf16[64,4096]{1,0:T(8,128)(2,1)}, u32[]{:S(2)}, u32[]{:S(2)}) %collective-permute-start.19) | collective-permute-done | bytes 524320 | tf_op jit(solution)/shard_map/ppermute | solution.py:336
  87.4 4.1 %collective-permute-done.25.gated_away = bf16[8,128,256]{2,1,0:T(8,128)(2,1)S(1)} collective-permute-done((bf16[8,128,256]{2,1,0:T(8,128)(2,1)S(1)}, bf16[8,128,256]{2,1,0:T(8,128)(2,1)S(1)}, u32[]{:S(2)}, u32[]{:S(2)}) %collective-permute-start.25) | collective-permute-done | bytes 524320 | tf_op jit(solution)/shard_map/ppermute | solution.py:347
  92.1 5.8 %collective-permute-done.23.refs_24_ = bf16[64,4096]{1,0:T(8,128)(2,1)S(1)} collective-permute-done((bf16[64,4096]{1,0:T(8,128)(2,1)}, bf16[64,4096]{1,0:T(8,128)(2,1)S(1)}, u32[]{:S(2)}, u32[]{:S(2)}) %collective-permute-start.23) | collective-permute-done | bytes 524320 | tf_op jit(solution)/shard_map/ppermute | solution.py:336
  101.8 10.0 %collective-permute-done.28.refs_28_ = bf16[64,4096]{1,0:T(8,128)(2,1)} collective-permute-done((bf16[64,4096]{1,0:T(8,128)(2,1)S(1)}, bf16[64,4096]{1,0:T(8,128)(2,1)}, u32[]{:S(2)}, u32[]{:S(2)}) %collective-permute-start.28) | collective-permute-done | bytes 524320 | tf_op jit(solution)/shard_map/ppermute | solution.py:336
  116.2 10.5 %shard_map.165 = (bf16[8,128,256]{2,1,0:T(8,128)(2,1)S(1)}, bf16[8,128,256]{2,1,0:T(8,128)(2,1)}) custom-call(s32[9]{0:T(128)S(1)} %stack.39.scalars, bf16[128,4096]{1,0:T(8,128)(2,1)} %cot_own, bf16[128,4096]{1,0:T(8,128)(2,1)} %collective-permute-done.cot_away, bf16[64,4096]{1,0:T(8,128)(2,1)} %get-tuple-element.47.refs_0_, ...), custom_call_target="tpu_custom_call" | custom-call | flops 4294967296 | bytes 18874368 | tf_op jit(solution)/shard_map/pallas_call | solution.py:234
  126.8 11.2 %shard_map.166 = (f32[128,4096]{1,0:T(8,128)}, bf16[128,1024]{1,0:T(8,128)(2,1)}, bf16[128,1024]{1,0:T(8,128)(2,1)}, bf16[128,1024]{1,0:T(8,128)(2,1)}, bf16[128,1024]{1,0:T(8,128)(2,1)}) custom-call(s32[9]{0:T(128)S(1)} %stack.39.scalars, bf16[8,128,256]{2,1,0:T(8,128)(2,1)} %copy-done.2, bf16[8,128,256]{2,1,0:T(8,128)(2,1)} %copy-done.37, ...), custom_call_target="tpu_custom_call" | custom-call | flops 4294967296 | bytes 19922944 | tf_op jit(solution)/shard_map/pallas_call | solution.py:264
  138.0 2.8 %collective-permute-done.32.away = bf16[8,128,256]{2,1,0:T(8,128)(2,1)S(1)} collective-permute-done((bf16[8,128,256]{2,1,0:T(8,128)(2,1)}, bf16[8,128,256]{2,1,0:T(8,128)(2,1)S(1)}, u32[]{:S(2)}, u32[]{:S(2)}) %collective-permute-start.32) | collective-permute-done | bytes 524320 | tf_op jit(solution)/shard_map/ppermute | solution.py:354
  150.1 6.1 %fusion.22 = f32[4096,256]{1,0:T(8,128)S(1)} fusion(f32[128,256]{1,0:T(8,128)S(1)} %copy-done.43, f32[256,4096]{1,0:T(8,128)} %copy-done.3, f32[256,4096]{1,0:T(8,128)} %copy-done.7), kind=kOutput, calls=%fused_computation.38 | convolution fusion | flops 806879232 | bytes 12713984 | tf_op jit(solution)/shard_map/dot_general | solution.py:44
  164.2 5.5 %collective-permute-done.36 = bf16[8,128,128]{2,1,0:T(8,128)(2,1)S(1)} collective-permute-done((bf16[8,128,128]{2,1,0:T(8,128)(2,1)S(1)}, bf16[8,128,128]{2,1,0:T(8,128)(2,1)S(1)}, u32[]{:S(2)}, u32[]{:S(2)}) %collective-permute-start.36) | collective-permute-done | bytes 262176 | tf_op jit(solution)/shard_map/ppermute | solution.py:111
  172.2 3.8 %collective-permute-done.40 = bf16[4,128,128]{2,1,0:T(8,128)(2,1)} collective-permute-done((bf16[4,128,128]{2,1,0:T(8,128)(2,1)S(1)}, bf16[4,128,128]{2,1,0:T(8,128)(2,1)}, u32[]{:S(2)}, u32[]{:S(2)}) %collective-permute-start.40) | collective-permute-done | bytes 131104 | tf_op jit(solution)/shard_map/ppermute | solution.py:111
  189.2 9.8 %collective-permute-done.42 = bf16[1,128,128]{2,1,0:T(8,128)(2,1)S(1)} collective-permute-done((bf16[1,128,128]{2,1,0:T(8,128)(2,1)S(1)}, bf16[1,128,128]{2,1,0:T(8,128)(2,1)S(1)}, u32[]{:S(2)}, u32[]{:S(2)}) %collective-permute-start.42) | collective-permute-done | bytes 32800 | tf_op jit(solution)/shard_map/ppermute | solution.py:111
  199.7 3.4 %fusion.16 = (bf16[128,4096]{0,1:T(8,128)(2,1)S(1)}, bf16[128,4096]{0,1:T(8,128)(2,1)}) fusion(bf16[128,4096]{0,1:T(8,128)(2,1)S(1)} %copy-done.12, bf16[128,4096]{0,1:T(8,128)(2,1)} %collective-permute-done.39, f32[256,4096]{0,1:T(8,128)} %copy-done.9, bf16[128,4096]{0,1:T(8,128)(2,1)S(1)} %copy-done.13), kind=kLoop, calls=%fused_computation.29 | loop fusion | flops 5242880 | bytes 7340032 | tf_op jit(solution)/shard_map/convert_element_type | solution.py:51
  (200 shorter events, 69.1 us)
Async XLA Ops:
  3.1 26.4 %collective-permute-start = (bf16[128,4096]{1,0:T(8,128)(2,1)}, bf16[128,4096]{1,0:T(8,128)(2,1)}, u32[]{:S(2)}, u32[]{:S(2)}) collective-permute-start(bf16[128,4096]{1,0:T(8,128)(2,1)} %cot_own), channel_id=1, source_target_pairs={{0,2},{1,3},{2,0},{3,1},{4,6},{5,7},{6,4},{7,5},{8,10},{9,11},{10,... | collective-permute-start | bytes 3145736 | tf_op jit(solution)/shard_map/ppermute | solution.py:329
  6.0 13.7 %collective-permute-start.2 = (bf16[64,4096]{1,0:T(8,128)(2,1)}, bf16[64,4096]{1,0:T(8,128)(2,1)}, u32[]{:S(2)}, u32[]{:S(2)}) collective-permute-start(bf16[64,4096]{1,0:T(8,128)(2,1)} %get-tuple-element.47.refs_0_), channel_id=1, source_target_pairs={{0,8},{1,9},{2,10},{3,11},{8,16},{9,17},{10,18},{11,19},{16,24},{1... | collective-permute-start | bytes 1572872 | tf_op jit(solution)/shard_map/ppermute | solution.py:336
  7.6 13.7 %collective-permute-start.3 = (bf16[64,4096]{1,0:T(8,128)(2,1)}, bf16[64,4096]{1,0:T(8,128)(2,1)}, u32[]{:S(2)}, u32[]{:S(2)}) collective-permute-start(bf16[64,4096]{1,0:T(8,128)(2,1)} %get-tuple-element.49.refs_2_), channel_id=1, source_target_pairs={{8,0},{9,1},{10,2},{11,3},{16,8},{17,9},{18,10},{19,11},{24,16},{2... | collective-permute-start | bytes 1572872 | tf_op jit(solution)/shard_map/ppermute | solution.py:336
  8.0 70.7 %collective-permute-start.1 = (bf16[128,4096]{1,0:T(8,128)(2,1)}, bf16[128,4096]{1,0:T(8,128)(2,1)}, u32[]{:S(2)}, u32[]{:S(2)}) collective-permute-start(bf16[128,4096]{1,0:T(8,128)(2,1)} %param.16), channel_id=1, source_target_pairs={{0,1},{1,0},{2,3},{3,2},{4,5},{5,4},{6,7},{7,6},{8,9},{9,8},{10,11... | collective-permute-start | bytes 3145736 | tf_op jit(solution)/shard_map/ppermute | solution.py:328
  19.7 16.5 %collective-permute-start.6 = (bf16[64,4096]{1,0:T(8,128)(2,1)}, bf16[64,4096]{1,0:T(8,128)(2,1)S(1)}, u32[]{:S(2)}, u32[]{:S(2)}) collective-permute-start(bf16[64,4096]{1,0:T(8,128)(2,1)} %collective-permute-done.2.refs_4_), channel_id=1, source_target_pairs={{0,8},{1,9},{2,10},{3,11},{8,16},{9,17},{10,18},{11,19},{16,24},{1... | collective-permute-start | bytes 1572872 | tf_op jit(solution)/shard_map/ppermute | solution.py:336
  21.3 16.5 %collective-permute-start.8 = (bf16[64,4096]{1,0:T(8,128)(2,1)}, bf16[64,4096]{1,0:T(8,128)(2,1)S(1)}, u32[]{:S(2)}, u32[]{:S(2)}) collective-permute-start(bf16[64,4096]{1,0:T(8,128)(2,1)} %collective-permute-done.3.refs_6_), channel_id=1, source_target_pairs={{8,0},{9,1},{10,2},{11,3},{16,8},{17,9},{18,10},{19,11},{24,16},{2... | collective-permute-start | bytes 1572872 | tf_op jit(solution)/shard_map/ppermute | solution.py:336
  29.5 27.5 %collective-permute-start.12 = (bf16[128,4096]{0,1:T(8,128)(2,1)S(1)}, bf16[128,4096]{0,1:T(8,128)(2,1)S(1)}, u32[]{:S(2)}, u32[]{:S(2)}) collective-permute-start(bf16[128,4096]{0,1:T(8,128)(2,1)S(1)} %fusion.11), channel_id=1, source_target_pairs={{0,1},{1,2},{2,3},{3,4},{4,5},{5,6},{6,7},{7,8},{8,9},{9,10},{10,1... | collective-permute-start | bytes 3145736 | tf_op jit(solution)/shard_map/ppermute | solution.py:331
  33.8 27.3 %collective-permute-start.4 = (bf16[64,4096]{1,0:T(8,128)(2,1)}, bf16[64,4096]{1,0:T(8,128)(2,1)S(1)}, u32[]{:S(2)}, u32[]{:S(2)}) collective-permute-start(bf16[64,4096]{1,0:T(8,128)(2,1)} %collective-permute-done.2.refs_4_), channel_id=1, source_target_pairs={{0,1},{1,0},{2,3},{3,2},{4,5},{5,4},{6,7},{7,6},{8,9},{9,8},{10,11... | collective-permute-start | bytes 1572872 | tf_op jit(solution)/shard_map/ppermute | solution.py:350
  36.2 13.9 %collective-permute-start.10 = (bf16[64,4096]{1,0:T(8,128)(2,1)S(1)}, bf16[64,4096]{1,0:T(8,128)(2,1)S(1)}, u32[]{:S(2)}, u32[]{:S(2)}) collective-permute-start(bf16[64,4096]{1,0:T(8,128)(2,1)S(1)} %collective-permute-done.6.refs_8_), channel_id=1, source_target_pairs={{0,8},{1,9},{2,10},{3,11},{8,16},{9,17},{10,18},{11,19},{16,24},{1... | collective-permute-start | bytes 1572872 | tf_op jit(solution)/shard_map/ppermute | solution.py:336
  37.8 19.2 %collective-permute-start.11 = (bf16[64,4096]{1,0:T(8,128)(2,1)S(1)}, bf16[64,4096]{1,0:T(8,128)(2,1)S(1)}, u32[]{:S(2)}, u32[]{:S(2)}) collective-permute-start(bf16[64,4096]{1,0:T(8,128)(2,1)S(1)} %collective-permute-done.8.refs_10_), channel_id=1, source_target_pairs={{8,0},{9,1},{10,2},{11,3},{16,8},{17,9},{18,10},{19,11},{24,16},{2... | collective-permute-start | bytes 1572872 | tf_op jit(solution)/shard_map/ppermute | solution.py:336
  57.0 14.7 %collective-permute-start.15 = (bf16[64,4096]{1,0:T(8,128)(2,1)S(1)}, bf16[64,4096]{1,0:T(8,128)(2,1)}, u32[]{:S(2)}, u32[]{:S(2)}) collective-permute-start(bf16[64,4096]{1,0:T(8,128)(2,1)S(1)} %collective-permute-done.10.refs_12_), channel_id=1, source_target_pairs={{0,8},{1,9},{2,10},{3,11},{8,16},{9,17},{10,18},{11,19},{16,24},{1... | collective-permute-start | bytes 1572872 | tf_op jit(solution)/shard_map/ppermute | solution.py:336
  57.0 14.7 %collective-permute-start.17 = (bf16[64,4096]{1,0:T(8,128)(2,1)S(1)}, bf16[64,4096]{1,0:T(8,128)(2,1)}, u32[]{:S(2)}, u32[]{:S(2)}) collective-permute-start(bf16[64,4096]{1,0:T(8,128)(2,1)S(1)} %collective-permute-done.11.refs_14_), channel_id=1, source_target_pairs={{8,0},{9,1},{10,2},{11,3},{16,8},{17,9},{18,10},{19,11},{24,16},{2... | collective-permute-start | bytes 1572872 | tf_op jit(solution)/shard_map/ppermute | solution.py:336
  61.1 17.6 %collective-permute-start.7 = (bf16[64,4096]{1,0:T(8,128)(2,1)S(1)}, bf16[64,4096]{1,0:T(8,128)(2,1)S(1)}, u32[]{:S(2)}, u32[]{:S(2)}) collective-permute-start(bf16[64,4096]{1,0:T(8,128)(2,1)S(1)} %collective-permute-done.6.refs_8_), channel_id=1, source_target_pairs={{0,1},{1,0},{2,3},{3,2},{4,5},{5,4},{6,7},{7,6},{8,9},{9,8},{10,11... | collective-permute-start | bytes 1572872 | tf_op jit(solution)/shard_map/ppermute | solution.py:350
  61.2 17.6 %collective-permute-start.9 = (bf16[64,4096]{1,0:T(8,128)(2,1)S(1)}, bf16[64,4096]{1,0:T(8,128)(2,1)S(1)}, u32[]{:S(2)}, u32[]{:S(2)}) collective-permute-start(bf16[64,4096]{1,0:T(8,128)(2,1)S(1)} %collective-permute-done.8.refs_10_), channel_id=1, source_target_pairs={{0,1},{1,0},{2,3},{3,2},{4,5},{5,4},{6,7},{7,6},{8,9},{9,8},{10,11... | collective-permute-start | bytes 1572872 | tf_op jit(solution)/shard_map/ppermute | solution.py:350
  71.7 13.6 %collective-permute-start.19 = (bf16[64,4096]{1,0:T(8,128)(2,1)}, bf16[64,4096]{1,0:T(8,128)(2,1)}, u32[]{:S(2)}, u32[]{:S(2)}) collective-permute-start(bf16[64,4096]{1,0:T(8,128)(2,1)} %collective-permute-done.15.refs_16_), channel_id=1, source_target_pairs={{0,8},{1,9},{2,10},{3,11},{8,16},{9,17},{10,18},{11,19},{16,24},{1... | collective-permute-start | bytes 1572872 | tf_op jit(solution)/shard_map/ppermute | solution.py:336
  71.7 15.3 %collective-permute-start.21 = (bf16[64,4096]{1,0:T(8,128)(2,1)}, bf16[64,4096]{1,0:T(8,128)(2,1)S(1)}, u32[]{:S(2)}, u32[]{:S(2)}) collective-permute-start(bf16[64,4096]{1,0:T(8,128)(2,1)} %collective-permute-done.17.refs_18_), channel_id=1, source_target_pairs={{8,0},{9,1},{10,2},{11,3},{16,8},{17,9},{18,10},{19,11},{24,16},{2... | collective-permute-start | bytes 1572872 | tf_op jit(solution)/shard_map/ppermute | solution.py:336
  78.8 13.1 %collective-permute-start.14 = (bf16[64,4096]{1,0:T(8,128)(2,1)S(1)}, bf16[64,4096]{1,0:T(8,128)(2,1)S(1)}, u32[]{:S(2)}, u32[]{:S(2)}) collective-permute-start(bf16[64,4096]{1,0:T(8,128)(2,1)S(1)} %collective-permute-done.11.refs_14_), channel_id=1, source_target_pairs={{0,1},{1,0},{2,3},{3,2},{4,5},{5,4},{6,7},{7,6},{8,9},{9,8},{10,11... | collective-permute-start | bytes 1572872 | tf_op jit(solution)/shard_map/ppermute | solution.py:350
  98.0 13.8 %collective-permute-start.28 = (bf16[64,4096]{1,0:T(8,128)(2,1)S(1)}, bf16[64,4096]{1,0:T(8,128)(2,1)}, u32[]{:S(2)}, u32[]{:S(2)}) collective-permute-start(bf16[64,4096]{1,0:T(8,128)(2,1)S(1)} %collective-permute-done.23.refs_24_), channel_id=1, source_target_pairs={{0,8},{1,9},{2,10},{3,11},{8,16},{9,17},{10,18},{11,19},{16,24},{1... | collective-permute-start | bytes 1572872 | tf_op jit(solution)/shard_map/ppermute | solution.py:336
  101.2 13.4 %collective-permute-start.22 = (bf16[64,4096]{1,0:T(8,128)(2,1)}, bf16[64,4096]{1,0:T(8,128)(2,1)S(1)}, u32[]{:S(2)}, u32[]{:S(2)}) collective-permute-start(bf16[64,4096]{1,0:T(8,128)(2,1)} %copy-done.23), channel_id=1, source_target_pairs={{0,1},{1,0},{2,3},{3,2},{4,5},{5,4},{6,7},{7,6},{8,9},{9,8},{10,11... | collective-permute-start | bytes 1572872 | tf_op jit(solution)/shard_map/ppermute | solution.py:350
  101.3 13.3 %collective-permute-start.26 = (bf16[64,4096]{1,0:T(8,128)(2,1)S(1)}, bf16[64,4096]{1,0:T(8,128)(2,1)S(1)}, u32[]{:S(2)}, u32[]{:S(2)}) collective-permute-start(bf16[64,4096]{1,0:T(8,128)(2,1)S(1)} %collective-permute-done.23.refs_24_), channel_id=1, source_target_pairs={{0,1},{1,0},{2,3},{3,2},{4,5},{5,4},{6,7},{7,6},{8,9},{9,8},{10,11... | collective-permute-start | bytes 1572872 | tf_op jit(solution)/shard_map/ppermute | solution.py:350
  126.7 14.1 %collective-permute-start.32 = (bf16[8,128,256]{2,1,0:T(8,128)(2,1)}, bf16[8,128,256]{2,1,0:T(8,128)(2,1)S(1)}, u32[]{:S(2)}, u32[]{:S(2)}) collective-permute-start(bf16[8,128,256]{2,1,0:T(8,128)(2,1)} %get-tuple-element.61), channel_id=1, source_target_pairs={{0,2},{1,3},{2,0},{3,1},{4,6},{5,7},{6,4},{7,5},{8,10},{9,11},{10,... | collective-permute-start | bytes 1572872 | tf_op jit(solution)/shard_map/ppermute | solution.py:354
  149.8 20.0 %collective-permute-start.37 = (bf16[128,1024]{1,0:T(8,128)(2,1)}, bf16[128,1024]{1,0:T(8,128)(2,1)S(1)}, u32[]{:S(2)}, u32[]{:S(2)}) collective-permute-start(bf16[128,1024]{1,0:T(8,128)(2,1)} %get-tuple-element.79), channel_id=1, source_target_pairs={{0,2},{1,3},{2,0},{3,1},{4,6},{5,7},{6,4},{7,5},{8,10},{9,11},{10,... | collective-permute-start | bytes 786440 | tf_op jit(solution)/shard_map/ppermute | solution.py:358
  182.3 17.4 %collective-permute-start.39 = (bf16[128,4096]{0,1:T(8,128)(2,1)}, bf16[128,4096]{0,1:T(8,128)(2,1)}, u32[]{:S(2)}, u32[]{:S(2)}) collective-permute-start(bf16[128,4096]{0,1:T(8,128)(2,1)} %fusion.18), channel_id=1, source_target_pairs={{1,0},{2,1},{3,2},{4,3},{5,4},{6,5},{7,6},{8,7},{9,8},{10,9},{11,1... | collective-permute-start | bytes 3145736 | tf_op jit(solution)/shard_map/ppermute | solution.py:368
  183.7 15.3 %collective-permute-start.42 = (bf16[1,128,128]{2,1,0:T(8,128)(2,1)S(1)}, bf16[1,128,128]{2,1,0:T(8,128)(2,1)S(1)}, u32[]{:S(2)}, u32[]{:S(2)}) collective-permute-start(bf16[1,128,128]{2,1,0:T(8,128)(2,1)S(1)} %dynamic-slice_convert_fusion.3), channel_id=1, source_target_pairs={{0,2},{1,3},{2,0},{3,1},{4,6},{5,7},{6,4},{7,5},{8,10},{9,11},{10,... | collective-permute-start | bytes 98312 | tf_op jit(solution)/shard_map/ppermute | solution.py:111
  (67 other events, 731.0 us)

commit v4 on v3

--- a/solution.py
+++ b/solution.py
@@ -359,13 +359,13 @@
     grad_queries = mul(grad_gated, filtered)
     grad_filtered = mul(grad_gated, queries)
     grads = forward_dft(high_now, low_now, grad_filtered, ((1,), (0,)))
-    filt, out_away[0] = tie((filt, out_away[0]))
     back = inverse_dft(table, times_conj(grads, filt), scale)
     across = jnp.where(linked, back[:length], 0.0).astype(BF16)
+    ahead = send(across, perm=earlier)
+    grads, across, out_away[0] = tie((grads, across, out_away[0]))
     taps_part = inverse_dft(table_now, times_conj(grads, data), scale)
-    guests = [out_away[1], (out_away[2], across), out_away[3]]
-    taps_grad, (out_away[1], (out_away[2], across), out_away[3]) = sum_over_ring(taps_part, nseq, place, guests)
-    ahead = send(across, perm=earlier)
+    guests = [out_away[1], ahead, out_away[2], out_away[3]]
+    taps_grad, (out_away[1], ahead, out_away[2], out_away[3]) = sum_over_ring(taps_part, nseq, place, guests)
     taps_grad = taps_grad.T
     outputs = (out_own + jnp.concatenate(out_away, 1).astype(F32)).astype(BF16)
     grad_product = (back[length:] + ahead.astype(F32)).astype(BF16)

time: 208 us -> 205 us (0.986)
  matrix products: 24.9 us -> 21.3 us
  starting transfers between devices: 36.2 us -> 39.5 us
  local copies, waits for them, and re-layouts: 18.6 us -> 16.4 us
    ppermute x4, waiting for transfers between devices: 2.29 us -> 16.7 us  [on_ring(): out_away = [send(chunk, perm=swap_pair) for chunk in out_away]]
    ppermute x4, waiting for transfers between devices: 19.1 us -> 5.51 us  [halve(): away = lax.ppermute(away, 'seq', [(i, i ^ bit) for i in range(nseq)])]
    ppermute x4, starting transfers between devices: 7.28 us -> 11.3 us  [halve(): away = lax.ppermute(away, 'seq', [(i, i ^ bit) for i in range(nseq)])]
    dot_general x6, matrix products: 15 us -> 11.3 us  [inverse_dft(): lax.dot_general(table, spectrum, (((0,), (0,)), ((), ())), precision=lax....]
    unnamed x101, local copies, waits for them, and re-layouts: 13.2 us -> 11 us
  transfers between devices with their start and end apart: 43 -> 43, of which waited for: 16 -> 15; matrix products, arithmetic and copies ran while one was open for 19% -> 19% of each run, Pallas kernels for 6% -> 6%
where the time goes in v4:
time: 205 us
  waiting for transfers between devices  90 us (44%)
  starting transfers between devices  39.5 us (19%)
  Pallas kernels  22.2 us (11%)
  matrix products  21.3 us (10%)
  local copies, waits for them, and re-layouts  16.4 us (8%)
  other arithmetic  12.8 us (6%)
  between operations  2.7 us (1%)
    ppermute x14, waiting for transfers between devices, on_ring(): first, second = (send(first, perm=onward), send(second, perm=behind))  57.6 us
    ppermute x4, waiting for transfers between devices, on_ring(): out_away = [send(chunk, perm=swap_pair) for chunk in out_away]  16.7 us
    ppermute x14, starting transfers between devices, on_ring(): first, second = (send(first, perm=onward), send(second, perm=behind))  13.9 us
    ppermute x4, starting transfers between devices, halve(): away = lax.ppermute(away, 'seq', [(i, i ^ bit) for i in range(nseq)])  11.3 us
    dot_general x6, matrix products, inverse_dft(): lax.dot_general(table, spectrum, (((0,), (0,)), ((), ())), precision=lax....  11.3 us
    pallas_call x1, Pallas kernels, output_of(): pl.pallas_call(functools.partial(output_kernel, size), out_shape=(pltpu.H...  11.2 us
    unnamed x101, local copies, waits for them, and re-layouts  11 us
    pallas_call x1, Pallas kernels, grad_of_gated(): pl.pallas_call(functools.partial(grad_kernel, size), out_shape=(jax.Shape...  10.5 us
  transfers between devices with their start and end apart: 43, of which 15 were waited for; matrix products, arithmetic and copies ran while one was open for 19% of the time, Pallas kernels for 6%

profile of v4, /device:TPU:0, one launch (start us, length us, event | category | flops | bytes accessed | tf_op | source)
XLA Modules:
  0.0 204.9 jit_solution(5957982254297489361)
XLA Ops:
  3.1 2.9 %collective-permute-start = (bf16[128,4096]{1,0:T(8,128)(2,1)}, bf16[128,4096]{1,0:T(8,128)(2,1)}, u32[]{:S(2)}, u32[]{:S(2)}) collective-permute-start(bf16[128,4096]{1,0:T(8,128)(2,1)} %cot_own), channel_id=1, source_target_pairs={{0,2},{1,3},{2,0},{3,1},{4,6},{5,7},{6,4},{7,5},{8,10},{9,11},{10,... | collective-permute-start | bytes 3145736 | tf_op jit(solution)/shard_map/ppermute | solution.py:329
  8.7 2.6 %copy.48 = bf16[128,4096]{0,1:T(8,128)(2,1)} copy(bf16[128,4096]{1,0:T(8,128)(2,1)} %param.15) | data formatting | bytes 2097152 | tf_op args[2]
  12.9 6.8 %collective-permute-done.2.refs_4_ = bf16[64,4096]{1,0:T(8,128)(2,1)} collective-permute-done((bf16[64,4096]{1,0:T(8,128)(2,1)}, bf16[64,4096]{1,0:T(8,128)(2,1)}, u32[]{:S(2)}, u32[]{:S(2)}) %collective-permute-start.2) | collective-permute-done | bytes 524320 | tf_op jit(solution)/shard_map/ppermute | solution.py:336
  21.7 2.7 %fusion.77 = f32[256,4096]{1,0:T(8,128)} fusion(bf16[256,128]{1,0:T(8,128)(2,1)S(1)} %copy-done.32, bf16[128,4096]{0,1:T(8,128)(2,1)S(1)} %bitcast.61), kind=kOutput, calls=%fused_computation.100 | convolution fusion | flops 268435456 | bytes 5308416 | tf_op jit(solution)/shard_map/dot_general | solution.py:26
  26.4 3.1 %collective-permute-done.cot_away = bf16[128,4096]{1,0:T(8,128)(2,1)} collective-permute-done((bf16[128,4096]{1,0:T(8,128)(2,1)}, bf16[128,4096]{1,0:T(8,128)(2,1)}, u32[]{:S(2)}, u32[]{:S(2)}) %collective-permute-start) | collective-permute-done | bytes 1048608 | tf_op jit(solution)/shard_map/ppermute | solution.py:329
  30.8 2.9 %convolution_add_fusion.4 = f32[256,4096]{1,0:T(8,128)S(1)} fusion(f32[256,4096]{1,0:T(8,128)} %fusion.77, bf16[256,128]{1,0:T(8,128)(2,1)S(1)} %copy-done.31, bf16[128,4096]{0,1:T(8,128)(2,1)S(1)} %bitcast.60), kind=kOutput, calls=%fused_computation.9 | convolution fusion | flops 269484032 | bytes 9502720 | tf_op jit(solution)/shard_map/dot_general | solution.py:27
  39.7 10.4 %collective-permute-done.10.refs_12_ = bf16[64,4096]{1,0:T(8,128)(2,1)S(1)} collective-permute-done((bf16[64,4096]{1,0:T(8,128)(2,1)S(1)}, bf16[64,4096]{1,0:T(8,128)(2,1)S(1)}, u32[]{:S(2)}, u32[]{:S(2)}) %collective-permute-start.10) | collective-permute-done | bytes 524320 | tf_op jit(solution)/shard_map/ppermute | solution.py:336
  50.2 6.9 %collective-permute-done.11.refs_14_ = bf16[64,4096]{1,0:T(8,128)(2,1)S(1)} collective-permute-done((bf16[64,4096]{1,0:T(8,128)(2,1)S(1)}, bf16[64,4096]{1,0:T(8,128)(2,1)S(1)}, u32[]{:S(2)}, u32[]{:S(2)}) %collective-permute-start.11) | collective-permute-done | bytes 524320 | tf_op jit(solution)/shard_map/ppermute | solution.py:336
  61.8 9.9 %collective-permute-done.15.refs_16_ = bf16[64,4096]{1,0:T(8,128)(2,1)} collective-permute-done((bf16[64,4096]{1,0:T(8,128)(2,1)S(1)}, bf16[64,4096]{1,0:T(8,128)(2,1)}, u32[]{:S(2)}, u32[]{:S(2)}) %collective-permute-start.15) | collective-permute-done | bytes 524320 | tf_op jit(solution)/shard_map/ppermute | solution.py:336
  75.0 2.7 %fusion.12 = (bf16[128,4096]{1,0:T(8,128)(2,1)S(1)}, f32[128,4096]{1,0:T(8,128)}) fusion(bf16[128,4096]{1,0:T(8,128)(2,1)S(1)} %copy-done.9, f32[4096,128]{0,1:T(8,128)S(1)} %fusion.36, f32[128,128]{1,0:T(8,128)S(1)} %copy-done.34, f32[256,4096]{1,0:T(8,128)S(1)} %fusion.4, f32[256,4096]{1,0:T(8,128)S(1)} %convolution_add_fusion.4), kind=kOutput, calls=%fused_computation.25 | convolution fusion | flops 407896064 | bytes 14745600 | tf_op jit(solution)/shard_map/dot_general | solution.py:44
  79.4 5.9 %collective-permute-done.19.refs_20_ = bf16[64,4096]{1,0:T(8,128)(2,1)} collective-permute-done((bf16[64,4096]{1,0:T(8,128)(2,1)}, bf16[64,4096]{1,0:T(8,128)(2,1)}, u32[]{:S(2)}, u32[]{:S(2)}) %collective-permute-start.19) | collective-permute-done | bytes 524320 | tf_op jit(solution)/shard_map/ppermute | solution.py:336
  87.4 4.1 %collective-permute-done.25.gated_away = bf16[8,128,256]{2,1,0:T(8,128)(2,1)S(1)} collective-permute-done((bf16[8,128,256]{2,1,0:T(8,128)(2,1)S(1)}, bf16[8,128,256]{2,1,0:T(8,128)(2,1)S(1)}, u32[]{:S(2)}, u32[]{:S(2)}) %collective-permute-start.25) | collective-permute-done | bytes 524320 | tf_op jit(solution)/shard_map/ppermute | solution.py:347
  92.2 5.8 %collective-permute-done.23.refs_24_ = bf16[64,4096]{1,0:T(8,128)(2,1)S(1)} collective-permute-done((bf16[64,4096]{1,0:T(8,128)(2,1)}, bf16[64,4096]{1,0:T(8,128)(2,1)S(1)}, u32[]{:S(2)}, u32[]{:S(2)}) %collective-permute-start.23) | collective-permute-done | bytes 524320 | tf_op jit(solution)/shard_map/ppermute | solution.py:336
  101.8 10.0 %collective-permute-done.28.refs_28_ = bf16[64,4096]{1,0:T(8,128)(2,1)} collective-permute-done((bf16[64,4096]{1,0:T(8,128)(2,1)S(1)}, bf16[64,4096]{1,0:T(8,128)(2,1)}, u32[]{:S(2)}, u32[]{:S(2)}) %collective-permute-start.28) | collective-permute-done | bytes 524320 | tf_op jit(solution)/shard_map/ppermute | solution.py:336
  116.2 10.5 %shard_map.165 = (bf16[8,128,256]{2,1,0:T(8,128)(2,1)S(1)}, bf16[8,128,256]{2,1,0:T(8,128)(2,1)}) custom-call(s32[9]{0:T(128)S(1)} %stack.39.scalars, bf16[128,4096]{1,0:T(8,128)(2,1)} %cot_own, bf16[128,4096]{1,0:T(8,128)(2,1)} %collective-permute-done.cot_away, bf16[64,4096]{1,0:T(8,128)(2,1)} %get-tuple-element.48.refs_0_, ...), custom_call_target="tpu_custom_call" | custom-call | flops 4294967296 | bytes 18874368 | tf_op jit(solution)/shard_map/pallas_call | solution.py:234
  126.8 11.2 %shard_map.166 = (f32[128,4096]{1,0:T(8,128)}, bf16[128,1024]{1,0:T(8,128)(2,1)}, bf16[128,1024]{1,0:T(8,128)(2,1)}, bf16[128,1024]{1,0:T(8,128)(2,1)}, bf16[128,1024]{1,0:T(8,128)(2,1)}) custom-call(s32[9]{0:T(128)S(1)} %stack.39.scalars, bf16[8,128,256]{2,1,0:T(8,128)(2,1)} %copy-done.2, bf16[8,128,256]{2,1,0:T(8,128)(2,1)} %copy-done.33, ...), custom_call_target="tpu_custom_call" | custom-call | flops 4294967296 | bytes 19922944 | tf_op jit(solution)/shard_map/pallas_call | solution.py:264
  138.0 2.8 %collective-permute-done.32.away = bf16[8,128,256]{2,1,0:T(8,128)(2,1)S(1)} collective-permute-done((bf16[8,128,256]{2,1,0:T(8,128)(2,1)}, bf16[8,128,256]{2,1,0:T(8,128)(2,1)S(1)}, u32[]{:S(2)}, u32[]{:S(2)}) %collective-permute-start.32) | collective-permute-done | bytes 524320 | tf_op jit(solution)/shard_map/ppermute | solution.py:354
  154.3 2.8 %collective-permute-start.35 = (bf16[128,1024]{1,0:T(8,128)(2,1)}, bf16[128,1024]{1,0:T(8,128)(2,1)S(1)}, u32[]{:S(2)}, u32[]{:S(2)}) collective-permute-start(bf16[128,1024]{1,0:T(8,128)(2,1)} %get-tuple-element.78), channel_id=1, source_target_pairs={{0,2},{1,3},{2,0},{3,1},{4,6},{5,7},{6,4},{7,5},{8,10},{9,11},{10,... | collective-permute-start | bytes 786440 | tf_op jit(solution)/shard_map/ppermute | solution.py:358
  158.4 16.7 %collective-permute-done.35 = bf16[128,1024]{1,0:T(8,128)(2,1)S(1)} collective-permute-done((bf16[128,1024]{1,0:T(8,128)(2,1)}, bf16[128,1024]{1,0:T(8,128)(2,1)S(1)}, u32[]{:S(2)}, u32[]{:S(2)}) %collective-permute-start.35) | collective-permute-done | bytes 262176 | tf_op jit(solution)/shard_map/ppermute | solution.py:358
  175.2 3.7 %collective-permute-start.36 = (bf16[8,128,128]{2,1,0:T(8,128)(2,1)S(1)}, bf16[8,128,128]{2,1,0:T(8,128)(2,1)}, u32[]{:S(2)}, u32[]{:S(2)}) collective-permute-start(bf16[8,128,128]{2,1,0:T(8,128)(2,1)S(1)} %fusion.69), channel_id=1, source_target_pairs={{0,4},{1,5},{2,6},{3,7},{4,0},{5,1},{6,2},{7,3},{8,12},{9,13},{10,... | collective-permute-start | bytes 786440 | tf_op jit(solution)/shard_map/ppermute | solution.py:111
  178.9 4.5 %collective-permute-done.36 = bf16[8,128,128]{2,1,0:T(8,128)(2,1)} collective-permute-done((bf16[8,128,128]{2,1,0:T(8,128)(2,1)S(1)}, bf16[8,128,128]{2,1,0:T(8,128)(2,1)}, u32[]{:S(2)}, u32[]{:S(2)}) %collective-permute-start.36) | collective-permute-done | bytes 262176 | tf_op jit(solution)/shard_map/ppermute | solution.py:111
  186.2 2.9 %fusion.14 = bf16[128,4096]{1,0:T(8,128)(2,1)} fusion(f32[128,4096]{1,0:T(8,128)} %get-tuple-element.111, bf16[128,4096]{1,0:T(8,128)(2,1)S(1)} %shard_map.167), kind=kLoop, calls=%fused_computation.27 | loop fusion | flops 1572864 | bytes 4194304 | tf_op jit(solution)/shard_map/convert_element_type | solution.py:51
  190.9 4.2 %collective-permute-start.41 = (bf16[2,128,128]{2,1,0:T(8,128)(2,1)S(1)}, bf16[2,128,128]{2,1,0:T(8,128)(2,1)S(1)}, u32[]{:S(2)}, u32[]{:S(2)}) collective-permute-start(bf16[2,128,128]{2,1,0:T(8,128)(2,1)S(1)} %fusion.71), channel_id=1, source_target_pairs={{0,16},{1,17},{2,18},{3,19},{4,20},{5,21},{6,22},{7,23},{8,24},{9,... | collective-permute-start | bytes 196616 | tf_op jit(solution)/shard_map/ppermute | solution.py:111
  201.3 2.8 %add_convert_fusion = bf16[128,4096]{1,0:T(8,128)(2,1)} fusion(f32[128,4096]{1,0:T(8,128)} %get-tuple-element.70, bf16[128,1024]{1,0:T(8,128)(2,1)} %collective-permute-done.40, bf16[128,1024]{1,0:T(8,128)(2,1)S(1)} %copy-done.41, bf16[128,1024]{1,0:T(8,128)(2,1)S(1)} %copy-done.39, bf16[128,1024]{1,0:T(8,128)(2,1)S(1)} %copy-done.37), kind=kLoop, calls=%fused_computation.34 | loop fusion | flops 5242880 | bytes 4194304 | tf_op jit(solution)/shard_map/convert_element_type | solution.py:370
  (200 shorter events, 63.3 us)
Async XLA Ops:
  3.1 26.4 %collective-permute-start = (bf16[128,4096]{1,0:T(8,128)(2,1)}, bf16[128,4096]{1,0:T(8,128)(2,1)}, u32[]{:S(2)}, u32[]{:S(2)}) collective-permute-start(bf16[128,4096]{1,0:T(8,128)(2,1)} %cot_own), channel_id=1, source_target_pairs={{0,2},{1,3},{2,0},{3,1},{4,6},{5,7},{6,4},{7,5},{8,10},{9,11},{10,... | collective-permute-start | bytes 3145736 | tf_op jit(solution)/shard_map/ppermute | solution.py:329
  6.0 13.7 %collective-permute-start.2 = (bf16[64,4096]{1,0:T(8,128)(2,1)}, bf16[64,4096]{1,0:T(8,128)(2,1)}, u32[]{:S(2)}, u32[]{:S(2)}) collective-permute-start(bf16[64,4096]{1,0:T(8,128)(2,1)} %get-tuple-element.48.refs_0_), channel_id=1, source_target_pairs={{0,8},{1,9},{2,10},{3,11},{8,16},{9,17},{10,18},{11,19},{16,24},{1... | collective-permute-start | bytes 1572872 | tf_op jit(solution)/shard_map/ppermute | solution.py:336
  7.6 13.7 %collective-permute-start.3 = (bf16[64,4096]{1,0:T(8,128)(2,1)}, bf16[64,4096]{1,0:T(8,128)(2,1)}, u32[]{:S(2)}, u32[]{:S(2)}) collective-permute-start(bf16[64,4096]{1,0:T(8,128)(2,1)} %get-tuple-element.50.refs_2_), channel_id=1, source_target_pairs={{8,0},{9,1},{10,2},{11,3},{16,8},{17,9},{18,10},{19,11},{24,16},{2... | collective-permute-start | bytes 1572872 | tf_op jit(solution)/shard_map/ppermute | solution.py:336
  8.0 70.7 %collective-permute-start.1 = (bf16[128,4096]{1,0:T(8,128)(2,1)}, bf16[128,4096]{1,0:T(8,128)(2,1)}, u32[]{:S(2)}, u32[]{:S(2)}) collective-permute-start(bf16[128,4096]{1,0:T(8,128)(2,1)} %param.16), channel_id=1, source_target_pairs={{0,1},{1,0},{2,3},{3,2},{4,5},{5,4},{6,7},{7,6},{8,9},{9,8},{10,11... | collective-permute-start | bytes 3145736 | tf_op jit(solution)/shard_map/ppermute | solution.py:328
  19.7 16.5 %collective-permute-start.6 = (bf16[64,4096]{1,0:T(8,128)(2,1)}, bf16[64,4096]{1,0:T(8,128)(2,1)S(1)}, u32[]{:S(2)}, u32[]{:S(2)}) collective-permute-start(bf16[64,4096]{1,0:T(8,128)(2,1)} %collective-permute-done.2.refs_4_), channel_id=1, source_target_pairs={{0,8},{1,9},{2,10},{3,11},{8,16},{9,17},{10,18},{11,19},{16,24},{1... | collective-permute-start | bytes 1572872 | tf_op jit(solution)/shard_map/ppermute | solution.py:336
  21.3 16.5 %collective-permute-start.8 = (bf16[64,4096]{1,0:T(8,128)(2,1)}, bf16[64,4096]{1,0:T(8,128)(2,1)S(1)}, u32[]{:S(2)}, u32[]{:S(2)}) collective-permute-start(bf16[64,4096]{1,0:T(8,128)(2,1)} %collective-permute-done.3.refs_6_), channel_id=1, source_target_pairs={{8,0},{9,1},{10,2},{11,3},{16,8},{17,9},{18,10},{19,11},{24,16},{2... | collective-permute-start | bytes 1572872 | tf_op jit(solution)/shard_map/ppermute | solution.py:336
  29.5 27.5 %collective-permute-start.12 = (bf16[128,4096]{0,1:T(8,128)(2,1)S(1)}, bf16[128,4096]{0,1:T(8,128)(2,1)S(1)}, u32[]{:S(2)}, u32[]{:S(2)}) collective-permute-start(bf16[128,4096]{0,1:T(8,128)(2,1)S(1)} %fusion.11), channel_id=1, source_target_pairs={{0,1},{1,2},{2,3},{3,4},{4,5},{5,6},{6,7},{7,8},{8,9},{9,10},{10,1... | collective-permute-start | bytes 3145736 | tf_op jit(solution)/shard_map/ppermute | solution.py:331
  33.8 27.3 %collective-permute-start.4 = (bf16[64,4096]{1,0:T(8,128)(2,1)}, bf16[64,4096]{1,0:T(8,128)(2,1)S(1)}, u32[]{:S(2)}, u32[]{:S(2)}) collective-permute-start(bf16[64,4096]{1,0:T(8,128)(2,1)} %collective-permute-done.2.refs_4_), channel_id=1, source_target_pairs={{0,1},{1,0},{2,3},{3,2},{4,5},{5,4},{6,7},{7,6},{8,9},{9,8},{10,11... | collective-permute-start | bytes 1572872 | tf_op jit(solution)/shard_map/ppermute | solution.py:350
  36.2 13.9 %collective-permute-start.10 = (bf16[64,4096]{1,0:T(8,128)(2,1)S(1)}, bf16[64,4096]{1,0:T(8,128)(2,1)S(1)}, u32[]{:S(2)}, u32[]{:S(2)}) collective-permute-start(bf16[64,4096]{1,0:T(8,128)(2,1)S(1)} %collective-permute-done.6.refs_8_), channel_id=1, source_target_pairs={{0,8},{1,9},{2,10},{3,11},{8,16},{9,17},{10,18},{11,19},{16,24},{1... | collective-permute-start | bytes 1572872 | tf_op jit(solution)/shard_map/ppermute | solution.py:336
  37.8 19.2 %collective-permute-start.11 = (bf16[64,4096]{1,0:T(8,128)(2,1)S(1)}, bf16[64,4096]{1,0:T(8,128)(2,1)S(1)}, u32[]{:S(2)}, u32[]{:S(2)}) collective-permute-start(bf16[64,4096]{1,0:T(8,128)(2,1)S(1)} %collective-permute-done.8.refs_10_), channel_id=1, source_target_pairs={{8,0},{9,1},{10,2},{11,3},{16,8},{17,9},{18,10},{19,11},{24,16},{2... | collective-permute-start | bytes 1572872 | tf_op jit(solution)/shard_map/ppermute | solution.py:336
  57.0 14.7 %collective-permute-start.15 = (bf16[64,4096]{1,0:T(8,128)(2,1)S(1)}, bf16[64,4096]{1,0:T(8,128)(2,1)}, u32[]{:S(2)}, u32[]{:S(2)}) collective-permute-start(bf16[64,4096]{1,0:T(8,128)(2,1)S(1)} %collective-permute-done.10.refs_12_), channel_id=1, source_target_pairs={{0,8},{1,9},{2,10},{3,11},{8,16},{9,17},{10,18},{11,19},{16,24},{1... | collective-permute-start | bytes 1572872 | tf_op jit(solution)/shard_map/ppermute | solution.py:336
  57.0 14.7 %collective-permute-start.17 = (bf16[64,4096]{1,0:T(8,128)(2,1)S(1)}, bf16[64,4096]{1,0:T(8,128)(2,1)S(1)}, u32[]{:S(2)}, u32[]{:S(2)}) collective-permute-start(bf16[64,4096]{1,0:T(8,128)(2,1)S(1)} %collective-permute-done.11.refs_14_), channel_id=1, source_target_pairs={{8,0},{9,1},{10,2},{11,3},{16,8},{17,9},{18,10},{19,11},{24,16},{2... | collective-permute-start | bytes 1572872 | tf_op jit(solution)/shard_map/ppermute | solution.py:336
  61.1 17.6 %collective-permute-start.7 = (bf16[64,4096]{1,0:T(8,128)(2,1)S(1)}, bf16[64,4096]{1,0:T(8,128)(2,1)S(1)}, u32[]{:S(2)}, u32[]{:S(2)}) collective-permute-start(bf16[64,4096]{1,0:T(8,128)(2,1)S(1)} %collective-permute-done.6.refs_8_), channel_id=1, source_target_pairs={{0,1},{1,0},{2,3},{3,2},{4,5},{5,4},{6,7},{7,6},{8,9},{9,8},{10,11... | collective-permute-start | bytes 1572872 | tf_op jit(solution)/shard_map/ppermute | solution.py:350
  61.2 17.6 %collective-permute-start.9 = (bf16[64,4096]{1,0:T(8,128)(2,1)S(1)}, bf16[64,4096]{1,0:T(8,128)(2,1)S(1)}, u32[]{:S(2)}, u32[]{:S(2)}) collective-permute-start(bf16[64,4096]{1,0:T(8,128)(2,1)S(1)} %collective-permute-done.8.refs_10_), channel_id=1, source_target_pairs={{0,1},{1,0},{2,3},{3,2},{4,5},{5,4},{6,7},{7,6},{8,9},{9,8},{10,11... | collective-permute-start | bytes 1572872 | tf_op jit(solution)/shard_map/ppermute | solution.py:350
  71.7 13.6 %collective-permute-start.19 = (bf16[64,4096]{1,0:T(8,128)(2,1)}, bf16[64,4096]{1,0:T(8,128)(2,1)}, u32[]{:S(2)}, u32[]{:S(2)}) collective-permute-start(bf16[64,4096]{1,0:T(8,128)(2,1)} %collective-permute-done.15.refs_16_), channel_id=1, source_target_pairs={{0,8},{1,9},{2,10},{3,11},{8,16},{9,17},{10,18},{11,19},{16,24},{1... | collective-permute-start | bytes 1572872 | tf_op jit(solution)/shard_map/ppermute | solution.py:336
  71.7 15.1 %collective-permute-start.21 = (bf16[64,4096]{1,0:T(8,128)(2,1)S(1)}, bf16[64,4096]{1,0:T(8,128)(2,1)}, u32[]{:S(2)}, u32[]{:S(2)}) collective-permute-start(bf16[64,4096]{1,0:T(8,128)(2,1)S(1)} %collective-permute-done.17.refs_18_), channel_id=1, source_target_pairs={{8,0},{9,1},{10,2},{11,3},{16,8},{17,9},{18,10},{19,11},{24,16},{2... | collective-permute-start | bytes 1572872 | tf_op jit(solution)/shard_map/ppermute | solution.py:336
  78.9 13.2 %collective-permute-start.14 = (bf16[64,4096]{1,0:T(8,128)(2,1)S(1)}, bf16[64,4096]{1,0:T(8,128)(2,1)S(1)}, u32[]{:S(2)}, u32[]{:S(2)}) collective-permute-start(bf16[64,4096]{1,0:T(8,128)(2,1)S(1)} %collective-permute-done.11.refs_14_), channel_id=1, source_target_pairs={{0,1},{1,0},{2,3},{3,2},{4,5},{5,4},{6,7},{7,6},{8,9},{9,8},{10,11... | collective-permute-start | bytes 1572872 | tf_op jit(solution)/shard_map/ppermute | solution.py:350
  98.0 13.8 %collective-permute-start.28 = (bf16[64,4096]{1,0:T(8,128)(2,1)S(1)}, bf16[64,4096]{1,0:T(8,128)(2,1)}, u32[]{:S(2)}, u32[]{:S(2)}) collective-permute-start(bf16[64,4096]{1,0:T(8,128)(2,1)S(1)} %collective-permute-done.23.refs_24_), channel_id=1, source_target_pairs={{0,8},{1,9},{2,10},{3,11},{8,16},{9,17},{10,18},{11,19},{16,24},{1... | collective-permute-start | bytes 1572872 | tf_op jit(solution)/shard_map/ppermute | solution.py:336
  101.2 13.4 %collective-permute-start.22 = (bf16[64,4096]{1,0:T(8,128)(2,1)}, bf16[64,4096]{1,0:T(8,128)(2,1)S(1)}, u32[]{:S(2)}, u32[]{:S(2)}) collective-permute-start(bf16[64,4096]{1,0:T(8,128)(2,1)} %collective-permute-done.21.refs_22_), channel_id=1, source_target_pairs={{0,1},{1,0},{2,3},{3,2},{4,5},{5,4},{6,7},{7,6},{8,9},{9,8},{10,11... | collective-permute-start | bytes 1572872 | tf_op jit(solution)/shard_map/ppermute | solution.py:350
  101.2 13.4 %collective-permute-start.26 = (bf16[64,4096]{1,0:T(8,128)(2,1)S(1)}, bf16[64,4096]{1,0:T(8,128)(2,1)S(1)}, u32[]{:S(2)}, u32[]{:S(2)}) collective-permute-start(bf16[64,4096]{1,0:T(8,128)(2,1)S(1)} %collective-permute-done.23.refs_24_), channel_id=1, source_target_pairs={{0,1},{1,0},{2,3},{3,2},{4,5},{5,4},{6,7},{7,6},{8,9},{9,8},{10,11... | collective-permute-start | bytes 1572872 | tf_op jit(solution)/shard_map/ppermute | solution.py:350
  101.7 12.9 %collective-permute-start.27 = (bf16[64,4096]{1,0:T(8,128)(2,1)}, bf16[64,4096]{1,0:T(8,128)(2,1)S(1)}, u32[]{:S(2)}, u32[]{:S(2)}) collective-permute-start(bf16[64,4096]{1,0:T(8,128)(2,1)} %collective-permute-done.24.refs_26_), channel_id=1, source_target_pairs={{0,1},{1,0},{2,3},{3,2},{4,5},{5,4},{6,7},{7,6},{8,9},{9,8},{10,11... | collective-permute-start | bytes 1572872 | tf_op jit(solution)/shard_map/ppermute | solution.py:350
  126.7 14.1 %collective-permute-start.32 = (bf16[8,128,256]{2,1,0:T(8,128)(2,1)}, bf16[8,128,256]{2,1,0:T(8,128)(2,1)S(1)}, u32[]{:S(2)}, u32[]{:S(2)}) collective-permute-start(bf16[8,128,256]{2,1,0:T(8,128)(2,1)} %get-tuple-element.62), channel_id=1, source_target_pairs={{0,2},{1,3},{2,0},{3,1},{4,6},{5,7},{6,4},{7,5},{8,10},{9,11},{10,... | collective-permute-start | bytes 1572872 | tf_op jit(solution)/shard_map/ppermute | solution.py:354
  153.0 31.4 %collective-permute-start.37 = (bf16[128,4096]{0,1:T(8,128)(2,1)}, bf16[128,4096]{0,1:T(8,128)(2,1)}, u32[]{:S(2)}, u32[]{:S(2)}) collective-permute-start(bf16[128,4096]{0,1:T(8,128)(2,1)} %fusion.18), channel_id=1, source_target_pairs={{1,0},{2,1},{3,2},{4,3},{5,4},{6,5},{7,6},{8,7},{9,8},{10,9},{11,1... | collective-permute-start | bytes 3145736 | tf_op jit(solution)/shard_map/ppermute | solution.py:364
  154.3 20.9 %collective-permute-start.35 = (bf16[128,1024]{1,0:T(8,128)(2,1)}, bf16[128,1024]{1,0:T(8,128)(2,1)S(1)}, u32[]{:S(2)}, u32[]{:S(2)}) collective-permute-start(bf16[128,1024]{1,0:T(8,128)(2,1)} %get-tuple-element.78), channel_id=1, source_target_pairs={{0,2},{1,3},{2,0},{3,1},{4,6},{5,7},{6,4},{7,5},{8,10},{9,11},{10,... | collective-permute-start | bytes 786440 | tf_op jit(solution)/shard_map/ppermute | solution.py:358
  (67 other events, 695.4 us)

commit v5 on v4

--- a/solution.py
+++ b/solution.py
@@ -364,8 +364,8 @@
     ahead = send(across, perm=earlier)
     grads, across, out_away[0] = tie((grads, across, out_away[0]))
     taps_part = inverse_dft(table_now, times_conj(grads, data), scale)
-    guests = [out_away[1], ahead, out_away[2], out_away[3]]
-    taps_grad, (out_away[1], ahead, out_away[2], out_away[3]) = sum_over_ring(taps_part, nseq, place, guests)
+    guests = [(), (), (ahead, out_away[1]), ()]
+    taps_grad, (_, _, (ahead, out_away[1]), _) = sum_over_ring(taps_part, nseq, place, guests)
     taps_grad = taps_grad.T
     outputs = (out_own + jnp.concatenate(out_away, 1).astype(F32)).astype(BF16)
     grad_product = (back[length:] + ahead.astype(F32)).astype(BF16)

time: 205 us -> 198 us (0.966)
  waiting for transfers between devices: 90 us -> 81.7 us
  starting transfers between devices: 39.5 us -> 45.5 us
  other arithmetic: 12.8 us -> 8.92 us
    ppermute x4, waiting for transfers between devices: 16.7 us -> 5.87 us  [on_ring(): out_away = [send(chunk, perm=swap_pair) for chunk in out_away]]
    ppermute x4, starting transfers between devices: 3.09 us -> 13.5 us  [on_ring(): out_away = [send(chunk, perm=swap_pair) for chunk in out_away]]
    ppermute x4, starting transfers between devices: 11.3 us -> 6.98 us  [halve(): away = lax.ppermute(away, 'seq', [(i, i ^ bit) for i in range(nseq)])]
    ppermute x1, waiting for transfers between devices: 0.01 us -> 2.78 us  [sum_over_ring(): part = kept + lax.ppermute(away, 'seq', [(i, i ^ 1) for i in range(nseq)])]
    unnamed x101 -> x97, local copies, waits for them, and re-layouts: 11 us -> 10.3 us
  transfers between devices with their start and end apart: 43 -> 43, of which waited for: 15 -> 17; matrix products, arithmetic and copies ran while one was open for 19% -> 17% of each run, Pallas kernels for 6% -> 6%
where the time goes in v5:
time: 198 us
  waiting for transfers between devices  81.7 us (41%)
  starting transfers between devices  45.5 us (23%)
  Pallas kernels  22.3 us (11%)
  matrix products  21.3 us (11%)
  local copies, waits for them, and re-layouts  15.7 us (8%)
  other arithmetic  8.92 us (5%)
  between operations  2.68 us (1%)
    ppermute x14, waiting for transfers between devices, on_ring(): first, second = (send(first, perm=onward), send(second, perm=behind))  57.6 us
    ppermute x14, starting transfers between devices, on_ring(): first, second = (send(first, perm=onward), send(second, perm=behind))  13.9 us
    ppermute x4, starting transfers between devices, on_ring(): out_away = [send(chunk, perm=swap_pair) for chunk in out_away]  13.5 us
    dot_general x6, matrix products, inverse_dft(): lax.dot_general(table, spectrum, (((0,), (0,)), ((), ())), precision=lax....  11.3 us
    pallas_call x1, Pallas kernels, output_of(): pl.pallas_call(functools.partial(output_kernel, size), out_shape=(pltpu.H...  11.2 us
    pallas_call x1, Pallas kernels, grad_of_gated(): pl.pallas_call(functools.partial(grad_kernel, size), out_shape=(jax.Shape...  10.5 us
    unnamed x97, local copies, waits for them, and re-layouts  10.3 us
    ppermute x4, starting transfers between devices, halve(): away = lax.ppermute(away, 'seq', [(i, i ^ bit) for i in range(nseq)])  6.98 us
  transfers between devices with their start and end apart: 43, of which 17 were waited for; matrix products, arithmetic and copies ran while one was open for 17% of the time, Pallas kernels for 6%

profile of v5, /device:TPU:0, one launch (start us, length us, event | category | flops | bytes accessed | tf_op | source)
XLA Modules:
  0.0 198.1 jit_solution(1355956296375477171)
XLA Ops:
  3.1 2.9 %collective-permute-start = (bf16[128,4096]{1,0:T(8,128)(2,1)}, bf16[128,4096]{1,0:T(8,128)(2,1)}, u32[]{:S(2)}, u32[]{:S(2)}) collective-permute-start(bf16[128,4096]{1,0:T(8,128)(2,1)} %cot_own), channel_id=1, source_target_pairs={{0,2},{1,3},{2,0},{3,1},{4,6},{5,7},{6,4},{7,5},{8,10},{9,11},{10,... | collective-permute-start | bytes 3145736 | tf_op jit(solution)/shard_map/ppermute | solution.py:329
  8.7 2.6 %copy.48 = bf16[128,4096]{0,1:T(8,128)(2,1)} copy(bf16[128,4096]{1,0:T(8,128)(2,1)} %param.15) | data formatting | bytes 2097152 | tf_op args[2]
  12.9 6.8 %collective-permute-done.2.refs_4_ = bf16[64,4096]{1,0:T(8,128)(2,1)} collective-permute-done((bf16[64,4096]{1,0:T(8,128)(2,1)}, bf16[64,4096]{1,0:T(8,128)(2,1)}, u32[]{:S(2)}, u32[]{:S(2)}) %collective-permute-start.2) | collective-permute-done | bytes 524320 | tf_op jit(solution)/shard_map/ppermute | solution.py:336
  21.8 2.7 %fusion.77 = f32[256,4096]{1,0:T(8,128)} fusion(bf16[256,128]{1,0:T(8,128)(2,1)S(1)} %copy-done.33, bf16[128,4096]{0,1:T(8,128)(2,1)S(1)} %bitcast.61), kind=kOutput, calls=%fused_computation.100 | convolution fusion | flops 268435456 | bytes 5308416 | tf_op jit(solution)/shard_map/dot_general | solution.py:26
  26.4 3.1 %collective-permute-done.cot_away = bf16[128,4096]{1,0:T(8,128)(2,1)} collective-permute-done((bf16[128,4096]{1,0:T(8,128)(2,1)}, bf16[128,4096]{1,0:T(8,128)(2,1)}, u32[]{:S(2)}, u32[]{:S(2)}) %collective-permute-start) | collective-permute-done | bytes 1048608 | tf_op jit(solution)/shard_map/ppermute | solution.py:329
  30.9 2.9 %convolution_add_fusion.4 = f32[256,4096]{1,0:T(8,128)S(1)} fusion(f32[256,4096]{1,0:T(8,128)} %fusion.77, bf16[256,128]{1,0:T(8,128)(2,1)S(1)} %copy-done.32, bf16[128,4096]{0,1:T(8,128)(2,1)S(1)} %bitcast.60), kind=kOutput, calls=%fused_computation.9 | convolution fusion | flops 269484032 | bytes 9502720 | tf_op jit(solution)/shard_map/dot_general | solution.py:27
  39.7 10.4 %collective-permute-done.10.refs_12_ = bf16[64,4096]{1,0:T(8,128)(2,1)S(1)} collective-permute-done((bf16[64,4096]{1,0:T(8,128)(2,1)S(1)}, bf16[64,4096]{1,0:T(8,128)(2,1)S(1)}, u32[]{:S(2)}, u32[]{:S(2)}) %collective-permute-start.10) | collective-permute-done | bytes 524320 | tf_op jit(solution)/shard_map/ppermute | solution.py:336
  50.2 6.9 %collective-permute-done.11.refs_14_ = bf16[64,4096]{1,0:T(8,128)(2,1)S(1)} collective-permute-done((bf16[64,4096]{1,0:T(8,128)(2,1)S(1)}, bf16[64,4096]{1,0:T(8,128)(2,1)S(1)}, u32[]{:S(2)}, u32[]{:S(2)}) %collective-permute-start.11) | collective-permute-done | bytes 524320 | tf_op jit(solution)/shard_map/ppermute | solution.py:336
  57.0 2.5 %collective-permute-start.17 = (bf16[64,4096]{1,0:T(8,128)(2,1)S(1)}, bf16[64,4096]{1,0:T(8,128)(2,1)S(1)}, u32[]{:S(2)}, u32[]{:S(2)}) collective-permute-start(bf16[64,4096]{1,0:T(8,128)(2,1)S(1)} %collective-permute-done.11.refs_14_), channel_id=1, source_target_pairs={{8,0},{9,1},{10,2},{11,3},{16,8},{17,9},{18,10},{19,11},{24,16},{2... | collective-permute-start | bytes 1572872 | tf_op jit(solution)/shard_map/ppermute | solution.py:336
  61.8 9.9 %collective-permute-done.15.refs_16_ = bf16[64,4096]{1,0:T(8,128)(2,1)} collective-permute-done((bf16[64,4096]{1,0:T(8,128)(2,1)S(1)}, bf16[64,4096]{1,0:T(8,128)(2,1)}, u32[]{:S(2)}, u32[]{:S(2)}) %collective-permute-start.15) | collective-permute-done | bytes 524320 | tf_op jit(solution)/shard_map/ppermute | solution.py:336
  75.1 2.7 %fusion.12 = (bf16[128,4096]{1,0:T(8,128)(2,1)S(1)}, f32[128,4096]{1,0:T(8,128)}) fusion(bf16[128,4096]{1,0:T(8,128)(2,1)S(1)} %copy-done.9, f32[4096,128]{0,1:T(8,128)S(1)} %fusion.36, f32[128,128]{1,0:T(8,128)S(1)} %copy-done.35, f32[256,4096]{1,0:T(8,128)S(1)} %fusion.4, f32[256,4096]{1,0:T(8,128)S(1)} %convolution_add_fusion.4), kind=kOutput, calls=%fused_computation.25 | convolution fusion | flops 407896064 | bytes 14745600 | tf_op jit(solution)/shard_map/dot_general | solution.py:44
  79.4 5.9 %collective-permute-done.19.refs_20_ = bf16[64,4096]{1,0:T(8,128)(2,1)} collective-permute-done((bf16[64,4096]{1,0:T(8,128)(2,1)}, bf16[64,4096]{1,0:T(8,128)(2,1)}, u32[]{:S(2)}, u32[]{:S(2)}) %collective-permute-start.19) | collective-permute-done | bytes 524320 | tf_op jit(solution)/shard_map/ppermute | solution.py:336
  87.4 4.1 %collective-permute-done.25.gated_away = bf16[8,128,256]{2,1,0:T(8,128)(2,1)S(1)} collective-permute-done((bf16[8,128,256]{2,1,0:T(8,128)(2,1)S(1)}, bf16[8,128,256]{2,1,0:T(8,128)(2,1)S(1)}, u32[]{:S(2)}, u32[]{:S(2)}) %collective-permute-start.25) | collective-permute-done | bytes 524320 | tf_op jit(solution)/shard_map/ppermute | solution.py:347
  92.2 5.8 %collective-permute-done.23.refs_24_ = bf16[64,4096]{1,0:T(8,128)(2,1)S(1)} collective-permute-done((bf16[64,4096]{1,0:T(8,128)(2,1)}, bf16[64,4096]{1,0:T(8,128)(2,1)S(1)}, u32[]{:S(2)}, u32[]{:S(2)}) %collective-permute-start.23) | collective-permute-done | bytes 524320 | tf_op jit(solution)/shard_map/ppermute | solution.py:336
  101.8 10.0 %collective-permute-done.28.refs_28_ = bf16[64,4096]{1,0:T(8,128)(2,1)} collective-permute-done((bf16[64,4096]{1,0:T(8,128)(2,1)S(1)}, bf16[64,4096]{1,0:T(8,128)(2,1)}, u32[]{:S(2)}, u32[]{:S(2)}) %collective-permute-start.28) | collective-permute-done | bytes 524320 | tf_op jit(solution)/shard_map/ppermute | solution.py:336
  116.2 10.5 %shard_map.165 = (bf16[8,128,256]{2,1,0:T(8,128)(2,1)S(1)}, bf16[8,128,256]{2,1,0:T(8,128)(2,1)}) custom-call(s32[9]{0:T(128)S(1)} %stack.39.scalars, bf16[128,4096]{1,0:T(8,128)(2,1)} %cot_own, bf16[128,4096]{1,0:T(8,128)(2,1)} %collective-permute-done.cot_away, bf16[64,4096]{1,0:T(8,128)(2,1)} %get-tuple-element.45.refs_0_, ...), custom_call_target="tpu_custom_call" | custom-call | flops 4294967296 | bytes 18874368 | tf_op jit(solution)/shard_map/pallas_call | solution.py:234
  126.8 11.2 %shard_map.166 = (f32[128,4096]{1,0:T(8,128)}, bf16[128,1024]{1,0:T(8,128)(2,1)}, bf16[128,1024]{1,0:T(8,128)(2,1)}, bf16[128,1024]{1,0:T(8,128)(2,1)}, bf16[128,1024]{1,0:T(8,128)(2,1)}) custom-call(s32[9]{0:T(128)S(1)} %stack.39.scalars, bf16[8,128,256]{2,1,0:T(8,128)(2,1)} %copy-done.2, bf16[8,128,256]{2,1,0:T(8,128)(2,1)} %copy-done.34, ...), custom_call_target="tpu_custom_call" | custom-call | flops 4294967296 | bytes 19922944 | tf_op jit(solution)/shard_map/pallas_call | solution.py:264
  138.0 2.8 %collective-permute-done.32.away = bf16[8,128,256]{2,1,0:T(8,128)(2,1)S(1)} collective-permute-done((bf16[8,128,256]{2,1,0:T(8,128)(2,1)}, bf16[8,128,256]{2,1,0:T(8,128)(2,1)S(1)}, u32[]{:S(2)}, u32[]{:S(2)}) %collective-permute-start.32) | collective-permute-done | bytes 524320 | tf_op jit(solution)/shard_map/ppermute | solution.py:354
  153.0 2.8 %collective-permute-done.34 = f32[2,8,128,128]{3,2,1,0:T(8,128)} collective-permute-done((f32[2,8,128,128]{3,2,1,0:T(8,128)S(1)}, f32[2,8,128,128]{3,2,1,0:T(8,128)}, u32[]{:S(2)}, u32[]{:S(2)}) %collective-permute-start.34) | collective-permute-done | bytes 1048608 | tf_op jit(solution)/shard_map/ppermute | solution.py:115
  157.2 2.8 %collective-permute-start.35 = (bf16[8,128,128]{2,1,0:T(8,128)(2,1)S(1)}, bf16[8,128,128]{2,1,0:T(8,128)(2,1)S(1)}, u32[]{:S(2)}, u32[]{:S(2)}) collective-permute-start(bf16[8,128,128]{2,1,0:T(8,128)(2,1)S(1)} %fusion.69), channel_id=1, source_target_pairs={{0,4},{1,5},{2,6},{3,7},{4,0},{5,1},{6,2},{7,3},{8,12},{9,13},{10,... | collective-permute-start | bytes 786440 | tf_op jit(solution)/shard_map/ppermute | solution.py:111
  163.4 3.2 %collective-permute-done.35 = bf16[8,128,128]{2,1,0:T(8,128)(2,1)S(1)} collective-permute-done((bf16[8,128,128]{2,1,0:T(8,128)(2,1)S(1)}, bf16[8,128,128]{2,1,0:T(8,128)(2,1)S(1)}, u32[]{:S(2)}, u32[]{:S(2)}) %collective-permute-start.35) | collective-permute-done | bytes 262176 | tf_op jit(solution)/shard_map/ppermute | solution.py:111
  168.3 2.9 %fusion.14 = bf16[128,4096]{1,0:T(8,128)(2,1)} fusion(f32[128,4096]{1,0:T(8,128)} %get-tuple-element.105, bf16[128,4096]{1,0:T(8,128)(2,1)S(1)} %shard_map.167), kind=kLoop, calls=%fused_computation.27 | loop fusion | flops 1572864 | bytes 4194304 | tf_op jit(solution)/shard_map/convert_element_type | solution.py:51
  171.2 11.0 %collective-permute-start.39 = (bf16[128,1024]{1,0:T(8,128)(2,1)}, bf16[128,1024]{1,0:T(8,128)(2,1)S(1)}, u32[]{:S(2)}, u32[]{:S(2)}) collective-permute-start(bf16[128,1024]{1,0:T(8,128)(2,1)} %get-tuple-element.77), channel_id=1, source_target_pairs={{0,2},{1,3},{2,0},{3,1},{4,6},{5,7},{6,4},{7,5},{8,10},{9,11},{10,... | collective-permute-start | bytes 786440 | tf_op jit(solution)/shard_map/ppermute | solution.py:358
  182.3 5.3 %collective-permute-done.38 = bf16[128,1024]{1,0:T(8,128)(2,1)S(1)} collective-permute-done((bf16[128,1024]{1,0:T(8,128)(2,1)}, bf16[128,1024]{1,0:T(8,128)(2,1)S(1)}, u32[]{:S(2)}, u32[]{:S(2)}) %collective-permute-start.38) | collective-permute-done | bytes 262176 | tf_op jit(solution)/shard_map/ppermute | solution.py:358
  (196 shorter events, 63.6 us)
Async XLA Ops:
  3.1 26.4 %collective-permute-start = (bf16[128,4096]{1,0:T(8,128)(2,1)}, bf16[128,4096]{1,0:T(8,128)(2,1)}, u32[]{:S(2)}, u32[]{:S(2)}) collective-permute-start(bf16[128,4096]{1,0:T(8,128)(2,1)} %cot_own), channel_id=1, source_target_pairs={{0,2},{1,3},{2,0},{3,1},{4,6},{5,7},{6,4},{7,5},{8,10},{9,11},{10,... | collective-permute-start | bytes 3145736 | tf_op jit(solution)/shard_map/ppermute | solution.py:329
  6.0 13.7 %collective-permute-start.2 = (bf16[64,4096]{1,0:T(8,128)(2,1)}, bf16[64,4096]{1,0:T(8,128)(2,1)}, u32[]{:S(2)}, u32[]{:S(2)}) collective-permute-start(bf16[64,4096]{1,0:T(8,128)(2,1)} %get-tuple-element.45.refs_0_), channel_id=1, source_target_pairs={{0,8},{1,9},{2,10},{3,11},{8,16},{9,17},{10,18},{11,19},{16,24},{1... | collective-permute-start | bytes 1572872 | tf_op jit(solution)/shard_map/ppermute | solution.py:336
  7.6 13.7 %collective-permute-start.3 = (bf16[64,4096]{1,0:T(8,128)(2,1)}, bf16[64,4096]{1,0:T(8,128)(2,1)}, u32[]{:S(2)}, u32[]{:S(2)}) collective-permute-start(bf16[64,4096]{1,0:T(8,128)(2,1)} %get-tuple-element.47.refs_2_), channel_id=1, source_target_pairs={{8,0},{9,1},{10,2},{11,3},{16,8},{17,9},{18,10},{19,11},{24,16},{2... | collective-permute-start | bytes 1572872 | tf_op jit(solution)/shard_map/ppermute | solution.py:336
  8.1 70.7 %collective-permute-start.1 = (bf16[128,4096]{1,0:T(8,128)(2,1)}, bf16[128,4096]{1,0:T(8,128)(2,1)}, u32[]{:S(2)}, u32[]{:S(2)}) collective-permute-start(bf16[128,4096]{1,0:T(8,128)(2,1)} %param.16), channel_id=1, source_target_pairs={{0,1},{1,0},{2,3},{3,2},{4,5},{5,4},{6,7},{7,6},{8,9},{9,8},{10,11... | collective-permute-start | bytes 3145736 | tf_op jit(solution)/shard_map/ppermute | solution.py:328
  19.7 16.5 %collective-permute-start.6 = (bf16[64,4096]{1,0:T(8,128)(2,1)}, bf16[64,4096]{1,0:T(8,128)(2,1)S(1)}, u32[]{:S(2)}, u32[]{:S(2)}) collective-permute-start(bf16[64,4096]{1,0:T(8,128)(2,1)} %collective-permute-done.2.refs_4_), channel_id=1, source_target_pairs={{0,8},{1,9},{2,10},{3,11},{8,16},{9,17},{10,18},{11,19},{16,24},{1... | collective-permute-start | bytes 1572872 | tf_op jit(solution)/shard_map/ppermute | solution.py:336
  21.3 16.5 %collective-permute-start.8 = (bf16[64,4096]{1,0:T(8,128)(2,1)}, bf16[64,4096]{1,0:T(8,128)(2,1)S(1)}, u32[]{:S(2)}, u32[]{:S(2)}) collective-permute-start(bf16[64,4096]{1,0:T(8,128)(2,1)} %collective-permute-done.3.refs_6_), channel_id=1, source_target_pairs={{8,0},{9,1},{10,2},{11,3},{16,8},{17,9},{18,10},{19,11},{24,16},{2... | collective-permute-start | bytes 1572872 | tf_op jit(solution)/shard_map/ppermute | solution.py:336
  29.5 27.5 %collective-permute-start.12 = (bf16[128,4096]{0,1:T(8,128)(2,1)S(1)}, bf16[128,4096]{0,1:T(8,128)(2,1)S(1)}, u32[]{:S(2)}, u32[]{:S(2)}) collective-permute-start(bf16[128,4096]{0,1:T(8,128)(2,1)S(1)} %fusion.11), channel_id=1, source_target_pairs={{0,1},{1,2},{2,3},{3,4},{4,5},{5,6},{6,7},{7,8},{8,9},{9,10},{10,1... | collective-permute-start | bytes 3145736 | tf_op jit(solution)/shard_map/ppermute | solution.py:331
  33.8 27.3 %collective-permute-start.4 = (bf16[64,4096]{1,0:T(8,128)(2,1)}, bf16[64,4096]{1,0:T(8,128)(2,1)S(1)}, u32[]{:S(2)}, u32[]{:S(2)}) collective-permute-start(bf16[64,4096]{1,0:T(8,128)(2,1)} %collective-permute-done.2.refs_4_), channel_id=1, source_target_pairs={{0,1},{1,0},{2,3},{3,2},{4,5},{5,4},{6,7},{7,6},{8,9},{9,8},{10,11... | collective-permute-start | bytes 1572872 | tf_op jit(solution)/shard_map/ppermute | solution.py:350
  36.3 13.9 %collective-permute-start.10 = (bf16[64,4096]{1,0:T(8,128)(2,1)S(1)}, bf16[64,4096]{1,0:T(8,128)(2,1)S(1)}, u32[]{:S(2)}, u32[]{:S(2)}) collective-permute-start(bf16[64,4096]{1,0:T(8,128)(2,1)S(1)} %collective-permute-done.6.refs_8_), channel_id=1, source_target_pairs={{0,8},{1,9},{2,10},{3,11},{8,16},{9,17},{10,18},{11,19},{16,24},{1... | collective-permute-start | bytes 1572872 | tf_op jit(solution)/shard_map/ppermute | solution.py:336
  37.8 19.2 %collective-permute-start.11 = (bf16[64,4096]{1,0:T(8,128)(2,1)S(1)}, bf16[64,4096]{1,0:T(8,128)(2,1)S(1)}, u32[]{:S(2)}, u32[]{:S(2)}) collective-permute-start(bf16[64,4096]{1,0:T(8,128)(2,1)S(1)} %collective-permute-done.8.refs_10_), channel_id=1, source_target_pairs={{8,0},{9,1},{10,2},{11,3},{16,8},{17,9},{18,10},{19,11},{24,16},{2... | collective-permute-start | bytes 1572872 | tf_op jit(solution)/shard_map/ppermute | solution.py:336
  57.0 14.7 %collective-permute-start.15 = (bf16[64,4096]{1,0:T(8,128)(2,1)S(1)}, bf16[64,4096]{1,0:T(8,128)(2,1)}, u32[]{:S(2)}, u32[]{:S(2)}) collective-permute-start(bf16[64,4096]{1,0:T(8,128)(2,1)S(1)} %collective-permute-done.10.refs_12_), channel_id=1, source_target_pairs={{0,8},{1,9},{2,10},{3,11},{8,16},{9,17},{10,18},{11,19},{16,24},{1... | collective-permute-start | bytes 1572872 | tf_op jit(solution)/shard_map/ppermute | solution.py:336
  57.0 14.7 %collective-permute-start.17 = (bf16[64,4096]{1,0:T(8,128)(2,1)S(1)}, bf16[64,4096]{1,0:T(8,128)(2,1)S(1)}, u32[]{:S(2)}, u32[]{:S(2)}) collective-permute-start(bf16[64,4096]{1,0:T(8,128)(2,1)S(1)} %collective-permute-done.11.refs_14_), channel_id=1, source_target_pairs={{8,0},{9,1},{10,2},{11,3},{16,8},{17,9},{18,10},{19,11},{24,16},{2... | collective-permute-start | bytes 1572872 | tf_op jit(solution)/shard_map/ppermute | solution.py:336
  61.1 17.6 %collective-permute-start.7 = (bf16[64,4096]{1,0:T(8,128)(2,1)S(1)}, bf16[64,4096]{1,0:T(8,128)(2,1)S(1)}, u32[]{:S(2)}, u32[]{:S(2)}) collective-permute-start(bf16[64,4096]{1,0:T(8,128)(2,1)S(1)} %collective-permute-done.6.refs_8_), channel_id=1, source_target_pairs={{0,1},{1,0},{2,3},{3,2},{4,5},{5,4},{6,7},{7,6},{8,9},{9,8},{10,11... | collective-permute-start | bytes 1572872 | tf_op jit(solution)/shard_map/ppermute | solution.py:350
  61.3 17.6 %collective-permute-start.9 = (bf16[64,4096]{1,0:T(8,128)(2,1)S(1)}, bf16[64,4096]{1,0:T(8,128)(2,1)S(1)}, u32[]{:S(2)}, u32[]{:S(2)}) collective-permute-start(bf16[64,4096]{1,0:T(8,128)(2,1)S(1)} %collective-permute-done.8.refs_10_), channel_id=1, source_target_pairs={{0,1},{1,0},{2,3},{3,2},{4,5},{5,4},{6,7},{7,6},{8,9},{9,8},{10,11... | collective-permute-start | bytes 1572872 | tf_op jit(solution)/shard_map/ppermute | solution.py:350
  71.7 13.6 %collective-permute-start.19 = (bf16[64,4096]{1,0:T(8,128)(2,1)}, bf16[64,4096]{1,0:T(8,128)(2,1)}, u32[]{:S(2)}, u32[]{:S(2)}) collective-permute-start(bf16[64,4096]{1,0:T(8,128)(2,1)} %collective-permute-done.15.refs_16_), channel_id=1, source_target_pairs={{0,8},{1,9},{2,10},{3,11},{8,16},{9,17},{10,18},{11,19},{16,24},{1... | collective-permute-start | bytes 1572872 | tf_op jit(solution)/shard_map/ppermute | solution.py:336
  71.7 15.1 %collective-permute-start.21 = (bf16[64,4096]{1,0:T(8,128)(2,1)S(1)}, bf16[64,4096]{1,0:T(8,128)(2,1)}, u32[]{:S(2)}, u32[]{:S(2)}) collective-permute-start(bf16[64,4096]{1,0:T(8,128)(2,1)S(1)} %collective-permute-done.17.refs_18_), channel_id=1, source_target_pairs={{8,0},{9,1},{10,2},{11,3},{16,8},{17,9},{18,10},{19,11},{24,16},{2... | collective-permute-start | bytes 1572872 | tf_op jit(solution)/shard_map/ppermute | solution.py:336
  98.0 13.8 %collective-permute-start.28 = (bf16[64,4096]{1,0:T(8,128)(2,1)S(1)}, bf16[64,4096]{1,0:T(8,128)(2,1)}, u32[]{:S(2)}, u32[]{:S(2)}) collective-permute-start(bf16[64,4096]{1,0:T(8,128)(2,1)S(1)} %collective-permute-done.23.refs_24_), channel_id=1, source_target_pairs={{0,8},{1,9},{2,10},{3,11},{8,16},{9,17},{10,18},{11,19},{16,24},{1... | collective-permute-start | bytes 1572872 | tf_op jit(solution)/shard_map/ppermute | solution.py:336
  101.2 13.4 %collective-permute-start.22 = (bf16[64,4096]{1,0:T(8,128)(2,1)}, bf16[64,4096]{1,0:T(8,128)(2,1)S(1)}, u32[]{:S(2)}, u32[]{:S(2)}) collective-permute-start(bf16[64,4096]{1,0:T(8,128)(2,1)} %collective-permute-done.21.refs_22_), channel_id=1, source_target_pairs={{0,1},{1,0},{2,3},{3,2},{4,5},{5,4},{6,7},{7,6},{8,9},{9,8},{10,11... | collective-permute-start | bytes 1572872 | tf_op jit(solution)/shard_map/ppermute | solution.py:350
  101.3 13.3 %collective-permute-start.26 = (bf16[64,4096]{1,0:T(8,128)(2,1)S(1)}, bf16[64,4096]{1,0:T(8,128)(2,1)S(1)}, u32[]{:S(2)}, u32[]{:S(2)}) collective-permute-start(bf16[64,4096]{1,0:T(8,128)(2,1)S(1)} %collective-permute-done.23.refs_24_), channel_id=1, source_target_pairs={{0,1},{1,0},{2,3},{3,2},{4,5},{5,4},{6,7},{7,6},{8,9},{9,8},{10,11... | collective-permute-start | bytes 1572872 | tf_op jit(solution)/shard_map/ppermute | solution.py:350
  126.7 14.1 %collective-permute-start.32 = (bf16[8,128,256]{2,1,0:T(8,128)(2,1)}, bf16[8,128,256]{2,1,0:T(8,128)(2,1)S(1)}, u32[]{:S(2)}, u32[]{:S(2)}) collective-permute-start(bf16[8,128,256]{2,1,0:T(8,128)(2,1)} %get-tuple-element.59), channel_id=1, source_target_pairs={{0,2},{1,3},{2,0},{3,1},{4,6},{5,7},{6,4},{7,5},{8,10},{9,11},{10,... | collective-permute-start | bytes 1572872 | tf_op jit(solution)/shard_map/ppermute | solution.py:354
  160.0 27.6 %collective-permute-start.37 = (bf16[128,4096]{0,1:T(8,128)(2,1)}, bf16[128,4096]{0,1:T(8,128)(2,1)S(1)}, u32[]{:S(2)}, u32[]{:S(2)}) collective-permute-start(bf16[128,4096]{0,1:T(8,128)(2,1)} %fusion.18), channel_id=1, source_target_pairs={{1,0},{2,1},{3,2},{4,3},{5,4},{6,5},{7,6},{8,7},{9,8},{10,9},{11,1... | collective-permute-start | bytes 3145736 | tf_op jit(solution)/shard_map/ppermute | solution.py:364
  161.2 26.3 %collective-permute-start.38 = (bf16[128,1024]{1,0:T(8,128)(2,1)}, bf16[128,1024]{1,0:T(8,128)(2,1)S(1)}, u32[]{:S(2)}, u32[]{:S(2)}) collective-permute-start(bf16[128,1024]{1,0:T(8,128)(2,1)} %get-tuple-element.75), channel_id=1, source_target_pairs={{0,2},{1,3},{2,0},{3,1},{4,6},{5,7},{6,4},{7,5},{8,10},{9,11},{10,... | collective-permute-start | bytes 786440 | tf_op jit(solution)/shard_map/ppermute | solution.py:358
  166.7 15.6 %collective-permute-start.36 = (bf16[4,128,128]{2,1,0:T(8,128)(2,1)S(1)}, bf16[4,128,128]{2,1,0:T(8,128)(2,1)S(1)}, u32[]{:S(2)}, u32[]{:S(2)}) collective-permute-start(bf16[4,128,128]{2,1,0:T(8,128)(2,1)S(1)} %fusion.70), channel_id=1, source_target_pairs={{0,8},{1,9},{2,10},{3,11},{4,12},{5,13},{6,14},{7,15},{8,0},{9,1},... | collective-permute-start | bytes 393224 | tf_op jit(solution)/shard_map/ppermute | solution.py:111
  171.2 21.7 %collective-permute-start.39 = (bf16[128,1024]{1,0:T(8,128)(2,1)}, bf16[128,1024]{1,0:T(8,128)(2,1)S(1)}, u32[]{:S(2)}, u32[]{:S(2)}) collective-permute-start(bf16[128,1024]{1,0:T(8,128)(2,1)} %get-tuple-element.77), channel_id=1, source_target_pairs={{0,2},{1,3},{2,0},{3,1},{4,6},{5,7},{6,4},{7,5},{8,10},{9,11},{10,... | collective-permute-start | bytes 786440 | tf_op jit(solution)/shard_map/ppermute | solution.py:358
  (65 other events, 739.0 us)

commit v6 on v0

--- a/solution.py
+++ b/solution.py
@@ -189,7 +189,7 @@
     rows, feats = cot_own.shape
     size, _, width = gated_own.shape
     depth = pieces[0].shape[0]
-    tile = min(512, feats)
+    tile = min(1024, feats)
     block = pl.BlockSpec((rows, tile), lambda j, s: (0, j))
     whole = pl.BlockSpec(gated_own.shape, lambda j, s: (0, 0, 0))
     return pl.pallas_call(
@@ -299,6 +299,7 @@
     back = inverse_dft(table, times_conj(grads, filt), scale)
     across = jnp.where(linked, back[:length], 0.0).astype(BF16)
     ahead = send(across, perm=earlier)
+    grads, across = tie((grads, across))
     taps_part = inverse_dft(table_now, times_conj(grads, data), scale)
     taps_grad = sum_over_ring(taps_part, nseq, place).T
     outputs = (out_own + out_away.astype(F32)).astype(BF16)

time: 196 us -> 207 us (1.056)
  waiting for transfers between devices: 90.1 us -> 98.5 us
  other arithmetic: 6.18 us -> 10.3 us
  matrix products: 24.8 us -> 21.2 us
  starting transfers between devices: 38.4 us -> 40.6 us
    ppermute x1, waiting for transfers between devices: 0.01 us -> 10.6 us  [on_ring(): out_away = send(out_away, perm=swap_pair)]
    ppermute x4, waiting for transfers between devices: 18.7 us -> 13.4 us  [halve(): away = lax.ppermute(away, 'seq', [(i, i ^ bit) for i in range(nseq)])]
    dot_general x6, matrix products: 14.8 us -> 11.2 us  [inverse_dft(): lax.dot_general(table, spectrum, (((0,), (0,)), ((), ())), precision=lax....]
    ppermute x1, waiting for transfers between devices: 0.01 us -> 3 us  [sum_over_ring(): part = kept + lax.ppermute(away, 'seq', [(i, i ^ 1) for i in range(nseq)])]
    ppermute x4, starting transfers between devices: 6.51 us -> 8.84 us  [halve(): away = lax.ppermute(away, 'seq', [(i, i ^ bit) for i in range(nseq)])]
    unnamed x97 -> x95, local copies, waits for them, and re-layouts: 12.2 us -> 12.4 us
  transfers between devices with their start and end apart: 40 -> 40, of which waited for: 16 -> 16; matrix products, arithmetic and copies ran while one was open for 19% -> 15% of each run, Pallas kernels for 0% -> 0%
where the time goes in v6:
time: 207 us
  waiting for transfers between devices  98.5 us (48%)
  starting transfers between devices  40.6 us (20%)
  matrix products  21.2 us (10%)
  local copies, waits for them, and re-layouts  18.4 us (9%)
  Pallas kernels  15.2 us (7%)
  other arithmetic  10.3 us (5%)
  between operations  2.7 us (1%)
    ppermute x14, waiting for transfers between devices, on_ring(): first, second = (send(first, perm=onward), send(second, perm=behind))  52.1 us
    ppermute x14, starting transfers between devices, on_ring(): first, second = (send(first, perm=onward), send(second, perm=behind))  20.5 us
    ppermute x1, waiting for transfers between devices, on_ring(): grad_gated = merge(pair, grad_own, send(grad_away, perm=swap_pair))  13.8 us
    pallas_call x1, Pallas kernels, products(): pl.pallas_call(functools.partial(products_kernel, size), out_shape=(jax.S...  13.7 us
    ppermute x4, waiting for transfers between devices, halve(): away = lax.ppermute(away, 'seq', [(i, i ^ bit) for i in range(nseq)])  13.4 us
    unnamed x95, local copies, waits for them, and re-layouts  12.4 us
    dot_general x6, matrix products, inverse_dft(): lax.dot_general(table, spectrum, (((0,), (0,)), ((), ())), precision=lax....  11.2 us
    ppermute x1, waiting for transfers between devices, on_ring(): out_away = send(out_away, perm=swap_pair)  10.6 us
  transfers between devices with their start and end apart: 40, of which 16 were waited for; matrix products, arithmetic and copies ran while one was open for 15% of the time, Pallas kernels for 0%

profile of v6, /device:TPU:0, one launch (start us, length us, event | category | flops | bytes accessed | tf_op | source)
XLA Modules:
  0.0 206.8 jit_solution(13916213265293469868)
XLA Ops:
  0.7 3.0 %collective-permute-start = (bf16[128,4096]{1,0:T(8,128)(2,1)}, bf16[128,4096]{1,0:T(8,128)(2,1)}, u32[]{:S(2)}, u32[]{:S(2)}) collective-permute-start(bf16[128,4096]{1,0:T(8,128)(2,1)} %cot_own.1), channel_id=1, source_target_pairs={{0,2},{1,3},{2,0},{3,1},{4,6},{5,7},{6,4},{7,5},{8,10},{9,11},{10,... | collective-permute-start | bytes 3145736 | tf_op jit(solution)/shard_map/ppermute | solution.py:270
  8.6 2.6 %copy.48 = bf16[128,4096]{0,1:T(8,128)(2,1)} copy(bf16[128,4096]{1,0:T(8,128)(2,1)} %param.15) | data formatting | bytes 2097152 | tf_op args[2]
  12.9 7.7 %collective-permute-done.1.refs_4_ = bf16[64,4096]{1,0:T(8,128)(2,1)} collective-permute-done((bf16[64,4096]{1,0:T(8,128)(2,1)}, bf16[64,4096]{1,0:T(8,128)(2,1)}, u32[]{:S(2)}, u32[]{:S(2)}) %collective-permute-start.1) | collective-permute-done | bytes 524320 | tf_op jit(solution)/shard_map/ppermute | solution.py:277
  22.6 2.7 %fusion.77 = f32[256,4096]{1,0:T(8,128)} fusion(bf16[256,128]{1,0:T(8,128)(2,1)S(1)} %copy-done.19, bf16[128,4096]{0,1:T(8,128)(2,1)S(1)} %bitcast.64), kind=kOutput, calls=%fused_computation.100 | convolution fusion | flops 268435456 | bytes 5308416 | tf_op jit(solution)/shard_map/dot_general | solution.py:25
  28.6 2.9 %convolution_add_fusion.4 = f32[256,4096]{1,0:T(8,128)S(1)} fusion(f32[256,4096]{1,0:T(8,128)} %fusion.77, bf16[256,128]{1,0:T(8,128)(2,1)S(1)} %copy-done.18, bf16[128,4096]{0,1:T(8,128)(2,1)S(1)} %bitcast.63), kind=kOutput, calls=%fused_computation.9 | convolution fusion | flops 269484032 | bytes 9502720 | tf_op jit(solution)/shard_map/dot_general | solution.py:26
  35.9 10.3 %collective-permute-done.5.refs_10_ = bf16[64,4096]{1,0:T(8,128)(2,1)S(1)} collective-permute-done((bf16[64,4096]{1,0:T(8,128)(2,1)}, bf16[64,4096]{1,0:T(8,128)(2,1)S(1)}, u32[]{:S(2)}, u32[]{:S(2)}) %collective-permute-start.5) | collective-permute-done | bytes 524320 | tf_op jit(solution)/shard_map/ppermute | solution.py:277
  50.1 8.0 %collective-permute-done.6.refs_14_ = bf16[64,4096]{1,0:T(8,128)(2,1)S(1)} collective-permute-done((bf16[64,4096]{1,0:T(8,128)(2,1)S(1)}, bf16[64,4096]{1,0:T(8,128)(2,1)S(1)}, u32[]{:S(2)}, u32[]{:S(2)}) %collective-permute-start.6) | collective-permute-done | bytes 524320 | tf_op jit(solution)/shard_map/ppermute | solution.py:277
  58.2 2.5 %collective-permute-start.18 = (bf16[64,4096]{1,0:T(8,128)(2,1)S(1)}, bf16[64,4096]{1,0:T(8,128)(2,1)S(1)}, u32[]{:S(2)}, u32[]{:S(2)}) collective-permute-start(bf16[64,4096]{1,0:T(8,128)(2,1)S(1)} %collective-permute-done.6.refs_14_), channel_id=1, source_target_pairs={{8,0},{9,1},{10,2},{11,3},{16,8},{17,9},{18,10},{19,11},{24,16},{2... | collective-permute-start | bytes 1572872 | tf_op jit(solution)/shard_map/ppermute | solution.py:277
  62.9 6.7 %collective-permute-done.16.refs_16_ = bf16[64,4096]{1,0:T(8,128)(2,1)} collective-permute-done((bf16[64,4096]{1,0:T(8,128)(2,1)S(1)}, bf16[64,4096]{1,0:T(8,128)(2,1)}, u32[]{:S(2)}, u32[]{:S(2)}) %collective-permute-start.16) | collective-permute-done | bytes 524320 | tf_op jit(solution)/shard_map/ppermute | solution.py:277
  73.0 2.7 %fusion.12 = (bf16[128,4096]{1,0:T(8,128)(2,1)S(1)}, f32[128,4096]{1,0:T(8,128)}) fusion(bf16[128,4096]{1,0:T(8,128)(2,1)S(1)} %copy-done.11, f32[4096,128]{0,1:T(8,128)S(1)} %fusion.36, f32[128,128]{1,0:T(8,128)S(1)} %copy-done.20, f32[256,4096]{1,0:T(8,128)S(1)} %fusion.4, f32[256,4096]{1,0:T(8,128)S(1)} %convolution_add_fusion.4), kind=kOutput, calls=%fused_computation.25 | convolution fusion | flops 407896064 | bytes 14745600 | tf_op jit(solution)/shard_map/dot_general | solution.py:43
  82.4 2.7 %collective-permute-start.26 = (bf16[64,4096]{1,0:T(8,128)(2,1)S(1)}, bf16[64,4096]{1,0:T(8,128)(2,1)}, u32[]{:S(2)}, u32[]{:S(2)}) collective-permute-start(bf16[64,4096]{1,0:T(8,128)(2,1)S(1)} %collective-permute-done.22.refs_22_), channel_id=1, source_target_pairs={{8,0},{9,1},{10,2},{11,3},{16,8},{17,9},{18,10},{19,11},{24,16},{2... | collective-permute-start | bytes 1572872 | tf_op jit(solution)/shard_map/ppermute | solution.py:277
  85.7 5.5 %collective-permute-done.8.gated_away = bf16[8,128,256]{2,1,0:T(8,128)(2,1)S(1)} collective-permute-done((bf16[8,128,256]{2,1,0:T(8,128)(2,1)S(1)}, bf16[8,128,256]{2,1,0:T(8,128)(2,1)S(1)}, u32[]{:S(2)}, u32[]{:S(2)}) %collective-permute-start.8) | collective-permute-done | bytes 524320 | tf_op jit(solution)/shard_map/ppermute | solution.py:288
  91.1 5.6 %collective-permute-done.24.refs_24_ = bf16[64,4096]{1,0:T(8,128)(2,1)} collective-permute-done((bf16[64,4096]{1,0:T(8,128)(2,1)}, bf16[64,4096]{1,0:T(8,128)(2,1)}, u32[]{:S(2)}, u32[]{:S(2)}) %collective-permute-start.24) | collective-permute-done | bytes 524320 | tf_op jit(solution)/shard_map/ppermute | solution.py:277
  96.9 2.9 %collective-permute-start.30 = (bf16[64,4096]{1,0:T(8,128)(2,1)}, bf16[64,4096]{1,0:T(8,128)(2,1)}, u32[]{:S(2)}, u32[]{:S(2)}) collective-permute-start(bf16[64,4096]{1,0:T(8,128)(2,1)} %collective-permute-done.26.refs_26_), channel_id=1, source_target_pairs={{8,0},{9,1},{10,2},{11,3},{16,8},{17,9},{18,10},{19,11},{24,16},{2... | collective-permute-start | bytes 1572872 | tf_op jit(solution)/shard_map/ppermute | solution.py:277
  100.5 10.3 %collective-permute-done.28.refs_28_ = bf16[64,4096]{1,0:T(8,128)(2,1)} collective-permute-done((bf16[64,4096]{1,0:T(8,128)(2,1)}, bf16[64,4096]{1,0:T(8,128)(2,1)}, u32[]{:S(2)}, u32[]{:S(2)}) %collective-permute-start.28) | collective-permute-done | bytes 524320 | tf_op jit(solution)/shard_map/ppermute | solution.py:277
  115.2 13.7 %shard_map.165 = (bf16[8,128,256]{2,1,0:T(8,128)(2,1)S(1)}, bf16[8,128,256]{2,1,0:T(8,128)(2,1)S(1)}, f32[128,4096]{1,0:T(8,128)S(1)}, bf16[128,4096]{1,0:T(8,128)(2,1)S(1)}) custom-call(s32[9]{0:T(128)S(1)} %stack.39.scalars, bf16[128,4096]{1,0:T(8,128)(2,1)} %cot_own.1, bf16[128,4096]{1,0:T(8,128)(2,1)} %collective-permute-done.cot_away, ...), custom_call_target="tpu_custom_call" | custom-call | flops 8589934592 | bytes 22020096 | tf_op jit(solution)/shard_map/pallas_call | solution.py:195
  129.0 13.8 %collective-permute-done.33.away = bf16[8,128,256]{2,1,0:T(8,128)(2,1)S(1)} collective-permute-done((bf16[8,128,256]{2,1,0:T(8,128)(2,1)S(1)}, bf16[8,128,256]{2,1,0:T(8,128)(2,1)S(1)}, u32[]{:S(2)}, u32[]{:S(2)}) %collective-permute-start.33) | collective-permute-done | bytes 524320 | tf_op jit(solution)/shard_map/ppermute | solution.py:294
  156.7 3.0 %collective-permute-done.35 = f32[2,8,128,128]{3,2,1,0:T(8,128)} collective-permute-done((f32[2,8,128,128]{3,2,1,0:T(8,128)}, f32[2,8,128,128]{3,2,1,0:T(8,128)}, u32[]{:S(2)}, u32[]{:S(2)}) %collective-permute-start.35) | collective-permute-done | bytes 1048608 | tf_op jit(solution)/shard_map/ppermute | solution.py:114
  166.4 5.2 %collective-permute-done.36 = bf16[8,128,128]{2,1,0:T(8,128)(2,1)S(1)} collective-permute-done((bf16[8,128,128]{2,1,0:T(8,128)(2,1)}, bf16[8,128,128]{2,1,0:T(8,128)(2,1)S(1)}, u32[]{:S(2)}, u32[]{:S(2)}) %collective-permute-start.36) | collective-permute-done | bytes 262176 | tf_op jit(solution)/shard_map/ppermute | solution.py:110
  174.6 2.9 %fusion.13 = bf16[128,4096]{1,0:T(8,128)(2,1)} fusion(f32[128,4096]{1,0:T(8,128)} %get-tuple-element.65, bf16[128,4096]{1,0:T(8,128)(2,1)S(1)} %shard_map.166), kind=kLoop, calls=%fused_computation.26 | loop fusion | flops 1572864 | bytes 4194304 | tf_op jit(solution)/shard_map/convert_element_type | solution.py:50
  177.4 8.2 %collective-permute-done.37 = bf16[4,128,128]{2,1,0:T(8,128)(2,1)S(1)} collective-permute-done((bf16[4,128,128]{2,1,0:T(8,128)(2,1)S(1)}, bf16[4,128,128]{2,1,0:T(8,128)(2,1)S(1)}, u32[]{:S(2)}, u32[]{:S(2)}) %collective-permute-start.37) | collective-permute-done | bytes 131104 | tf_op jit(solution)/shard_map/ppermute | solution.py:110
  185.7 2.8 %collective-permute-start.38 = (bf16[2,128,128]{2,1,0:T(8,128)(2,1)S(1)}, bf16[2,128,128]{2,1,0:T(8,128)(2,1)S(1)}, u32[]{:S(2)}, u32[]{:S(2)}) collective-permute-start(bf16[2,128,128]{2,1,0:T(8,128)(2,1)S(1)} %fusion.71), channel_id=1, source_target_pairs={{0,16},{1,17},{2,18},{3,19},{4,20},{5,21},{6,22},{7,23},{8,24},{9,... | collective-permute-start | bytes 196616 | tf_op jit(solution)/shard_map/ppermute | solution.py:110
  188.5 10.6 %collective-permute-done.32 = bf16[128,4096]{1,0:T(8,128)(2,1)S(1)} collective-permute-done((bf16[128,4096]{1,0:T(8,128)(2,1)}, bf16[128,4096]{1,0:T(8,128)(2,1)S(1)}, u32[]{:S(2)}, u32[]{:S(2)}) %collective-permute-start.32) | collective-permute-done | bytes 1048608 | tf_op jit(solution)/shard_map/ppermute | solution.py:295
  200.4 2.4 %collective-permute-start.39 = (bf16[1,128,128]{2,1,0:T(8,128)(2,1)S(1)}, bf16[1,128,128]{2,1,0:T(8,128)(2,1)S(1)}, u32[]{:S(2)}, u32[]{:S(2)}) collective-permute-start(bf16[1,128,128]{2,1,0:T(8,128)(2,1)S(1)} %dynamic-slice_convert_fusion.2), channel_id=1, source_target_pairs={{0,2},{1,3},{2,0},{3,1},{4,6},{5,7},{6,4},{7,5},{8,10},{9,11},{10,... | collective-permute-start | bytes 98312 | tf_op jit(solution)/shard_map/ppermute | solution.py:110
  (187 shorter events, 65.2 us)
Async XLA Ops:
  0.7 26.6 %collective-permute-start = (bf16[128,4096]{1,0:T(8,128)(2,1)}, bf16[128,4096]{1,0:T(8,128)(2,1)}, u32[]{:S(2)}, u32[]{:S(2)}) collective-permute-start(bf16[128,4096]{1,0:T(8,128)(2,1)} %cot_own.1), channel_id=1, source_target_pairs={{0,2},{1,3},{2,0},{3,1},{4,6},{5,7},{6,4},{7,5},{8,10},{9,11},{10,... | collective-permute-start | bytes 3145736 | tf_op jit(solution)/shard_map/ppermute | solution.py:270
  3.7 73.0 %collective-permute-start.9 = (bf16[128,4096]{1,0:T(8,128)(2,1)}, bf16[128,4096]{1,0:T(8,128)(2,1)}, u32[]{:S(2)}, u32[]{:S(2)}) collective-permute-start(bf16[128,4096]{1,0:T(8,128)(2,1)} %param.16), channel_id=1, source_target_pairs={{0,1},{1,0},{2,3},{3,2},{4,5},{5,4},{6,7},{7,6},{8,9},{9,8},{10,11... | collective-permute-start | bytes 3145736 | tf_op jit(solution)/shard_map/ppermute | solution.py:269
  5.9 14.7 %collective-permute-start.1 = (bf16[64,4096]{1,0:T(8,128)(2,1)}, bf16[64,4096]{1,0:T(8,128)(2,1)}, u32[]{:S(2)}, u32[]{:S(2)}) collective-permute-start(bf16[64,4096]{1,0:T(8,128)(2,1)} %get-tuple-element.61.refs_0_), channel_id=1, source_target_pairs={{0,8},{1,9},{2,10},{3,11},{8,16},{9,17},{10,18},{11,19},{16,24},{1... | collective-permute-start | bytes 1572872 | tf_op jit(solution)/shard_map/ppermute | solution.py:277
  7.5 14.7 %collective-permute-start.4 = (bf16[64,4096]{1,0:T(8,128)(2,1)}, bf16[64,4096]{1,0:T(8,128)(2,1)}, u32[]{:S(2)}, u32[]{:S(2)}) collective-permute-start(bf16[64,4096]{1,0:T(8,128)(2,1)} %get-tuple-element.60.refs_2_), channel_id=1, source_target_pairs={{8,0},{9,1},{10,2},{11,3},{16,8},{17,9},{18,10},{19,11},{24,16},{2... | collective-permute-start | bytes 1572872 | tf_op jit(solution)/shard_map/ppermute | solution.py:277
  20.6 13.8 %collective-permute-start.2 = (bf16[64,4096]{1,0:T(8,128)(2,1)}, bf16[64,4096]{1,0:T(8,128)(2,1)S(1)}, u32[]{:S(2)}, u32[]{:S(2)}) collective-permute-start(bf16[64,4096]{1,0:T(8,128)(2,1)} %collective-permute-done.1.refs_4_), channel_id=1, source_target_pairs={{0,8},{1,9},{2,10},{3,11},{8,16},{9,17},{10,18},{11,19},{16,24},{1... | collective-permute-start | bytes 1572872 | tf_op jit(solution)/shard_map/ppermute | solution.py:277
  22.2 24.1 %collective-permute-start.5 = (bf16[64,4096]{1,0:T(8,128)(2,1)}, bf16[64,4096]{1,0:T(8,128)(2,1)S(1)}, u32[]{:S(2)}, u32[]{:S(2)}) collective-permute-start(bf16[64,4096]{1,0:T(8,128)(2,1)} %collective-permute-done.4.refs_6_), channel_id=1, source_target_pairs={{8,0},{9,1},{10,2},{11,3},{16,8},{17,9},{18,10},{19,11},{24,16},{2... | collective-permute-start | bytes 1572872 | tf_op jit(solution)/shard_map/ppermute | solution.py:277
  27.3 30.9 %collective-permute-start.7 = (bf16[128,4096]{0,1:T(8,128)(2,1)S(1)}, bf16[128,4096]{0,1:T(8,128)(2,1)S(1)}, u32[]{:S(2)}, u32[]{:S(2)}) collective-permute-start(bf16[128,4096]{0,1:T(8,128)(2,1)S(1)} %fusion.11), channel_id=1, source_target_pairs={{0,1},{1,2},{2,3},{3,4},{4,5},{5,6},{6,7},{7,8},{8,9},{9,10},{10,1... | collective-permute-start | bytes 3145736 | tf_op jit(solution)/shard_map/ppermute | solution.py:272
  31.5 30.7 %collective-permute-start.10 = (bf16[64,4096]{1,0:T(8,128)(2,1)}, bf16[64,4096]{1,0:T(8,128)(2,1)S(1)}, u32[]{:S(2)}, u32[]{:S(2)}) collective-permute-start(bf16[64,4096]{1,0:T(8,128)(2,1)} %collective-permute-done.1.refs_4_), channel_id=1, source_target_pairs={{0,1},{1,0},{2,3},{3,2},{4,5},{5,4},{6,7},{7,6},{8,9},{9,8},{10,11... | collective-permute-start | bytes 1572872 | tf_op jit(solution)/shard_map/ppermute | solution.py:289
  34.4 15.7 %collective-permute-start.3 = (bf16[64,4096]{1,0:T(8,128)(2,1)S(1)}, bf16[64,4096]{1,0:T(8,128)(2,1)S(1)}, u32[]{:S(2)}, u32[]{:S(2)}) collective-permute-start(bf16[64,4096]{1,0:T(8,128)(2,1)S(1)} %collective-permute-done.2.refs_8_), channel_id=1, source_target_pairs={{0,8},{1,9},{2,10},{3,11},{8,16},{9,17},{10,18},{11,19},{16,24},{1... | collective-permute-start | bytes 1572872 | tf_op jit(solution)/shard_map/ppermute | solution.py:277
  62.2 14.4 %collective-permute-start.12 = (bf16[64,4096]{1,0:T(8,128)(2,1)S(1)}, bf16[64,4096]{1,0:T(8,128)(2,1)S(1)}, u32[]{:S(2)}, u32[]{:S(2)}) collective-permute-start(bf16[64,4096]{1,0:T(8,128)(2,1)S(1)} %collective-permute-done.2.refs_8_), channel_id=1, source_target_pairs={{0,1},{1,0},{2,3},{3,2},{4,5},{5,4},{6,7},{7,6},{8,9},{9,8},{10,11... | collective-permute-start | bytes 1572872 | tf_op jit(solution)/shard_map/ppermute | solution.py:289
  62.4 14.8 %collective-permute-start.13 = (bf16[64,4096]{1,0:T(8,128)(2,1)S(1)}, bf16[64,4096]{1,0:T(8,128)(2,1)S(1)}, u32[]{:S(2)}, u32[]{:S(2)}) collective-permute-start(bf16[64,4096]{1,0:T(8,128)(2,1)S(1)} %collective-permute-done.5.refs_10_), channel_id=1, source_target_pairs={{0,1},{1,0},{2,3},{3,2},{4,5},{5,4},{6,7},{7,6},{8,9},{9,8},{10,11... | collective-permute-start | bytes 1572872 | tf_op jit(solution)/shard_map/ppermute | solution.py:289
  77.2 13.9 %collective-permute-start.8 = (bf16[8,128,256]{2,1,0:T(8,128)(2,1)S(1)}, bf16[8,128,256]{2,1,0:T(8,128)(2,1)S(1)}, u32[]{:S(2)}, u32[]{:S(2)}) collective-permute-start(bf16[8,128,256]{2,1,0:T(8,128)(2,1)S(1)} %get-tuple-element.29), channel_id=1, source_target_pairs={{0,2},{1,3},{2,0},{3,1},{4,6},{5,7},{6,4},{7,5},{8,10},{9,11},{10,... | collective-permute-start | bytes 1572872 | tf_op jit(solution)/shard_map/ppermute | solution.py:288
  79.1 17.6 %collective-permute-start.24 = (bf16[64,4096]{1,0:T(8,128)(2,1)}, bf16[64,4096]{1,0:T(8,128)(2,1)}, u32[]{:S(2)}, u32[]{:S(2)}) collective-permute-start(bf16[64,4096]{1,0:T(8,128)(2,1)} %collective-permute-done.20.refs_20_), channel_id=1, source_target_pairs={{0,8},{1,9},{2,10},{3,11},{8,16},{9,17},{10,18},{11,19},{16,24},{1... | collective-permute-start | bytes 1572872 | tf_op jit(solution)/shard_map/ppermute | solution.py:277
  82.4 14.5 %collective-permute-start.26 = (bf16[64,4096]{1,0:T(8,128)(2,1)S(1)}, bf16[64,4096]{1,0:T(8,128)(2,1)}, u32[]{:S(2)}, u32[]{:S(2)}) collective-permute-start(bf16[64,4096]{1,0:T(8,128)(2,1)S(1)} %collective-permute-done.22.refs_22_), channel_id=1, source_target_pairs={{8,0},{9,1},{10,2},{11,3},{16,8},{17,9},{18,10},{19,11},{24,16},{2... | collective-permute-start | bytes 1572872 | tf_op jit(solution)/shard_map/ppermute | solution.py:277
  85.1 14.8 %collective-permute-start.17 = (bf16[64,4096]{1,0:T(8,128)(2,1)}, bf16[64,4096]{1,0:T(8,128)(2,1)}, u32[]{:S(2)}, u32[]{:S(2)}) collective-permute-start(bf16[64,4096]{1,0:T(8,128)(2,1)} %collective-permute-done.16.refs_16_), channel_id=1, source_target_pairs={{0,1},{1,0},{2,3},{3,2},{4,5},{5,4},{6,7},{7,6},{8,9},{9,8},{10,11... | collective-permute-start | bytes 1572872 | tf_op jit(solution)/shard_map/ppermute | solution.py:289
  85.1 14.8 %collective-permute-start.19 = (bf16[64,4096]{1,0:T(8,128)(2,1)S(1)}, bf16[64,4096]{1,0:T(8,128)(2,1)}, u32[]{:S(2)}, u32[]{:S(2)}) collective-permute-start(bf16[64,4096]{1,0:T(8,128)(2,1)S(1)} %collective-permute-done.18.refs_18_), channel_id=1, source_target_pairs={{0,1},{1,0},{2,3},{3,2},{4,5},{5,4},{6,7},{7,6},{8,9},{9,8},{10,11... | collective-permute-start | bytes 1572872 | tf_op jit(solution)/shard_map/ppermute | solution.py:289
  96.7 14.1 %collective-permute-start.28 = (bf16[64,4096]{1,0:T(8,128)(2,1)}, bf16[64,4096]{1,0:T(8,128)(2,1)}, u32[]{:S(2)}, u32[]{:S(2)}) collective-permute-start(bf16[64,4096]{1,0:T(8,128)(2,1)} %collective-permute-done.24.refs_24_), channel_id=1, source_target_pairs={{0,8},{1,9},{2,10},{3,11},{8,16},{9,17},{10,18},{11,19},{16,24},{1... | collective-permute-start | bytes 1572872 | tf_op jit(solution)/shard_map/ppermute | solution.py:277
  96.9 14.0 %collective-permute-start.30 = (bf16[64,4096]{1,0:T(8,128)(2,1)}, bf16[64,4096]{1,0:T(8,128)(2,1)}, u32[]{:S(2)}, u32[]{:S(2)}) collective-permute-start(bf16[64,4096]{1,0:T(8,128)(2,1)} %collective-permute-done.26.refs_26_), channel_id=1, source_target_pairs={{8,0},{9,1},{10,2},{11,3},{16,8},{17,9},{18,10},{19,11},{24,16},{2... | collective-permute-start | bytes 1572872 | tf_op jit(solution)/shard_map/ppermute | solution.py:277
  99.9 13.8 %collective-permute-start.23 = (bf16[64,4096]{1,0:T(8,128)(2,1)}, bf16[64,4096]{1,0:T(8,128)(2,1)S(1)}, u32[]{:S(2)}, u32[]{:S(2)}) collective-permute-start(bf16[64,4096]{1,0:T(8,128)(2,1)} %copy-done.36), channel_id=1, source_target_pairs={{0,1},{1,0},{2,3},{3,2},{4,5},{5,4},{6,7},{7,6},{8,9},{9,8},{10,11... | collective-permute-start | bytes 1572872 | tf_op jit(solution)/shard_map/ppermute | solution.py:289
  100.0 13.7 %collective-permute-start.25 = (bf16[64,4096]{1,0:T(8,128)(2,1)}, bf16[64,4096]{1,0:T(8,128)(2,1)S(1)}, u32[]{:S(2)}, u32[]{:S(2)}) collective-permute-start(bf16[64,4096]{1,0:T(8,128)(2,1)} %collective-permute-done.24.refs_24_), channel_id=1, source_target_pairs={{0,1},{1,0},{2,3},{3,2},{4,5},{5,4},{6,7},{7,6},{8,9},{9,8},{10,11... | collective-permute-start | bytes 1572872 | tf_op jit(solution)/shard_map/ppermute | solution.py:289
  128.9 13.9 %collective-permute-start.33 = (bf16[8,128,256]{2,1,0:T(8,128)(2,1)S(1)}, bf16[8,128,256]{2,1,0:T(8,128)(2,1)S(1)}, u32[]{:S(2)}, u32[]{:S(2)}) collective-permute-start(bf16[8,128,256]{2,1,0:T(8,128)(2,1)S(1)} %get-tuple-element.37), channel_id=1, source_target_pairs={{0,2},{1,3},{2,0},{3,1},{4,6},{5,7},{6,4},{7,5},{8,10},{9,11},{10,... | collective-permute-start | bytes 1572872 | tf_op jit(solution)/shard_map/ppermute | solution.py:294
  164.8 34.3 %collective-permute-start.32 = (bf16[128,4096]{1,0:T(8,128)(2,1)}, bf16[128,4096]{1,0:T(8,128)(2,1)S(1)}, u32[]{:S(2)}, u32[]{:S(2)}) collective-permute-start(bf16[128,4096]{1,0:T(8,128)(2,1)} %copy-done.3), channel_id=1, source_target_pairs={{0,2},{1,3},{2,0},{3,1},{4,6},{5,7},{6,4},{7,5},{8,10},{9,11},{10,... | collective-permute-start | bytes 3145736 | tf_op jit(solution)/shard_map/ppermute | solution.py:295
  165.1 37.7 %collective-permute-start.34 = (bf16[128,4096]{0,1:T(8,128)(2,1)}, bf16[128,4096]{0,1:T(8,128)(2,1)S(1)}, u32[]{:S(2)}, u32[]{:S(2)}) collective-permute-start(bf16[128,4096]{0,1:T(8,128)(2,1)} %fusion.17), channel_id=1, source_target_pairs={{1,0},{2,1},{3,2},{4,3},{5,4},{6,5},{7,6},{8,7},{9,8},{10,9},{11,1... | collective-permute-start | bytes 3145736 | tf_op jit(solution)/shard_map/ppermute | solution.py:301
  185.7 14.7 %collective-permute-start.38 = (bf16[2,128,128]{2,1,0:T(8,128)(2,1)S(1)}, bf16[2,128,128]{2,1,0:T(8,128)(2,1)S(1)}, u32[]{:S(2)}, u32[]{:S(2)}) collective-permute-start(bf16[2,128,128]{2,1,0:T(8,128)(2,1)S(1)} %fusion.71), channel_id=1, source_target_pairs={{0,16},{1,17},{2,18},{3,19},{4,20},{5,21},{6,22},{7,23},{8,24},{9,... | collective-permute-start | bytes 196616 | tf_op jit(solution)/shard_map/ppermute | solution.py:110
  (61 other events, 681.1 us)

commit v7 on v6

--- a/solution.py
+++ b/solution.py
@@ -299,7 +299,6 @@
     back = inverse_dft(table, times_conj(grads, filt), scale)
     across = jnp.where(linked, back[:length], 0.0).astype(BF16)
     ahead = send(across, perm=earlier)
-    grads, across = tie((grads, across))
     taps_part = inverse_dft(table_now, times_conj(grads, data), scale)
     taps_grad = sum_over_ring(taps_part, nseq, place).T
     outputs = (out_own + out_away.astype(F32)).astype(BF16)

time: 207 us -> 195 us (0.942)
  waiting for transfers between devices: 98.5 us -> 90.1 us
  other arithmetic: 10.3 us -> 6.18 us
  matrix products: 21.2 us -> 24.8 us
  starting transfers between devices: 40.6 us -> 38.4 us
    ppermute x1, waiting for transfers between devices: 10.6 us -> 0.01 us  [on_ring(): out_away = send(out_away, perm=swap_pair)]
    ppermute x4, waiting for transfers between devices: 13.4 us -> 18.7 us  [halve(): away = lax.ppermute(away, 'seq', [(i, i ^ bit) for i in range(nseq)])]
    dot_general x6, matrix products: 11.2 us -> 14.8 us  [inverse_dft(): lax.dot_general(table, spectrum, (((0,), (0,)), ((), ())), precision=lax....]
    ppermute x1, waiting for transfers between devices: 3 us -> 0.01 us  [sum_over_ring(): part = kept + lax.ppermute(away, 'seq', [(i, i ^ 1) for i in range(nseq)])]
    ppermute x4, starting transfers between devices: 8.84 us -> 6.52 us  [halve(): away = lax.ppermute(away, 'seq', [(i, i ^ bit) for i in range(nseq)])]
    unnamed x95 -> x97, local copies, waits for them, and re-layouts: 12.4 us -> 12.2 us
  transfers between devices with their start and end apart: 40 -> 40, of which waited for: 16 -> 16; matrix products, arithmetic and copies ran while one was open for 15% -> 20% of each run, Pallas kernels for 0% -> 0%
where the time goes in v7:
time: 195 us
  waiting for transfers between devices  90.1 us (46%)
  starting transfers between devices  38.4 us (20%)
  matrix products  24.8 us (13%)
  local copies, waits for them, and re-layouts  17.5 us (9%)
  Pallas kernels  15.2 us (8%)
  other arithmetic  6.18 us (3%)
  between operations  2.75 us (1%)
    ppermute x14, waiting for transfers between devices, on_ring(): first, second = (send(first, perm=onward), send(second, perm=behind))  52.1 us
    ppermute x14, starting transfers between devices, on_ring(): first, second = (send(first, perm=onward), send(second, perm=behind))  20.5 us
    ppermute x4, waiting for transfers between devices, halve(): away = lax.ppermute(away, 'seq', [(i, i ^ bit) for i in range(nseq)])  18.7 us
    dot_general x6, matrix products, inverse_dft(): lax.dot_general(table, spectrum, (((0,), (0,)), ((), ())), precision=lax....  14.8 us
    ppermute x1, waiting for transfers between devices, on_ring(): grad_gated = merge(pair, grad_own, send(grad_away, perm=swap_pair))  13.8 us
    pallas_call x1, Pallas kernels, products(): pl.pallas_call(functools.partial(products_kernel, size), out_shape=(jax.S...  13.7 us
    unnamed x97, local copies, waits for them, and re-layouts  12.2 us
    ppermute x4, starting transfers between devices, halve(): away = lax.ppermute(away, 'seq', [(i, i ^ bit) for i in range(nseq)])  6.52 us
  transfers between devices with their start and end apart: 40, of which 16 were waited for; matrix products, arithmetic and copies ran while one was open for 20% of the time, Pallas kernels for 0%

profile of v7, /device:TPU:0, one launch (start us, length us, event | category | flops | bytes accessed | tf_op | source)
XLA Modules:
  0.0 194.9 jit_solution(15616231103809056704)
XLA Ops:
  0.7 3.0 %collective-permute-start = (bf16[128,4096]{1,0:T(8,128)(2,1)}, bf16[128,4096]{1,0:T(8,128)(2,1)}, u32[]{:S(2)}, u32[]{:S(2)}) collective-permute-start(bf16[128,4096]{1,0:T(8,128)(2,1)} %cot_own.1), channel_id=1, source_target_pairs={{0,2},{1,3},{2,0},{3,1},{4,6},{5,7},{6,4},{7,5},{8,10},{9,11},{10,... | collective-permute-start | bytes 3145736 | tf_op jit(solution)/shard_map/ppermute | solution.py:270
  8.6 2.6 %copy.48 = bf16[128,4096]{0,1:T(8,128)(2,1)} copy(bf16[128,4096]{1,0:T(8,128)(2,1)} %param.15) | data formatting | bytes 2097152 | tf_op args[2]
  12.8 7.7 %collective-permute-done.1.refs_4_ = bf16[64,4096]{1,0:T(8,128)(2,1)} collective-permute-done((bf16[64,4096]{1,0:T(8,128)(2,1)}, bf16[64,4096]{1,0:T(8,128)(2,1)}, u32[]{:S(2)}, u32[]{:S(2)}) %collective-permute-start.1) | collective-permute-done | bytes 524320 | tf_op jit(solution)/shard_map/ppermute | solution.py:277
  22.6 2.7 %fusion.77 = f32[256,4096]{1,0:T(8,128)} fusion(bf16[256,128]{1,0:T(8,128)(2,1)S(1)} %copy-done.20, bf16[128,4096]{0,1:T(8,128)(2,1)S(1)} %bitcast.64), kind=kOutput, calls=%fused_computation.100 | convolution fusion | flops 268435456 | bytes 5308416 | tf_op jit(solution)/shard_map/dot_general | solution.py:25
  28.6 2.9 %convolution_add_fusion.4 = f32[256,4096]{1,0:T(8,128)S(1)} fusion(f32[256,4096]{1,0:T(8,128)} %fusion.77, bf16[256,128]{1,0:T(8,128)(2,1)S(1)} %copy-done.19, bf16[128,4096]{0,1:T(8,128)(2,1)S(1)} %bitcast.63), kind=kOutput, calls=%fused_computation.9 | convolution fusion | flops 269484032 | bytes 9502720 | tf_op jit(solution)/shard_map/dot_general | solution.py:26
  31.5 2.4 %collective-permute-start.10 = (bf16[64,4096]{1,0:T(8,128)(2,1)}, bf16[64,4096]{1,0:T(8,128)(2,1)S(1)}, u32[]{:S(2)}, u32[]{:S(2)}) collective-permute-start(bf16[64,4096]{1,0:T(8,128)(2,1)} %collective-permute-done.1.refs_4_), channel_id=1, source_target_pairs={{0,1},{1,0},{2,3},{3,2},{4,5},{5,4},{6,7},{7,6},{8,9},{9,8},{10,11... | collective-permute-start | bytes 1572872 | tf_op jit(solution)/shard_map/ppermute | solution.py:289
  35.9 10.3 %collective-permute-done.5.refs_10_ = bf16[64,4096]{1,0:T(8,128)(2,1)S(1)} collective-permute-done((bf16[64,4096]{1,0:T(8,128)(2,1)}, bf16[64,4096]{1,0:T(8,128)(2,1)S(1)}, u32[]{:S(2)}, u32[]{:S(2)}) %collective-permute-start.5) | collective-permute-done | bytes 524320 | tf_op jit(solution)/shard_map/ppermute | solution.py:277
  46.2 2.4 %collective-permute-start.6 = (bf16[64,4096]{1,0:T(8,128)(2,1)S(1)}, bf16[64,4096]{1,0:T(8,128)(2,1)S(1)}, u32[]{:S(2)}, u32[]{:S(2)}) collective-permute-start(bf16[64,4096]{1,0:T(8,128)(2,1)S(1)} %collective-permute-done.5.refs_10_), channel_id=1, source_target_pairs={{8,0},{9,1},{10,2},{11,3},{16,8},{17,9},{18,10},{19,11},{24,16},{2... | collective-permute-start | bytes 1572872 | tf_op jit(solution)/shard_map/ppermute | solution.py:277
  50.1 8.0 %collective-permute-done.6.refs_14_ = bf16[64,4096]{1,0:T(8,128)(2,1)S(1)} collective-permute-done((bf16[64,4096]{1,0:T(8,128)(2,1)S(1)}, bf16[64,4096]{1,0:T(8,128)(2,1)S(1)}, u32[]{:S(2)}, u32[]{:S(2)}) %collective-permute-start.6) | collective-permute-done | bytes 524320 | tf_op jit(solution)/shard_map/ppermute | solution.py:277
  58.2 2.5 %collective-permute-start.18 = (bf16[64,4096]{1,0:T(8,128)(2,1)S(1)}, bf16[64,4096]{1,0:T(8,128)(2,1)S(1)}, u32[]{:S(2)}, u32[]{:S(2)}) collective-permute-start(bf16[64,4096]{1,0:T(8,128)(2,1)S(1)} %collective-permute-done.6.refs_14_), channel_id=1, source_target_pairs={{8,0},{9,1},{10,2},{11,3},{16,8},{17,9},{18,10},{19,11},{24,16},{2... | collective-permute-start | bytes 1572872 | tf_op jit(solution)/shard_map/ppermute | solution.py:277
  62.9 6.7 %collective-permute-done.16.refs_16_ = bf16[64,4096]{1,0:T(8,128)(2,1)} collective-permute-done((bf16[64,4096]{1,0:T(8,128)(2,1)S(1)}, bf16[64,4096]{1,0:T(8,128)(2,1)}, u32[]{:S(2)}, u32[]{:S(2)}) %collective-permute-start.16) | collective-permute-done | bytes 524320 | tf_op jit(solution)/shard_map/ppermute | solution.py:277
  72.9 2.7 %fusion.12 = (bf16[128,4096]{1,0:T(8,128)(2,1)S(1)}, f32[128,4096]{1,0:T(8,128)}) fusion(bf16[128,4096]{1,0:T(8,128)(2,1)S(1)} %copy-done.12, f32[4096,128]{0,1:T(8,128)S(1)} %fusion.36, f32[128,128]{1,0:T(8,128)S(1)} %copy-done.21, f32[256,4096]{1,0:T(8,128)S(1)} %fusion.4, f32[256,4096]{1,0:T(8,128)S(1)} %convolution_add_fusion.4), kind=kOutput, calls=%fused_computation.25 | convolution fusion | flops 407896064 | bytes 14745600 | tf_op jit(solution)/shard_map/dot_general | solution.py:43
  79.1 2.4 %collective-permute-start.24 = (bf16[64,4096]{1,0:T(8,128)(2,1)}, bf16[64,4096]{1,0:T(8,128)(2,1)}, u32[]{:S(2)}, u32[]{:S(2)}) collective-permute-start(bf16[64,4096]{1,0:T(8,128)(2,1)} %collective-permute-done.20.refs_20_), channel_id=1, source_target_pairs={{0,8},{1,9},{2,10},{3,11},{8,16},{9,17},{10,18},{11,19},{16,24},{1... | collective-permute-start | bytes 1572872 | tf_op jit(solution)/shard_map/ppermute | solution.py:277
  82.4 2.7 %collective-permute-start.26 = (bf16[64,4096]{1,0:T(8,128)(2,1)S(1)}, bf16[64,4096]{1,0:T(8,128)(2,1)}, u32[]{:S(2)}, u32[]{:S(2)}) collective-permute-start(bf16[64,4096]{1,0:T(8,128)(2,1)S(1)} %collective-permute-done.22.refs_22_), channel_id=1, source_target_pairs={{8,0},{9,1},{10,2},{11,3},{16,8},{17,9},{18,10},{19,11},{24,16},{2... | collective-permute-start | bytes 1572872 | tf_op jit(solution)/shard_map/ppermute | solution.py:277
  85.6 5.5 %collective-permute-done.8.gated_away = bf16[8,128,256]{2,1,0:T(8,128)(2,1)S(1)} collective-permute-done((bf16[8,128,256]{2,1,0:T(8,128)(2,1)S(1)}, bf16[8,128,256]{2,1,0:T(8,128)(2,1)S(1)}, u32[]{:S(2)}, u32[]{:S(2)}) %collective-permute-start.8) | collective-permute-done | bytes 524320 | tf_op jit(solution)/shard_map/ppermute | solution.py:288
  91.1 5.6 %collective-permute-done.24.refs_24_ = bf16[64,4096]{1,0:T(8,128)(2,1)} collective-permute-done((bf16[64,4096]{1,0:T(8,128)(2,1)}, bf16[64,4096]{1,0:T(8,128)(2,1)}, u32[]{:S(2)}, u32[]{:S(2)}) %collective-permute-start.24) | collective-permute-done | bytes 524320 | tf_op jit(solution)/shard_map/ppermute | solution.py:277
  96.9 2.9 %collective-permute-start.30 = (bf16[64,4096]{1,0:T(8,128)(2,1)}, bf16[64,4096]{1,0:T(8,128)(2,1)}, u32[]{:S(2)}, u32[]{:S(2)}) collective-permute-start(bf16[64,4096]{1,0:T(8,128)(2,1)} %collective-permute-done.26.refs_26_), channel_id=1, source_target_pairs={{8,0},{9,1},{10,2},{11,3},{16,8},{17,9},{18,10},{19,11},{24,16},{2... | collective-permute-start | bytes 1572872 | tf_op jit(solution)/shard_map/ppermute | solution.py:277
  100.5 10.3 %collective-permute-done.28.refs_28_ = bf16[64,4096]{1,0:T(8,128)(2,1)} collective-permute-done((bf16[64,4096]{1,0:T(8,128)(2,1)}, bf16[64,4096]{1,0:T(8,128)(2,1)}, u32[]{:S(2)}, u32[]{:S(2)}) %collective-permute-start.28) | collective-permute-done | bytes 524320 | tf_op jit(solution)/shard_map/ppermute | solution.py:277
  115.2 13.7 %shard_map.165 = (bf16[8,128,256]{2,1,0:T(8,128)(2,1)S(1)}, bf16[8,128,256]{2,1,0:T(8,128)(2,1)S(1)}, f32[128,4096]{1,0:T(8,128)S(1)}, bf16[128,4096]{1,0:T(8,128)(2,1)S(1)}) custom-call(s32[9]{0:T(128)S(1)} %stack.39.scalars, bf16[128,4096]{1,0:T(8,128)(2,1)} %cot_own.1, bf16[128,4096]{1,0:T(8,128)(2,1)} %collective-permute-done.cot_away, ...), custom_call_target="tpu_custom_call" | custom-call | flops 8589934592 | bytes 22020096 | tf_op jit(solution)/shard_map/pallas_call | solution.py:195
  129.0 13.8 %collective-permute-done.33.away = bf16[8,128,256]{2,1,0:T(8,128)(2,1)S(1)} collective-permute-done((bf16[8,128,256]{2,1,0:T(8,128)(2,1)S(1)}, bf16[8,128,256]{2,1,0:T(8,128)(2,1)S(1)}, u32[]{:S(2)}, u32[]{:S(2)}) %collective-permute-start.33) | collective-permute-done | bytes 524320 | tf_op jit(solution)/shard_map/ppermute | solution.py:294
  151.9 5.9 %fusion.29 = f32[4096,256]{1,0:T(8,128)S(1)} fusion(f32[128,256]{1,0:T(8,128)S(1)} %copy-done.24, f32[256,4096]{1,0:T(8,128)} %copy-done.10, f32[256,4096]{1,0:T(8,128)} %copy-done.6), kind=kOutput, calls=%fused_computation.44 | convolution fusion | flops 806879232 | bytes 12713984 | tf_op jit(solution)/shard_map/dot_general | solution.py:43
  164.9 5.1 %collective-permute-done.36 = bf16[8,128,128]{2,1,0:T(8,128)(2,1)S(1)} collective-permute-done((bf16[8,128,128]{2,1,0:T(8,128)(2,1)S(1)}, bf16[8,128,128]{2,1,0:T(8,128)(2,1)S(1)}, u32[]{:S(2)}, u32[]{:S(2)}) %collective-permute-start.36) | collective-permute-done | bytes 262176 | tf_op jit(solution)/shard_map/ppermute | solution.py:110
  173.2 11.7 %collective-permute-done.37 = bf16[4,128,128]{2,1,0:T(8,128)(2,1)S(1)} collective-permute-done((bf16[4,128,128]{2,1,0:T(8,128)(2,1)S(1)}, bf16[4,128,128]{2,1,0:T(8,128)(2,1)S(1)}, u32[]{:S(2)}, u32[]{:S(2)}) %collective-permute-start.37) | collective-permute-done | bytes 131104 | tf_op jit(solution)/shard_map/ppermute | solution.py:110
  184.9 2.8 %collective-permute-start.38 = (bf16[2,128,128]{2,1,0:T(8,128)(2,1)S(1)}, bf16[2,128,128]{2,1,0:T(8,128)(2,1)S(1)}, u32[]{:S(2)}, u32[]{:S(2)}) collective-permute-start(bf16[2,128,128]{2,1,0:T(8,128)(2,1)S(1)} %fusion.71), channel_id=1, source_target_pairs={{0,16},{1,17},{2,18},{3,19},{4,20},{5,21},{6,22},{7,23},{8,24},{9,... | collective-permute-start | bytes 196616 | tf_op jit(solution)/shard_map/ppermute | solution.py:110
  (189 shorter events, 55.8 us)
Async XLA Ops:
  0.7 26.6 %collective-permute-start = (bf16[128,4096]{1,0:T(8,128)(2,1)}, bf16[128,4096]{1,0:T(8,128)(2,1)}, u32[]{:S(2)}, u32[]{:S(2)}) collective-permute-start(bf16[128,4096]{1,0:T(8,128)(2,1)} %cot_own.1), channel_id=1, source_target_pairs={{0,2},{1,3},{2,0},{3,1},{4,6},{5,7},{6,4},{7,5},{8,10},{9,11},{10,... | collective-permute-start | bytes 3145736 | tf_op jit(solution)/shard_map/ppermute | solution.py:270
  3.7 72.9 %collective-permute-start.9 = (bf16[128,4096]{1,0:T(8,128)(2,1)}, bf16[128,4096]{1,0:T(8,128)(2,1)}, u32[]{:S(2)}, u32[]{:S(2)}) collective-permute-start(bf16[128,4096]{1,0:T(8,128)(2,1)} %param.16), channel_id=1, source_target_pairs={{0,1},{1,0},{2,3},{3,2},{4,5},{5,4},{6,7},{7,6},{8,9},{9,8},{10,11... | collective-permute-start | bytes 3145736 | tf_op jit(solution)/shard_map/ppermute | solution.py:269
  5.9 14.7 %collective-permute-start.1 = (bf16[64,4096]{1,0:T(8,128)(2,1)}, bf16[64,4096]{1,0:T(8,128)(2,1)}, u32[]{:S(2)}, u32[]{:S(2)}) collective-permute-start(bf16[64,4096]{1,0:T(8,128)(2,1)} %get-tuple-element.59.refs_0_), channel_id=1, source_target_pairs={{0,8},{1,9},{2,10},{3,11},{8,16},{9,17},{10,18},{11,19},{16,24},{1... | collective-permute-start | bytes 1572872 | tf_op jit(solution)/shard_map/ppermute | solution.py:277
  7.5 14.7 %collective-permute-start.4 = (bf16[64,4096]{1,0:T(8,128)(2,1)}, bf16[64,4096]{1,0:T(8,128)(2,1)}, u32[]{:S(2)}, u32[]{:S(2)}) collective-permute-start(bf16[64,4096]{1,0:T(8,128)(2,1)} %get-tuple-element.58.refs_2_), channel_id=1, source_target_pairs={{8,0},{9,1},{10,2},{11,3},{16,8},{17,9},{18,10},{19,11},{24,16},{2... | collective-permute-start | bytes 1572872 | tf_op jit(solution)/shard_map/ppermute | solution.py:277
  20.6 13.8 %collective-permute-start.2 = (bf16[64,4096]{1,0:T(8,128)(2,1)}, bf16[64,4096]{1,0:T(8,128)(2,1)S(1)}, u32[]{:S(2)}, u32[]{:S(2)}) collective-permute-start(bf16[64,4096]{1,0:T(8,128)(2,1)} %collective-permute-done.1.refs_4_), channel_id=1, source_target_pairs={{0,8},{1,9},{2,10},{3,11},{8,16},{9,17},{10,18},{11,19},{16,24},{1... | collective-permute-start | bytes 1572872 | tf_op jit(solution)/shard_map/ppermute | solution.py:277
  22.2 24.1 %collective-permute-start.5 = (bf16[64,4096]{1,0:T(8,128)(2,1)}, bf16[64,4096]{1,0:T(8,128)(2,1)S(1)}, u32[]{:S(2)}, u32[]{:S(2)}) collective-permute-start(bf16[64,4096]{1,0:T(8,128)(2,1)} %collective-permute-done.4.refs_6_), channel_id=1, source_target_pairs={{8,0},{9,1},{10,2},{11,3},{16,8},{17,9},{18,10},{19,11},{24,16},{2... | collective-permute-start | bytes 1572872 | tf_op jit(solution)/shard_map/ppermute | solution.py:277
  27.2 30.9 %collective-permute-start.7 = (bf16[128,4096]{0,1:T(8,128)(2,1)S(1)}, bf16[128,4096]{0,1:T(8,128)(2,1)S(1)}, u32[]{:S(2)}, u32[]{:S(2)}) collective-permute-start(bf16[128,4096]{0,1:T(8,128)(2,1)S(1)} %fusion.11), channel_id=1, source_target_pairs={{0,1},{1,2},{2,3},{3,4},{4,5},{5,6},{6,7},{7,8},{8,9},{9,10},{10,1... | collective-permute-start | bytes 3145736 | tf_op jit(solution)/shard_map/ppermute | solution.py:272
  31.5 30.7 %collective-permute-start.10 = (bf16[64,4096]{1,0:T(8,128)(2,1)}, bf16[64,4096]{1,0:T(8,128)(2,1)S(1)}, u32[]{:S(2)}, u32[]{:S(2)}) collective-permute-start(bf16[64,4096]{1,0:T(8,128)(2,1)} %collective-permute-done.1.refs_4_), channel_id=1, source_target_pairs={{0,1},{1,0},{2,3},{3,2},{4,5},{5,4},{6,7},{7,6},{8,9},{9,8},{10,11... | collective-permute-start | bytes 1572872 | tf_op jit(solution)/shard_map/ppermute | solution.py:289
  34.4 15.7 %collective-permute-start.3 = (bf16[64,4096]{1,0:T(8,128)(2,1)S(1)}, bf16[64,4096]{1,0:T(8,128)(2,1)S(1)}, u32[]{:S(2)}, u32[]{:S(2)}) collective-permute-start(bf16[64,4096]{1,0:T(8,128)(2,1)S(1)} %collective-permute-done.2.refs_8_), channel_id=1, source_target_pairs={{0,8},{1,9},{2,10},{3,11},{8,16},{9,17},{10,18},{11,19},{16,24},{1... | collective-permute-start | bytes 1572872 | tf_op jit(solution)/shard_map/ppermute | solution.py:277
  62.2 14.4 %collective-permute-start.12 = (bf16[64,4096]{1,0:T(8,128)(2,1)S(1)}, bf16[64,4096]{1,0:T(8,128)(2,1)S(1)}, u32[]{:S(2)}, u32[]{:S(2)}) collective-permute-start(bf16[64,4096]{1,0:T(8,128)(2,1)S(1)} %collective-permute-done.2.refs_8_), channel_id=1, source_target_pairs={{0,1},{1,0},{2,3},{3,2},{4,5},{5,4},{6,7},{7,6},{8,9},{9,8},{10,11... | collective-permute-start | bytes 1572872 | tf_op jit(solution)/shard_map/ppermute | solution.py:289
  62.3 14.8 %collective-permute-start.13 = (bf16[64,4096]{1,0:T(8,128)(2,1)S(1)}, bf16[64,4096]{1,0:T(8,128)(2,1)S(1)}, u32[]{:S(2)}, u32[]{:S(2)}) collective-permute-start(bf16[64,4096]{1,0:T(8,128)(2,1)S(1)} %collective-permute-done.5.refs_10_), channel_id=1, source_target_pairs={{0,1},{1,0},{2,3},{3,2},{4,5},{5,4},{6,7},{7,6},{8,9},{9,8},{10,11... | collective-permute-start | bytes 1572872 | tf_op jit(solution)/shard_map/ppermute | solution.py:289
  77.2 13.9 %collective-permute-start.8 = (bf16[8,128,256]{2,1,0:T(8,128)(2,1)S(1)}, bf16[8,128,256]{2,1,0:T(8,128)(2,1)S(1)}, u32[]{:S(2)}, u32[]{:S(2)}) collective-permute-start(bf16[8,128,256]{2,1,0:T(8,128)(2,1)S(1)} %get-tuple-element.28), channel_id=1, source_target_pairs={{0,2},{1,3},{2,0},{3,1},{4,6},{5,7},{6,4},{7,5},{8,10},{9,11},{10,... | collective-permute-start | bytes 1572872 | tf_op jit(solution)/shard_map/ppermute | solution.py:288
  79.1 17.6 %collective-permute-start.24 = (bf16[64,4096]{1,0:T(8,128)(2,1)}, bf16[64,4096]{1,0:T(8,128)(2,1)}, u32[]{:S(2)}, u32[]{:S(2)}) collective-permute-start(bf16[64,4096]{1,0:T(8,128)(2,1)} %collective-permute-done.20.refs_20_), channel_id=1, source_target_pairs={{0,8},{1,9},{2,10},{3,11},{8,16},{9,17},{10,18},{11,19},{16,24},{1... | collective-permute-start | bytes 1572872 | tf_op jit(solution)/shard_map/ppermute | solution.py:277
  82.4 14.5 %collective-permute-start.26 = (bf16[64,4096]{1,0:T(8,128)(2,1)S(1)}, bf16[64,4096]{1,0:T(8,128)(2,1)}, u32[]{:S(2)}, u32[]{:S(2)}) collective-permute-start(bf16[64,4096]{1,0:T(8,128)(2,1)S(1)} %collective-permute-done.22.refs_22_), channel_id=1, source_target_pairs={{8,0},{9,1},{10,2},{11,3},{16,8},{17,9},{18,10},{19,11},{24,16},{2... | collective-permute-start | bytes 1572872 | tf_op jit(solution)/shard_map/ppermute | solution.py:277
  85.1 14.8 %collective-permute-start.17 = (bf16[64,4096]{1,0:T(8,128)(2,1)}, bf16[64,4096]{1,0:T(8,128)(2,1)}, u32[]{:S(2)}, u32[]{:S(2)}) collective-permute-start(bf16[64,4096]{1,0:T(8,128)(2,1)} %collective-permute-done.16.refs_16_), channel_id=1, source_target_pairs={{0,1},{1,0},{2,3},{3,2},{4,5},{5,4},{6,7},{7,6},{8,9},{9,8},{10,11... | collective-permute-start | bytes 1572872 | tf_op jit(solution)/shard_map/ppermute | solution.py:289
  85.1 14.8 %collective-permute-start.19 = (bf16[64,4096]{1,0:T(8,128)(2,1)S(1)}, bf16[64,4096]{1,0:T(8,128)(2,1)}, u32[]{:S(2)}, u32[]{:S(2)}) collective-permute-start(bf16[64,4096]{1,0:T(8,128)(2,1)S(1)} %collective-permute-done.18.refs_18_), channel_id=1, source_target_pairs={{0,1},{1,0},{2,3},{3,2},{4,5},{5,4},{6,7},{7,6},{8,9},{9,8},{10,11... | collective-permute-start | bytes 1572872 | tf_op jit(solution)/shard_map/ppermute | solution.py:289
  96.7 14.1 %collective-permute-start.28 = (bf16[64,4096]{1,0:T(8,128)(2,1)}, bf16[64,4096]{1,0:T(8,128)(2,1)}, u32[]{:S(2)}, u32[]{:S(2)}) collective-permute-start(bf16[64,4096]{1,0:T(8,128)(2,1)} %collective-permute-done.24.refs_24_), channel_id=1, source_target_pairs={{0,8},{1,9},{2,10},{3,11},{8,16},{9,17},{10,18},{11,19},{16,24},{1... | collective-permute-start | bytes 1572872 | tf_op jit(solution)/shard_map/ppermute | solution.py:277
  96.9 14.0 %collective-permute-start.30 = (bf16[64,4096]{1,0:T(8,128)(2,1)}, bf16[64,4096]{1,0:T(8,128)(2,1)}, u32[]{:S(2)}, u32[]{:S(2)}) collective-permute-start(bf16[64,4096]{1,0:T(8,128)(2,1)} %collective-permute-done.26.refs_26_), channel_id=1, source_target_pairs={{8,0},{9,1},{10,2},{11,3},{16,8},{17,9},{18,10},{19,11},{24,16},{2... | collective-permute-start | bytes 1572872 | tf_op jit(solution)/shard_map/ppermute | solution.py:277
  99.9 13.8 %collective-permute-start.23 = (bf16[64,4096]{1,0:T(8,128)(2,1)}, bf16[64,4096]{1,0:T(8,128)(2,1)S(1)}, u32[]{:S(2)}, u32[]{:S(2)}) collective-permute-start(bf16[64,4096]{1,0:T(8,128)(2,1)} %copy-done.37), channel_id=1, source_target_pairs={{0,1},{1,0},{2,3},{3,2},{4,5},{5,4},{6,7},{7,6},{8,9},{9,8},{10,11... | collective-permute-start | bytes 1572872 | tf_op jit(solution)/shard_map/ppermute | solution.py:289
  99.9 13.7 %collective-permute-start.25 = (bf16[64,4096]{1,0:T(8,128)(2,1)}, bf16[64,4096]{1,0:T(8,128)(2,1)S(1)}, u32[]{:S(2)}, u32[]{:S(2)}) collective-permute-start(bf16[64,4096]{1,0:T(8,128)(2,1)} %collective-permute-done.24.refs_24_), channel_id=1, source_target_pairs={{0,1},{1,0},{2,3},{3,2},{4,5},{5,4},{6,7},{7,6},{8,9},{9,8},{10,11... | collective-permute-start | bytes 1572872 | tf_op jit(solution)/shard_map/ppermute | solution.py:289
  128.9 13.9 %collective-permute-start.33 = (bf16[8,128,256]{2,1,0:T(8,128)(2,1)S(1)}, bf16[8,128,256]{2,1,0:T(8,128)(2,1)S(1)}, u32[]{:S(2)}, u32[]{:S(2)}) collective-permute-start(bf16[8,128,256]{2,1,0:T(8,128)(2,1)S(1)} %get-tuple-element.36), channel_id=1, source_target_pairs={{0,2},{1,3},{2,0},{3,1},{4,6},{5,7},{6,4},{7,5},{8,10},{9,11},{10,... | collective-permute-start | bytes 1572872 | tf_op jit(solution)/shard_map/ppermute | solution.py:294
  151.5 36.3 %collective-permute-start.32 = (bf16[128,4096]{1,0:T(8,128)(2,1)}, bf16[128,4096]{1,0:T(8,128)(2,1)S(1)}, u32[]{:S(2)}, u32[]{:S(2)}) collective-permute-start(bf16[128,4096]{1,0:T(8,128)(2,1)} %copy-done.4), channel_id=1, source_target_pairs={{0,2},{1,3},{2,0},{3,1},{4,6},{5,7},{6,4},{7,5},{8,10},{9,11},{10,... | collective-permute-start | bytes 3145736 | tf_op jit(solution)/shard_map/ppermute | solution.py:295
  163.6 26.6 %collective-permute-start.34 = (bf16[128,4096]{0,1:T(8,128)(2,1)S(1)}, bf16[128,4096]{0,1:T(8,128)(2,1)S(1)}, u32[]{:S(2)}, u32[]{:S(2)}) collective-permute-start(bf16[128,4096]{0,1:T(8,128)(2,1)S(1)} %fusion.17), channel_id=1, source_target_pairs={{1,0},{2,1},{3,2},{4,3},{5,4},{6,5},{7,6},{8,7},{9,8},{10,9},{11,1... | collective-permute-start | bytes 3145736 | tf_op jit(solution)/shard_map/ppermute | solution.py:301
  170.2 14.7 %collective-permute-start.37 = (bf16[4,128,128]{2,1,0:T(8,128)(2,1)S(1)}, bf16[4,128,128]{2,1,0:T(8,128)(2,1)S(1)}, u32[]{:S(2)}, u32[]{:S(2)}) collective-permute-start(bf16[4,128,128]{2,1,0:T(8,128)(2,1)S(1)} %fusion.70), channel_id=1, source_target_pairs={{0,8},{1,9},{2,10},{3,11},{4,12},{5,13},{6,14},{7,15},{8,0},{9,1},... | collective-permute-start | bytes 393224 | tf_op jit(solution)/shard_map/ppermute | solution.py:110
  (62 other events, 658.5 us)
